TPU v7x, 512 devices: a whole 4x8x8 slice. The times are simulated.
512 devices in a mesh: gx: 16 (over z, y_hi), gy: 32 (over x, y_lo, core).
Axes of the slice: x: 4, y: 8 (y_hi: 2, y_lo: 4; y = y_hi * 4 + y_lo), z: 8, core: 2. Of those that a mesh axis runs over, the one named last changes fastest.
Arguments:
- voxel_material: int32 [1, 4096, 4096], P(None, 'gx', 'gy'), may hold values 0 or 1
- wetted_indicator: int32 [1, 4096, 4096], P(None, 'gx', 'gy'), may hold values 0 or 1
- starting_deficit_map: float32 [1, 4096, 4096], P(None, 'gx', 'gy'), may hold values from -6 to 6
- applied_thermal_slope: float32 [1, 2], replicated, may hold values from -4 to 4
Outputs:
- phase: float32 [1, 4096, 4096], P(None, 'gx', 'gy')
- heat: float32 [1, 4096, 4096], P(None, 'gx', 'gy')
- gradient: float32 [2, 1, 4096, 4096], P(None, None, 'gx', 'gy')
All inputs are finite; a program needn't handle non-finite values. No bound on the sum of `voxel_material` or of `wetted_indicator` on one device may be relied on, other than what follows from the above.
Results may differ from a plain program's by a relative error of at most 0.0001.
Values sent between devices are 32-bit elements; how exact they have to be, the bound alone decides.
No kernel may reach another device: no remote copies, remote signals or barrier semaphores. Data moves between devices by JAX's collectives and lax.ppermute only.
A program may use at most 64 MiB of HBM per device.

v0:
```python
import math

import jax
import jax.numpy as jnp
from jax import lax
from jax.sharding import PartitionSpec as P

solid_conduct = 1.7
gas_conduct = 0.026
liquid_conduct = 0.6
reference_conduct = 0.863
step_grad = 0.1
step_well = 0.3
step_drive = 0.2
step_heat = 0.12
latent_heat = 0.5
gradient_gain = 0.5
highest = lax.Precision.HIGHEST


def with_halo(block, sides, width):
    for axis, dim in sides:
        count = lax.axis_size(axis)
        forward = [(i, i + 1) for i in range(count - 1)]
        backward = [(target, source) for source, target in forward]
        low = lax.ppermute(
            lax.slice_in_dim(block, block.shape[dim] - width, None, axis=dim), axis, forward
        )
        high = lax.ppermute(lax.slice_in_dim(block, 0, width, axis=dim), axis, backward)
        block = jnp.concatenate([low, block, high], axis=dim)
    return block


def through_plane(centre):
    zeros_layer = jnp.zeros_like(centre)
    above = jnp.concatenate([centre[1:], zeros_layer], axis=0)
    below = jnp.concatenate([zeros_layer, centre[:-1]], axis=0)
    return above + below


def laplace(padded, centre):
    inplane = (
        padded[:, 2:, 1:-1] + padded[:, :-2, 1:-1] + padded[:, 1:-1, 2:] + padded[:, 1:-1, :-2]
    )
    return inplane + through_plane(centre) - 6.0 * centre


def progress_clock_increment(phase, heat, woven_backing_mesh):
    padded = with_halo(jnp.stack([phase, heat]), (("gx", 2), ("gy", 3)), 1)
    well = 2.0 * phase * (1.0 - phase) * (1.0 - 2.0 * phase)
    growth = 30.0 * phase * phase * (1.0 - phase) * (1.0 - phase)
    new_phase = woven_backing_mesh * (
        phase
        + step_grad * laplace(padded[0], phase)
        - step_well * well
        + step_drive * heat * growth
    )
    new_heat = heat + step_heat * laplace(padded[1], heat) - latent_heat * (new_phase - phase)
    return (new_phase, new_heat, padded[1])


def dft_tables(count, sign):
    index = jnp.arange(count, dtype=jnp.int32)
    product = index[:, None] * index[None, :] % count
    angle = 2.0 * math.pi / count * product.astype(jnp.float32)
    return (jnp.cos(angle), sign * jnp.sin(angle))


def twiddle(outer, inner, length, sign):
    index_outer = jnp.arange(outer, dtype=jnp.int32)
    index_inner = jnp.arange(inner, dtype=jnp.int32)
    product = index_outer[:, None] * index_inner[None, :] % length
    angle = 2.0 * math.pi / length * product.astype(jnp.float32)
    return (jnp.cos(angle), sign * jnp.sin(angle))


def complex_outer(count, sign):
    cosine, sine = dft_tables(count, sign)
    return jnp.stack(
        [jnp.stack([cosine, -sine], axis=1), jnp.stack([sine, cosine], axis=1)], axis=0
    )


def complex_inner(count, sign):
    cosine, sine = dft_tables(count, sign)
    return jnp.stack(
        [jnp.stack([cosine, sine], axis=1), jnp.stack([-sine, cosine], axis=1)], axis=0
    )


def rotate(pair, cosine, sine):
    return jnp.stack([pair[0] * cosine - pair[1] * sine, pair[0] * sine + pair[1] * cosine])


def contract(form, left, right):
    return jnp.einsum(form, left, right, precision=highest, preferred_element_type=jnp.float32)


def finish_forward(first, length):
    outer = length // 128
    twist_cos, twist_sin = twiddle(outer, 128, length, -1.0)
    turned = rotate(first, twist_cos, twist_sin)
    final = contract("q...kb,qbpj->p...kj", turned, complex_inner(128, -1.0))
    return final.reshape(final.shape[:-2] + (length,))


def forward_dft(pair):
    length = pair.shape[-1]
    outer = length // 128
    grid = pair.reshape(pair.shape[:-1] + (outer, 128))
    first = contract("pkqa,q...ab->p...kb", complex_outer(outer, -1.0), grid)
    return finish_forward(first, length)


def forward_real(real_part):
    length = real_part.shape[-1]
    outer = length // 128
    grid = real_part.reshape(real_part.shape[:-1] + (outer, 128))
    first = contract("pka,...ab->p...kb", complex_outer(outer, -1.0)[:, :, 0, :], grid)
    return finish_forward(first, length)


def inverse_dft(pair, keep_imag):
    length = pair.shape[-1]
    outer = length // 128
    grid = pair.reshape(pair.shape[:-1] + (outer, 128))
    first = contract("q...kj,qjpb->p...kb", grid, complex_inner(128, 1.0))
    twist_cos, twist_sin = twiddle(outer, 128, length, 1.0)
    turned = rotate(first, twist_cos, twist_sin)
    table = complex_outer(outer, 1.0)
    scale = 1.0 / length
    if keep_imag:
        final = contract("paqk,q...kb->p...ab", table, turned)
    else:
        final = contract("aqk,q...kb->...ab", table[0], turned)
    return (final * scale).reshape(final.shape[:-2] + (length,))


def spectral_freq(position, length):
    return position // 128 + length // 128 * (position % 128)


def green_apply(wave, ypos, xpos, total_y, total_x):
    yfreq = spectral_freq(ypos, total_y)
    xfreq = spectral_freq(xpos, total_x)
    ywave = jnp.where(yfreq >= total_y // 2, yfreq - total_y, yfreq).astype(jnp.float32)[:, None]
    xwave = jnp.where(xfreq >= total_x // 2, xfreq - total_x, xfreq).astype(jnp.float32)[None, :]
    valid = (
        (yfreq != total_y // 2)[:, None]
        & (xfreq != total_x // 2)[None, :]
        & ((yfreq != 0)[:, None] | (xfreq != 0)[None, :])
    )
    denom = reference_conduct * jnp.maximum(xwave * xwave + ywave * ywave, 1.0)
    coef_x = jnp.where(valid, xwave / denom, 0.0)
    coef_y = jnp.where(valid, ywave / denom, 0.0)
    along = xwave * wave[:, 0] + ywave * wave[:, 1]
    return jnp.stack([coef_x * along, coef_y * along], axis=1)


def inverse_rows(pair):
    return inverse_dft(pair, False)


def body(voxel_material, wetted_indicator, starting_deficit_map, applied_thermal_slope):
    woven_backing_mesh = voxel_material.astype(jnp.float32)
    order_parameter_initial_state = woven_backing_mesh * wetted_indicator.astype(jnp.float32)
    phase_single, heat_single, border_margin = progress_clock_increment(
        order_parameter_initial_state, starting_deficit_map, woven_backing_mesh
    )
    phase_two, heat_two, warmth_boundary_strip = progress_clock_increment(
        phase_single, heat_single, woven_backing_mesh
    )
    grad_x = gradient_gain * (
        warmth_boundary_strip[:, 2:, 1:-1] - warmth_boundary_strip[:, :-2, 1:-1]
    )
    grad_y = gradient_gain * (
        warmth_boundary_strip[:, 1:-1, 2:] - warmth_boundary_strip[:, 1:-1, :-2]
    )
    start_x = applied_thermal_slope[:, 0][:, None, None] + grad_x
    start_y = applied_thermal_slope[:, 1][:, None, None] + grad_y
    conduct = (
        woven_backing_mesh * (gas_conduct + (liquid_conduct - gas_conduct) * phase_two)
        + (1.0 - woven_backing_mesh) * solid_conduct
    )
    contrast = conduct - reference_conduct
    polar = jnp.stack([contrast * start_x, contrast * start_y])
    row_count = polar.shape[2]
    col_count = polar.shape[3]
    gx_size = lax.axis_size("gx")
    gy_size = lax.axis_size("gy")
    total_x = row_count * gx_size
    total_y = col_count * gy_size
    gx_index = lax.axis_index("gx")
    gy_index = lax.axis_index("gy")
    row_spec = forward_real(lax.all_to_all(polar, "gy", split_axis=2, concat_axis=3, tiled=True))
    spec = lax.all_to_all(row_spec, "gy", split_axis=4, concat_axis=3, tiled=True)
    turn = jnp.swapaxes(spec, 3, 4)
    slab = col_count // gx_size
    ypos = gy_index * col_count + gx_index * slab + jnp.arange(slab, dtype=jnp.int32)
    xpos = jnp.arange(total_x, dtype=jnp.int32)
    wave = forward_dft(lax.all_to_all(turn, "gx", split_axis=3, concat_axis=4, tiled=True))
    green = green_apply(wave, ypos, xpos, total_y, total_x)
    result = inverse_dft(green, True)
    back = lax.all_to_all(result, "gx", split_axis=4, concat_axis=3, tiled=True)
    grid = jnp.swapaxes(back, 3, 4)
    answer = inverse_rows(lax.all_to_all(grid, "gy", split_axis=3, concat_axis=4, tiled=True))
    answer = lax.all_to_all(answer, "gy", split_axis=3, concat_axis=2, tiled=True)
    gradient = jnp.stack(
        [
            applied_thermal_slope[:, 0][:, None, None] - answer[0],
            applied_thermal_slope[:, 1][:, None, None] - answer[1],
        ]
    )
    return (phase_two, heat_two, gradient)


def solution(mesh):
    in_specs = (P(None, "gx", "gy"), P(None, "gx", "gy"), P(None, "gx", "gy"), P())
    out_specs = (P(None, "gx", "gy"), P(None, "gx", "gy"), P(None, None, "gx", "gy"))
    return jax.shard_map(body, mesh=mesh, in_specs=in_specs, out_specs=out_specs, check_vma=False)
```

profile of v0, /device:TPU:1, one launch (start us, length us, event | category | flops | bytes accessed | tf_op | source)
XLA Modules:
  0.0 332.8 jit_solution(13352846701854406444)
XLA Ops:
  0.7 1.0 fusion.54
  1.7 0.7 pad_maximum_fusion.20
  2.4 8.3 %collective-permute-start = (f32[2,1,1,128]{3,2,1,0:T(1,128)S(1)}, f32[2,1,1,128]{3,2,1,0:T(1,128)S(1)}, u32[]{:S(2)}, u32[]{:S(2)}) collective-permute-start(f32[2,1,1,128]{3,2,1,0:T(1,128)S(1)} %get-tuple-element.31), channel_id=1, source_target_pairs={{0,32},{32,64},{64,96},{96,128},{128,160},{160,192},{192,224},{224... | collective-permute-start | bytes 3080 | tf_op jit(solution)/shard_map/ppermute | solution.py:26
  10.7 1.3 collective-permute-start.1
  12.3 6.6 %collective-permute-done.1 = f32[2,1,1,128]{3,2,1,0:T(1,128)S(1)} collective-permute-done((f32[2,1,1,128]{3,2,1,0:T(1,128)S(1)}, f32[2,1,1,128]{3,2,1,0:T(1,128)S(1)}, u32[]{:S(2)}, u32[]{:S(2)}) %collective-permute-start.1) | collective-permute-done | bytes 1056 | tf_op jit(solution)/shard_map/ppermute | solution.py:29
  18.9 0.9 pad_maximum_fusion.3
  20.0 4.3 %collective-permute-start.2 = (f32[2,1,258,1]{3,2,1,0:T(8,128)S(1)}, f32[2,1,258,1]{3,2,1,0:T(8,128)S(1)}, u32[]{:S(2)}, u32[]{:S(2)}) collective-permute-start(f32[2,1,258,1]{3,2,1,0:T(8,128)S(1)} %get-tuple-element.25), channel_id=1, source_target_pairs={{0,1},{1,2},{2,3},{3,4},{4,5},{5,6},{6,7},{7,8},{8,9},{9,10},{10,1... | collective-permute-start | bytes 6200 | tf_op jit(solution)/shard_map/ppermute | solution.py:26
  24.3 1.9 collective-permute-start.3
  26.3 1.4 collective-permute-done.2
  27.6 7.1 %collective-permute-done.3 = f32[2,1,258,1]{3,2,1,0:T(8,128)S(1)} collective-permute-done((f32[2,1,258,1]{3,2,1,0:T(8,128)S(1)}, f32[2,1,258,1]{3,2,1,0:T(8,128)S(1)}, u32[]{:S(2)}, u32[]{:S(2)}) %collective-permute-start.3) | collective-permute-done | bytes 2096 | tf_op jit(solution)/shard_map/ppermute | solution.py:29
  34.8 1.2 pad_maximum_fusion
  36.0 1.3 fusion.39
  37.4 4.4 %collective-permute-start.4 = (f32[2,1,1,128]{3,2,1,0:T(1,128)S(1)}, f32[2,1,1,128]{3,2,1,0:T(1,128)S(1)}, u32[]{:S(2)}, u32[]{:S(2)}) collective-permute-start(f32[2,1,1,128]{3,2,1,0:T(1,128)S(1)} %get-tuple-element.29), channel_id=1, source_target_pairs={{0,32},{32,64},{64,96},{96,128},{128,160},{160,192},{192,224},{224... | collective-permute-start | bytes 3080 | tf_op jit(solution)/shard_map/ppermute | solution.py:26
  41.8 1.3 collective-permute-start.5
  43.2 6.8 %collective-permute-done.5 = f32[2,1,1,128]{3,2,1,0:T(1,128)S(1)} collective-permute-done((f32[2,1,1,128]{3,2,1,0:T(1,128)S(1)}, f32[2,1,1,128]{3,2,1,0:T(1,128)S(1)}, u32[]{:S(2)}, u32[]{:S(2)}) %collective-permute-start.5) | collective-permute-done | bytes 1056 | tf_op jit(solution)/shard_map/ppermute | solution.py:29
  50.2 3.2 collective-permute-start.6
  53.4 1.9 collective-permute-start.7
  55.3 0.7 fusion.112
  56.0 0.8 collective-permute-done.6
  56.8 7.1 %collective-permute-done.7 = f32[2,1,258,1]{3,2,1,0:T(8,128)S(1)} collective-permute-done((f32[2,1,258,1]{3,2,1,0:T(8,128)S(1)}, f32[2,1,258,1]{3,2,1,0:T(8,128)S(1)}, u32[]{:S(2)}, u32[]{:S(2)}) %collective-permute-start.7) | collective-permute-done | bytes 2096 | tf_op jit(solution)/shard_map/ppermute | solution.py:29
  63.9 0.3 pad_maximum_fusion.1
  64.2 0.9 add_multiply_fusion.1
  65.1 1.5 add_multiply_fusion
  66.6 0.9 pad_maximum_fusion.5
  67.6 7.7 %all-to-all-start = ((f32[2,1,256,128]{3,0,1,2:T(2,128)}), f32[2,1,256,128]{3,0,1,2:T(2,128)S(1)}, u32[]{:S(2)}, u32[]{:S(2)}) async-start(f32[2,1,256,128]{3,0,1,2:T(2,128)} %pad_maximum_fusion.5), calls=%async_computation | async-start | bytes 524288 | tf_op jit(solution)/shard_map/all_to_all | solution.py:195
  75.4 0.3 broadcast_multiply_fusion
  75.7 0.3 fusion.67
  76.0 10.6 %all-to-all-done = f32[2,1,256,128]{3,0,1,2:T(2,128)S(1)} async-done(((f32[2,1,256,128]{3,0,1,2:T(2,128)}), f32[2,1,256,128]{3,0,1,2:T(2,128)S(1)}, u32[]{:S(2)}, u32[]{:S(2)}) %all-to-all-start) | async-done | bytes 262176 | tf_op jit(solution)/shard_map/all_to_all | solution.py:195
  86.6 0.6 convolution_bitcast_fusion.6
  87.3 0.6 convolution_bitcast_fusion.5
  87.9 5.9 %copy.180 = f32[2,2,1,8,32,128]{3,1,0,5,4,2:T(2,128)} copy(f32[2,2,1,8,32,128]{5,4,3,1,0,2:T(8,128)S(1)} %convolution_bitcast_fusion.5) | data formatting | bytes 1048576 | tf_op jit(solution)/shard_map/reshape | solution.py:104
  93.8 15.6 %reshape.789 = f32[32,1,4096]{2,1,0:T(1,128)} reshape(f32[4096,1,2,2,8]{4,3,2,1,0:T(2,128)} %bitcast.245) | data formatting | bytes 1048576
  109.4 3.9 %all-to-all-start.1 = ((f32[32,1,4096]{2,1,0:T(1,128)}), f32[32,1,4096]{2,1,0:T(1,128)S(1)}, u32[]{:S(2)}, u32[]{:S(2)}) async-start(f32[32,1,4096]{2,1,0:T(1,128)} %reshape.789), calls=%async_computation.1 | async-start | bytes 1048576 | tf_op jit(solution)/shard_map/all_to_all | solution.py:196
  113.5 16.5 %all-to-all-done.1 = f32[32,1,4096]{2,1,0:T(1,128)S(1)} async-done(((f32[32,1,4096]{2,1,0:T(1,128)}), f32[32,1,4096]{2,1,0:T(1,128)S(1)}, u32[]{:S(2)}, u32[]{:S(2)}) %all-to-all-start.1) | async-done | bytes 524320 | tf_op jit(solution)/shard_map/all_to_all | solution.py:196
  129.9 0.5 broadcast.1411
  130.4 1.9 reduce
  132.3 14.1 %reshape.790 = f32[4096,1,2,2,8]{4,3,2,1,0:T(2,128)} reshape(f32[32,4096]{1,0:T(8,128)S(1)} %reduce) | data formatting | bytes 1048576
  146.4 9.5 %copy.134 = f32[2,2,1,8,4096]{4,2,3,1,0:T(1,128)S(1)} copy(f32[2,2,1,8,4096]{3,1,0,2,4:T(2,128)} %bitcast.246) | data formatting | bytes 1048576 | tf_op jit(solution)/shard_map/all_to_all | solution.py:196
  155.9 0.3 copy.215
  156.2 1.0 copy.136
  157.2 15.3 %all-to-all-start.2 = ((f32[2,2,1,128,256]{4,1,0,2,3:T(2,128)}), f32[2,2,1,128,256]{4,1,0,2,3:T(2,128)S(1)}, u32[]{:S(2)}, u32[]{:S(2)}) async-start(f32[2,2,1,128,256]{4,1,0,2,3:T(2,128)} %copy.136), calls=%async_computation.2 | async-start | bytes 1048576 | tf_op jit(solution)/shard_map/all_to_all | solution.py:201
  172.7 14.9 %all-to-all-done.2 = f32[2,2,1,128,256]{4,1,0,2,3:T(2,128)S(1)} async-done(((f32[2,2,1,128,256]{4,1,0,2,3:T(2,128)}), f32[2,2,1,128,256]{4,1,0,2,3:T(2,128)S(1)}, u32[]{:S(2)}, u32[]{:S(2)}) %all-to-all-start.2) | async-done | bytes 524320 | tf_op jit(solution)/shard_map/all_to_all | solution.py:201
  187.9 0.6 convolution_bitcast_fusion.2
  188.6 0.6 convolution_bitcast_fusion.4
  189.6 0.6 convolution_bitcast_fusion.1
  190.3 0.6 fusion.1
  190.9 5.9 %copy.187 = f32[2,2,1,8,32,128]{3,1,0,5,4,2:T(2,128)} copy(f32[2,2,1,8,32,128]{5,4,0,3,1,2:T(8,128)S(1)} %fusion.1) | data formatting | bytes 1048576 | tf_op jit(solution)/shard_map/reshape | solution.py:136
  196.7 14.9 %reshape.791 = f32[16,1,8192]{2,1,0:T(1,128)S(1)} reshape(f32[4096,1,2,2,8]{4,3,2,1,0:T(2,128)} %bitcast.247) | data formatting | bytes 1048576
  211.7 22.9 %all_to_all.96 = f32[16,1,8192]{2,1,0:T(1,128)S(1)} all-to-all(f32[16,1,8192]{2,1,0:T(1,128)S(1)} %reshape.791), channel_id=1, replica_groups=mesh['gx'=16,'gy'=32] {'gx'}, dimensions={0} | all-to-all | bytes 1048576 | tf_op jit(solution)/shard_map/all_to_all | solution.py:204
  234.6 1.9 reduce.1
  236.5 14.8 %reshape.792 = f32[4096,1,2,2,8]{4,3,2,1,0:T(2,128)} reshape(f32[16,8192]{1,0:T(8,128)S(1)} %reduce.1) | data formatting | bytes 1048576
  251.3 10.1 %copy.189 = f32[2,2,1,8,16,256]{5,3,4,1,0,2:T(8,128)S(1)} copy(f32[2,2,1,8,16,256]{3,1,0,5,4,2:T(2,128)} %bitcast.248) | data formatting | bytes 1048576 | tf_op jit(solution)/shard_map/all_to_all | solution.py:204
  261.4 0.3 copy.147
  261.7 28.6 %all_to_all.97 = f32[2,2,1,256,128]{4,1,0,2,3:T(2,128)S(1)} all-to-all(f32[2,2,1,256,128]{4,1,0,2,3:T(2,128)S(1)} %copy.147), channel_id=1, replica_groups=mesh['gx'=16,'gy'=32] {'gy'}, dimensions={3} | all-to-all | bytes 1048576 | tf_op jit(solution)/shard_map/all_to_all | solution.py:206
  290.3 0.8 convolution_bitcast_fusion
  291.3 0.4 fusion.3
  291.7 3.1 copy.193
  294.7 7.2 %reshape.793 = f32[32,1,2048]{2,1,0:T(1,128)S(1)} reshape(f32[4096,1,2,8]{3,2,1,0:T(2,128)} %bitcast.249) | data formatting | bytes 524288
  302.0 14.8 %all_to_all.98 = f32[32,1,2048]{2,1,0:T(1,128)S(1)} all-to-all(f32[32,1,2048]{2,1,0:T(1,128)S(1)} %reshape.793), channel_id=1, replica_groups=mesh['gx'=16,'gy'=32] {'gy'}, dimensions={0} | all-to-all | bytes 524288 | tf_op jit(solution)/shard_map/all_to_all | solution.py:207
  316.7 1.3 reduce.2
  318.0 7.7 %reshape.794 = f32[4096,1,2,8]{3,2,1,0:T(2,128)} reshape(f32[32,2048]{1,0:T(8,128)S(1)} %reduce.2) | data formatting | bytes 524288
  325.7 5.1 %copy.154 = f32[2,1,8,32,128]{4,2,3,1,0:T(8,128)S(1)} copy(f32[2,1,8,32,128]{2,0,4,3,1:T(2,128)} %bitcast.250) | data formatting | bytes 524288 | tf_op jit(solution)/shard_map/all_to_all | solution.py:207
  330.8 1.3 fusion.31
  332.1 0.7 pad_maximum_fusion.6
  (40 shorter events, 2.2 us)
Async XLA Ops:
  0.6 63.6 %copy-start = (s32[1,256,128]{2,1,0:T(8,128)S(1)}, s32[1,256,128]{2,1,0:T(8,128)}, u32[]{:S(2)}) copy-start(s32[1,256,128]{2,1,0:T(8,128)} %param.4) | copy-start | bytes 393220
  0.6 54.7 %copy-start.2 = (f32[1,2]{1,0:T(1,128)S(1)}, f32[1,2]{1,0:T(1,128)}, u32[]{:S(2)}) copy-start(f32[1,2]{1,0:T(1,128)} %param.7) | copy-start | bytes 28
  2.4 9.9 %collective-permute-start = (f32[2,1,1,128]{3,2,1,0:T(1,128)S(1)}, f32[2,1,1,128]{3,2,1,0:T(1,128)S(1)}, u32[]{:S(2)}, u32[]{:S(2)}) collective-permute-start(f32[2,1,1,128]{3,2,1,0:T(1,128)S(1)} %get-tuple-element.31), channel_id=1, source_target_pairs={{0,32},{32,64},{64,96},{96,128},{128,160},{160,192},{192,224},{224... | collective-permute-start | bytes 3080 | tf_op jit(solution)/shard_map/ppermute | solution.py:26
  10.7 8.2 %collective-permute-start.1 = (f32[2,1,1,128]{3,2,1,0:T(1,128)S(1)}, f32[2,1,1,128]{3,2,1,0:T(1,128)S(1)}, u32[]{:S(2)}, u32[]{:S(2)}) collective-permute-start(f32[2,1,1,128]{3,2,1,0:T(1,128)S(1)} %get-tuple-element.32), channel_id=1, source_target_pairs={{32,0},{64,32},{96,64},{128,96},{160,128},{192,160},{224,192},{256... | collective-permute-start | bytes 3080 | tf_op jit(solution)/shard_map/ppermute | solution.py:29
  20.0 7.7 %collective-permute-start.2 = (f32[2,1,258,1]{3,2,1,0:T(8,128)S(1)}, f32[2,1,258,1]{3,2,1,0:T(8,128)S(1)}, u32[]{:S(2)}, u32[]{:S(2)}) collective-permute-start(f32[2,1,258,1]{3,2,1,0:T(8,128)S(1)} %get-tuple-element.25), channel_id=1, source_target_pairs={{0,1},{1,2},{2,3},{3,4},{4,5},{5,6},{6,7},{7,8},{8,9},{9,10},{10,1... | collective-permute-start | bytes 6200 | tf_op jit(solution)/shard_map/ppermute | solution.py:26
  24.3 10.5 %collective-permute-start.3 = (f32[2,1,258,1]{3,2,1,0:T(8,128)S(1)}, f32[2,1,258,1]{3,2,1,0:T(8,128)S(1)}, u32[]{:S(2)}, u32[]{:S(2)}) collective-permute-start(f32[2,1,258,1]{3,2,1,0:T(8,128)S(1)} %get-tuple-element.26), channel_id=1, source_target_pairs={{1,0},{2,1},{3,2},{4,3},{5,4},{6,5},{7,6},{8,7},{9,8},{10,9},{11,1... | collective-permute-start | bytes 6200 | tf_op jit(solution)/shard_map/ppermute | solution.py:29
  37.4 5.8 %collective-permute-start.4 = (f32[2,1,1,128]{3,2,1,0:T(1,128)S(1)}, f32[2,1,1,128]{3,2,1,0:T(1,128)S(1)}, u32[]{:S(2)}, u32[]{:S(2)}) collective-permute-start(f32[2,1,1,128]{3,2,1,0:T(1,128)S(1)} %get-tuple-element.29), channel_id=1, source_target_pairs={{0,32},{32,64},{64,96},{96,128},{128,160},{160,192},{192,224},{224... | collective-permute-start | bytes 3080 | tf_op jit(solution)/shard_map/ppermute | solution.py:26
  41.8 8.2 %collective-permute-start.5 = (f32[2,1,1,128]{3,2,1,0:T(1,128)S(1)}, f32[2,1,1,128]{3,2,1,0:T(1,128)S(1)}, u32[]{:S(2)}, u32[]{:S(2)}) collective-permute-start(f32[2,1,1,128]{3,2,1,0:T(1,128)S(1)} %get-tuple-element.30), channel_id=1, source_target_pairs={{32,0},{64,32},{96,64},{128,96},{160,128},{192,160},{224,192},{256... | collective-permute-start | bytes 3080 | tf_op jit(solution)/shard_map/ppermute | solution.py:29
  50.2 6.6 %collective-permute-start.6 = (f32[2,1,258,1]{3,2,1,0:T(8,128)S(1)}, f32[2,1,258,1]{3,2,1,0:T(8,128)S(1)}, u32[]{:S(2)}, u32[]{:S(2)}) collective-permute-start(f32[2,1,258,1]{3,2,1,0:T(8,128)S(1)} %get-tuple-element.23), channel_id=1, source_target_pairs={{0,1},{1,2},{2,3},{3,4},{4,5},{5,6},{6,7},{7,8},{8,9},{9,10},{10,1... | collective-permute-start | bytes 6200 | tf_op jit(solution)/shard_map/ppermute | solution.py:26
  53.4 10.5 %collective-permute-start.7 = (f32[2,1,258,1]{3,2,1,0:T(8,128)S(1)}, f32[2,1,258,1]{3,2,1,0:T(8,128)S(1)}, u32[]{:S(2)}, u32[]{:S(2)}) collective-permute-start(f32[2,1,258,1]{3,2,1,0:T(8,128)S(1)} %get-tuple-element.24), channel_id=1, source_target_pairs={{1,0},{2,1},{3,2},{4,3},{5,4},{6,5},{7,6},{8,7},{9,8},{10,9},{11,1... | collective-permute-start | bytes 6200 | tf_op jit(solution)/shard_map/ppermute | solution.py:29
  65.1 44.3 %copy-start.1 = (f32[1,256,128]{2,1,0:T(8,128)}, f32[1,256,128]{2,1,0:T(8,128)S(1)}, u32[]{:S(2)}) copy-start(f32[1,256,128]{2,1,0:T(8,128)S(1)} %get-tuple-element.4) | copy-start | bytes 393220
  67.6 19.0 %all-to-all-start = ((f32[2,1,256,128]{3,0,1,2:T(2,128)}), f32[2,1,256,128]{3,0,1,2:T(2,128)S(1)}, u32[]{:S(2)}, u32[]{:S(2)}) async-start(f32[2,1,256,128]{3,0,1,2:T(2,128)} %pad_maximum_fusion.5), calls=%async_computation | async-start | bytes 524288 | tf_op jit(solution)/shard_map/all_to_all | solution.py:195
  109.4 20.5 %all-to-all-start.1 = ((f32[32,1,4096]{2,1,0:T(1,128)}), f32[32,1,4096]{2,1,0:T(1,128)S(1)}, u32[]{:S(2)}, u32[]{:S(2)}) async-start(f32[32,1,4096]{2,1,0:T(1,128)} %reshape.789), calls=%async_computation.1 | async-start | bytes 1048576 | tf_op jit(solution)/shard_map/all_to_all | solution.py:196
  157.2 30.4 %all-to-all-start.2 = ((f32[2,2,1,128,256]{4,1,0,2,3:T(2,128)}), f32[2,2,1,128,256]{4,1,0,2,3:T(2,128)S(1)}, u32[]{:S(2)}, u32[]{:S(2)}) async-start(f32[2,2,1,128,256]{4,1,0,2,3:T(2,128)} %copy.136), calls=%async_computation.2 | async-start | bytes 1048576 | tf_op jit(solution)/shard_map/all_to_all | solution.py:201
where the time goes:
time: 334 us; the launch traced here: 333 us
  local copies, waits for them, and re-layouts  117 us (35%)
  waiting for transfers between devices  71.7 us (21%)
  blocking collectives  66.3 us (20%)
  starting transfers between devices  53.5 us (16%)
  other arithmetic  17.8 us (5%)
  matrix products  4.91 us (1%)
    unnamed x14, local copies, waits for them, and re-layouts  74.4 us
    all_to_all x1, blocking collectives, body(): lax.all_to_all(grid, 'gy', split_axis=3, concat_axis=4, tiled=True)  28.6 us
    ppermute x4, waiting for transfers between devices, with_halo(): lax.ppermute(lax.slice_in_dim(block, 0, width, axis=dim), axis, backward)  27.6 us
    all_to_all x1, blocking collectives, body(): back = lax.all_to_all(result, 'gx', split_axis=4, concat_axis=3, tiled=True)  22.9 us
    ppermute x4, starting transfers between devices, with_halo(): lax.ppermute(lax.slice_in_dim(block, block.shape[dim] - width, None, axis...  20.2 us
    all_to_all x1, waiting for transfers between devices, body(): lax.all_to_all(row_spec, 'gy', split_axis=4, concat_axis=3, tiled=True)  16.5 us
    all_to_all x1, starting transfers between devices, body(): lax.all_to_all(turn, 'gx', split_axis=3, concat_axis=4, tiled=True)  15.3 us
    all_to_all x1, waiting for transfers between devices, body(): lax.all_to_all(turn, 'gx', split_axis=3, concat_axis=4, tiled=True)  14.9 us
  transfers between devices with their start and end apart: 11, of which 9 were waited for; matrix products, arithmetic and copies ran while one was open for 1% of the time, Pallas kernels for 0%

commit v1 on v0

v1 whole, which is shorter than its diff:
```python
import functools
import math

import jax
import jax.numpy as jnp
import numpy as np
from jax import lax
from jax.experimental import pallas as pl
from jax.experimental.pallas import tpu as pltpu
from jax.sharding import Mesh
from jax.sharding import PartitionSpec as P

solid_conduct = 1.7
gas_conduct = 0.026
liquid_conduct = 0.6
reference_conduct = 0.863
step_grad = 0.1
step_well = 0.3
step_drive = 0.2
step_heat = 0.12
latent_heat = 0.5
gradient_gain = 0.5
highest = lax.Precision.HIGHEST

TILE_ROWS = 256
TILE_COLS = 128
EDGE = 8
TALL = TILE_ROWS + 2 * EDGE
WIDE = 384
OUTER = 32
SLAB = 16
CHIPS = 256
COLS = 4096
ROWS = 4096
VMEM = pl.BlockSpec(memory_space=pltpu.VMEM)
SMEM = pl.BlockSpec(memory_space=pltpu.SMEM)


def dot(left, right, contract=((1,), (0,))):
    return lax.dot_general(
        left, right, (contract, ((), ())), precision=highest, preferred_element_type=jnp.float32
    )


def call(kernel, outs, *args, smem=()):
    shapes = [jax.ShapeDtypeStruct(shape, jnp.float32) for shape in outs]
    return pl.pallas_call(
        kernel,
        out_shape=shapes,
        in_specs=[SMEM if i in smem else VMEM for i in range(len(args))],
        out_specs=[VMEM] * len(outs),
        compiler_params=pltpu.CompilerParams(vmem_limit_bytes=32 * 1024 * 1024),
    )(*args)


def angles(left, right, length):
    product = np.outer(np.arange(left), np.arange(right)) % length
    return 2.0 * math.pi / length * product


def table(array):
    return jnp.asarray(np.asarray(array, dtype=np.float32))


def column_tables():
    first = angles(OUTER, OUTER, OUTER)
    second = angles(64, 128, 128)
    twist = angles(OUTER, 128, COLS)
    cosine, sine = np.cos(second), np.sin(second)
    forward_first = np.concatenate([np.cos(first), -np.sin(first)], axis=0)
    forward_second = np.block([[cosine, sine], [-sine, cosine]])
    backward_second = np.block([[cosine, sine], [-sine, cosine]])
    backward_first = np.concatenate([np.cos(first), -np.sin(first)], axis=1)
    return forward_first, forward_second, backward_first, backward_second, np.cos(twist), np.sin(twist)


def row_tables():
    first = angles(CHIPS, CHIPS, CHIPS)
    second = angles(SLAB, SLAB, SLAB)
    twist = np.repeat(angles(CHIPS, SLAB, ROWS), 8, axis=1)
    cosine, sine = np.kron(np.cos(second), np.eye(8)), np.kron(np.sin(second), np.eye(8))
    both = np.concatenate([np.cos(first), np.sin(first)], axis=0)
    forward = np.block([[cosine, -sine], [sine, cosine]])
    backward = np.block([[cosine, sine], [-sine, cosine]])
    return both, forward, backward, np.cos(twist), np.sin(twist)


def extend(voxel, wetted, heat, above, below):
    porous = voxel[...].astype(jnp.float32)
    phase = porous * wetted[...].astype(jnp.float32)
    middle = (porous, phase, heat[...])
    return [jnp.concatenate([above[f], middle[f], below[f]], axis=0) for f in range(3)]


def edge_kernel(voxel, wetted, heat, above, below, left, right):
    spare = jnp.zeros((WIDE - TALL, TILE_COLS), jnp.float32)
    for f, field in enumerate(extend(voxel, wetted, heat, above, below)):
        flipped = jnp.concatenate([field, spare], axis=0).T
        left[f] = flipped[:EDGE]
        right[f] = flipped[TILE_COLS - EDGE :]


def progress(phase, heat, porous, phase_lap, heat_lap):
    well = 2.0 * phase * (1.0 - phase) * (1.0 - 2.0 * phase)
    growth = 30.0 * phase * phase * (1.0 - phase) * (1.0 - phase)
    new_phase = porous * (
        phase + step_grad * phase_lap - step_well * well + step_drive * heat * growth
    )
    new_heat = heat + step_heat * heat_lap - latent_heat * (new_phase - phase)
    return new_phase, new_heat


def neighbours(field):
    tall, wide = field.shape
    return (
        pltpu.roll(field, tall - 1, 0),
        pltpu.roll(field, 1, 0),
        pltpu.roll(field, wide - 1, 1),
        pltpu.roll(field, 1, 1),
    )


def laplace(around, field):
    return around[0] + around[1] + around[2] + around[3] - 6.0 * field


def stencil_kernel(
    place, slope, voxel, wetted, heat, above, below, left, right, phase_out, heat_out, polar_out
):
    spare = jnp.zeros((TILE_COLS - 2 * EDGE, WIDE), jnp.float32)
    fields = []
    for f, field in enumerate(extend(voxel, wetted, heat, above, below)):
        side = jnp.concatenate([right[f], spare, left[f]], axis=0).T
        fields.append(jnp.concatenate([field, side[:TALL]], axis=1))
    porous, phase, warmth = fields
    row = lax.broadcasted_iota(jnp.int32, porous.shape, 0) - EDGE + TILE_ROWS * place[0]
    lane = lax.broadcasted_iota(jnp.int32, porous.shape, 1)
    column = jnp.where(lane < 192, lane, lane - 256) + TILE_COLS * place[1]
    inside = (row >= 0) & (row < ROWS) & (column >= 0) & (column < COLS)
    phase_one, heat_one = progress(
        phase, warmth, porous, laplace(neighbours(phase), phase), laplace(neighbours(warmth), warmth)
    )
    heat_one = jnp.where(inside, heat_one, 0.0)

    def centre(field):
        return field[EDGE : EDGE + TILE_ROWS, :TILE_COLS]

    phase_around = [centre(field) for field in neighbours(phase_one)]
    heat_around = [centre(field) for field in neighbours(heat_one)]
    phase_one, heat_one, porous = centre(phase_one), centre(heat_one), centre(porous)
    phase_two, heat_two = progress(
        phase_one, heat_one, porous, laplace(phase_around, phase_one), laplace(heat_around, heat_one)
    )
    phase_out[...] = phase_two
    heat_out[...] = heat_two
    start_x = slope[0, 0] + gradient_gain * (heat_around[0] - heat_around[1])
    start_y = slope[0, 1] + gradient_gain * (heat_around[2] - heat_around[3])
    conduct = (
        porous * (gas_conduct + (liquid_conduct - gas_conduct) * phase_two)
        + (1.0 - porous) * solid_conduct
    )
    contrast = conduct - reference_conduct
    polar_out[:, 0] = (contrast * start_x).reshape(TILE_ROWS // SLAB, SLAB, TILE_COLS)
    polar_out[:, 1] = (contrast * start_y).reshape(TILE_ROWS // SLAB, SLAB, TILE_COLS)


def columns_forward_kernel(data, first, second, twist_cos, twist_sin, out):
    rows = jnp.concatenate([data[pl.ds(s, OUTER, stride=SLAB), :] for s in range(SLAB)], axis=1)
    spread = dot(first[...], rows)
    cosine, sine = twist_cos[...], twist_sin[...]
    real, imag = [], []
    for s in range(SLAB):
        part = slice(s * 128, (s + 1) * 128)
        re, im = spread[:OUTER, part], spread[OUTER:, part]
        real.append(re * cosine + im * sine)
        imag.append(im * cosine - re * sine)
    for g in range(4):
        span = slice(g * 8, (g + 1) * 8)
        re = jnp.concatenate([part[span] for part in real], axis=0)
        im = jnp.concatenate([part[span] for part in imag], axis=0)
        both = jnp.concatenate([re, im], axis=1)
        final = dot(second[...], both, ((1,), (1,)))
        out[pl.ds(2 * g, 64, stride=8), :] = final[:64]
        out[pl.ds(2 * g + 1, 64, stride=8), :] = final[64:]


def columns_backward_kernel(data, first, second, twist_cos, twist_sin, out):
    real, imag = [], []
    for g in range(4):
        span = slice(g * 8, (g + 1) * 8)
        both = jnp.concatenate(
            [data[pl.ds(2 * g, 64, stride=8), :], data[pl.ds(2 * g + 1, 64, stride=8), :]], axis=0
        )
        spread = dot(both, second[...], ((0,), (0,)))
        re = spread[:, :128].reshape(SLAB, 8, 128)
        im = spread[:, 128:].reshape(SLAB, 8, 128)
        cosine, sine = twist_cos[span][None], twist_sin[span][None]
        real.append(re * cosine - im * sine)
        imag.append(im * cosine + re * sine)
    stacked = jnp.concatenate(
        [jnp.concatenate([part[s] for part in real + imag], axis=0) for s in range(SLAB)], axis=1
    )
    final = dot(first[...], stacked)
    for s in range(SLAB):
        out[pl.ds(s, OUTER, stride=SLAB), :] = final[:, s * 128 : (s + 1) * 128]


def wave_numbers(place):
    shape = (CHIPS, 128)
    kp = lax.broadcasted_iota(jnp.int32, shape, 0)
    lane = lax.broadcasted_iota(jnp.int32, shape, 1)
    row_freq = kp + CHIPS * (lane // 8)
    col_freq = 8 * place[2] + lane % 8
    row_wave = jnp.where(row_freq >= ROWS // 2, row_freq - ROWS, row_freq).astype(jnp.float32)
    return row_freq, col_freq, row_wave, col_freq.astype(jnp.float32)


def rows_forward_kernel(place, data, first, second, twist_cos, twist_sin, out):
    real = data[pl.ds(0, CHIPS, stride=2), :]
    imag = data[pl.ds(1, CHIPS, stride=2), :]
    spread = dot(first[...], jnp.concatenate([real, imag], axis=1))
    re = spread[:CHIPS, :128] + spread[CHIPS:, 128:]
    im = spread[:CHIPS, 128:] - spread[CHIPS:, :128]
    cosine, sine = twist_cos[...], twist_sin[...]
    turned = jnp.concatenate([re * cosine + im * sine, im * cosine - re * sine], axis=1)
    final = dot(turned, second[...])
    _, _, row_wave, col_wave = wave_numbers(place)
    wave = jnp.where(place[3] == 0, row_wave, col_wave)
    out[:CHIPS] = wave * final[:, :128]
    out[CHIPS:] = wave * final[:, 128:]


def rows_backward_kernel(place, mine, other, first, second, twist_cos, twist_sin, out):
    row_freq, col_freq, row_wave, col_wave = wave_numbers(place)
    valid = (
        (row_freq != ROWS // 2)
        & (col_freq != COLS // 2)
        & ((row_freq != 0) | (col_freq != 0))
    )
    denom = reference_conduct * jnp.maximum(row_wave * row_wave + col_wave * col_wave, 1.0)
    weight = jnp.where(col_freq == 0, 1.0, 2.0) / (ROWS * COLS)
    wave = jnp.where(place[3] == 0, row_wave, col_wave)
    coef = jnp.where(valid, weight * wave / denom, 0.0)
    along = mine[...] + other[...]
    green = jnp.concatenate([coef * along[:CHIPS], coef * along[CHIPS:]], axis=1)
    spread = dot(green, second[...])
    re, im = spread[:, :128], spread[:, 128:]
    cosine, sine = twist_cos[...], twist_sin[...]
    turned = jnp.concatenate([re * cosine - im * sine, im * cosine + re * sine], axis=1)
    final = dot(first[...], turned)
    out[pl.ds(0, CHIPS, stride=2), :] = final[:CHIPS, :128] - final[CHIPS:, 128:]
    out[pl.ds(1, CHIPS, stride=2), :] = final[:CHIPS, 128:] + final[CHIPS:, :128]


def exchange(array, axes, count):
    blocks = array.reshape((count, array.size // count // 128, 128))
    return lax.all_to_all(blocks, axes, split_axis=0, concat_axis=0, tiled=True)


def shift(block, axes, count, step):
    pairs = [(i, i + step) for i in range(count) if 0 <= i + step < count]
    return lax.ppermute(block, axes, pairs)


def body(voxel_material, wetted_indicator, starting_deficit_map, applied_thermal_slope):
    gx_size = lax.axis_size("gx")
    gt_size = lax.axis_size("gt")
    core_size = lax.axis_size("core")
    gy_size = gt_size * core_size
    gx_index = lax.axis_index("gx")
    gt_index = lax.axis_index("gt")
    core_index = lax.axis_index("core")
    place = jnp.stack(
        [gx_index, gt_index * core_size + core_index, gx_index * gt_size + gt_index, core_index]
    ).astype(jnp.int32)
    voxel, wetted, heat = voxel_material[0], wetted_indicator[0], starting_deficit_map[0]

    def strip(part):
        porous = voxel[part].astype(jnp.float32)
        return jnp.stack([porous, porous * wetted[part].astype(jnp.float32), heat[part]])

    above = shift(strip(slice(TILE_ROWS - EDGE, TILE_ROWS)), "gx", gx_size, 1)
    below = shift(strip(slice(0, EDGE)), "gx", gx_size, -1)
    first_columns, last_columns = call(
        edge_kernel, [(3, EDGE, WIDE)] * 2, voxel, wetted, heat, above, below
    )
    gy = ("gt", "core")
    left = shift(last_columns, gy, gy_size, 1)
    right = shift(first_columns, gy, gy_size, -1)
    phase_two, heat_two, polar = call(
        stencil_kernel,
        [
            (TILE_ROWS, TILE_COLS),
            (TILE_ROWS, TILE_COLS),
            (TILE_ROWS // SLAB, 2, SLAB, TILE_COLS),
        ],
        place, applied_thermal_slope, voxel, wetted, heat, above, below, left, right,
        smem=(0, 1),
    )
    first_to, second_to, first_back, second_back, col_cos, col_sin = map(table, column_tables())
    both, rows_to, rows_back, row_cos, row_sin = map(table, row_tables())
    chips = ("gx", "gt")
    slab = exchange(polar, gy, gy_size).reshape(-1, 128)
    (spec,) = call(
        columns_forward_kernel, [(2 * CHIPS, 128)], slab, first_to, second_to, col_cos, col_sin
    )
    spec = exchange(spec, chips, CHIPS).reshape(-1, 128)
    (mine,) = call(
        rows_forward_kernel, [(2 * CHIPS, 128)], place, spec, both, rows_to, row_cos, row_sin, smem=(0,)
    )
    other = lax.ppermute(mine, "core", [(0, 1), (1, 0)])
    (green,) = call(
        rows_backward_kernel, [(2 * CHIPS, 128)],
        place, mine, other, both, rows_back, row_cos, row_sin, smem=(0,),
    )
    green = exchange(green, chips, CHIPS).reshape(-1, 128)
    (answer,) = call(
        columns_backward_kernel, [(OUTER * SLAB, 128)], green, first_back, second_back, col_cos, col_sin
    )
    answer = exchange(answer, gy, gy_size).reshape(TILE_ROWS // SLAB, 2, SLAB, TILE_COLS)
    answer = jnp.swapaxes(answer, 0, 1).reshape(2, 1, TILE_ROWS, TILE_COLS)
    gradient = applied_thermal_slope[0][:, None, None, None] - answer
    return (phase_two[None], heat_two[None], gradient)


def solution(mesh):
    gx_size, gy_size = mesh.devices.shape
    fine = Mesh(mesh.devices.reshape(gx_size, gy_size // 2, 2), ("gx", "gt", "core"))
    gy = ("gt", "core")
    in_specs = (P(None, "gx", gy), P(None, "gx", gy), P(None, "gx", gy), P())
    out_specs = (P(None, "gx", gy), P(None, "gx", gy), P(None, None, "gx", gy))
    return jax.shard_map(body, mesh=fine, in_specs=in_specs, out_specs=out_specs, check_vma=False)
```

time: 334 us -> 138 us (0.41)
  local copies, waits for them, and re-layouts: 117 us -> 1.89 us
  waiting for transfers between devices: 71.7 us -> 11.7 us
  starting transfers between devices: 53.5 us -> 19.3 us
  blocking collectives: 66.3 us -> 92.9 us
  other arithmetic: 17.8 us -> 2.41 us
  Pallas kernels: 0 us -> 8.27 us
  matrix products: 4.91 us -> 0 us
    unnamed x14 -> x28, local copies, waits for them, and re-layouts: 74.4 us -> 1.88 us
    all_to_all x3 -> x0, waiting for transfers between devices: 42 us -> none  [the longest x1 16.5 us: body(): lax.all_to_all(row_spec, 'gy', split_axis=4, concat_axis=3, tiled=True)]
    all_to_all x3 -> x0, starting transfers between devices: 26.9 us -> none  [the longest x1 15.3 us: body(): lax.all_to_all(turn, 'gx', split_axis=3, concat_axis=4, tiled=True)]
    all_to_all x3 -> x4, blocking collectives: 66.3 us -> 92.9 us  [exchange(): return lax.all_to_all(blocks, axes, split_axis=0, concat_axis=0, tiled=True)]
    all_to_all x7 -> x0, local copies, waits for them, and re-layouts: 25.7 us -> none  [the longest x3 10.3 us: body(): lax.all_to_all(row_spec, 'gy', split_axis=4, concat_axis=3, tiled=True)]
    ppermute x8 -> x5, waiting for transfers between devices: 29.8 us -> 11.7 us  [the longest x4 10.5 us: shift(): return lax.ppermute(block, axes, pairs)]
    reshape x4 -> x1, local copies, waits for them, and re-layouts: 14.9 us -> 0.02 us  [body(): exchange(answer, gy, gy_size).reshape(TILE_ROWS // SLAB, 2, SLAB, TILE_COLS)]
    pallas_call x0 -> x6, Pallas kernels: none -> 8.27 us  [call(): pl.pallas_call(kernel, out_shape=shapes, in_specs=[SMEM if i in smem else...]
  transfers between devices with their start and end apart: 11 -> 5, of which waited for: 9 -> 3; matrix products, arithmetic and copies ran while one was open for 1% -> 0% of each run, Pallas kernels for 0% -> 0%
where the time goes in v1:
time: 138 us; the launch traced here: 137 us
  blocking collectives  92.9 us (67%)
  starting transfers between devices  19.3 us (14%)
  waiting for transfers between devices  11.7 us (8%)
  Pallas kernels  8.27 us (6%)
  other arithmetic  2.41 us (2%)
  local copies, waits for them, and re-layouts  1.89 us (1%)
    all_to_all x4, blocking collectives, exchange(): return lax.all_to_all(blocks, axes, split_axis=0, concat_axis=0, tiled=True)  92.9 us
    ppermute x4, starting transfers between devices, shift(): return lax.ppermute(block, axes, pairs)  15.8 us
    ppermute x4, waiting for transfers between devices, shift(): return lax.ppermute(block, axes, pairs)  10.5 us
    pallas_call x6, Pallas kernels, call(): pl.pallas_call(kernel, out_shape=shapes, in_specs=[SMEM if i in smem else...  8.27 us
    ppermute x1, starting transfers between devices, body(): other = lax.ppermute(mine, 'core', [(0, 1), (1, 0)])  3.52 us
  transfers between devices with their start and end apart: 5, of which 3 were waited for; matrix products, arithmetic and copies ran while one was open for 0% of the time, Pallas kernels for 0%

profile of v1, /device:TPU:1, one launch (start us, length us, event | category | flops | bytes accessed | tf_op | source)
XLA Modules:
  0.0 137.3 jit_solution(16362494154645330137)
XLA Ops:
  0.6 0.0 copy-start.1
  0.6 0.8 slice_convert_fusion
  1.4 0.8 convert_multiply_fusion
  2.2 8.3 %collective-permute-start = (f32[3,8,128]{2,1,0:T(8,128)S(1)}, f32[3,8,128]{2,1,0:T(8,128)S(1)}, u32[]{:S(2)}, u32[]{:S(2)}) collective-permute-start(f32[3,8,128]{2,1,0:T(8,128)S(1)} %pad_maximum_fusion), channel_id=1, source_target_pairs={{0,32},{32,64},{64,96},{96,128},{128,160},{160,192},{192,224},{224... | collective-permute-start | bytes 36872 | tf_op jit(solution)/shard_map/ppermute | solution.py:262
  10.5 1.3 collective-permute-start.1
  11.8 0.0 collective-permute-done.above
  11.8 7.0 %collective-permute-done.1.below = f32[3,8,128]{2,1,0:T(8,128)S(1)} collective-permute-done((f32[3,8,128]{2,1,0:T(8,128)S(1)}, f32[3,8,128]{2,1,0:T(8,128)S(1)}, u32[]{:S(2)}, u32[]{:S(2)}) %collective-permute-start.1) | collective-permute-done | bytes 12320 | tf_op jit(solution)/shard_map/ppermute | solution.py:262
  18.8 0.0 copy-done.1
  18.8 0.0 copy-start.2
  18.8 0.9 copy-done.2
  19.7 0.0 copy-start.3
  19.7 0.9 copy-done.3
  20.6 0.2 shard_map.166
  20.8 4.3 %collective-permute-start.2 = (f32[3,8,384]{2,1,0:T(8,128)S(1)}, f32[3,8,384]{2,1,0:T(8,128)S(1)}, u32[]{:S(2)}, u32[]{:S(2)}) collective-permute-start(f32[3,8,384]{2,1,0:T(8,128)S(1)} %get-tuple-element.8), channel_id=1, source_target_pairs={{0,1},{1,2},{2,3},{3,4},{4,5},{5,6},{6,7},{7,8},{8,9},{9,10},{10,1... | collective-permute-start | bytes 110600 | tf_op jit(solution)/shard_map/ppermute | solution.py:262
  25.2 1.9 %collective-permute-start.3 = (f32[3,8,384]{2,1,0:T(8,128)S(1)}, f32[3,8,384]{2,1,0:T(8,128)S(1)}, u32[]{:S(2)}, u32[]{:S(2)}) collective-permute-start(f32[3,8,384]{2,1,0:T(8,128)S(1)} %get-tuple-element.9), channel_id=1, source_target_pairs={{1,0},{2,1},{3,2},{4,3},{5,4},{6,5},{7,6},{8,7},{9,8},{10,9},{11,1... | collective-permute-start | bytes 110600 | tf_op jit(solution)/shard_map/ppermute | solution.py:262
  27.1 0.0 copy-start.13
  27.1 0.1 pad_add_fusion.place
  27.2 0.0 collective-permute-done.2.left
  27.2 3.5 %collective-permute-done.3.right = f32[3,8,384]{2,1,0:T(8,128)S(1)} collective-permute-done((f32[3,8,384]{2,1,0:T(8,128)S(1)}, f32[3,8,384]{2,1,0:T(8,128)S(1)}, u32[]{:S(2)}, u32[]{:S(2)}) %collective-permute-start.3) | collective-permute-done | bytes 36896 | tf_op jit(solution)/shard_map/ppermute | solution.py:262
  30.7 0.0 copy-done.13
  30.7 2.1 %shard_map.167 = (f32[256,128]{1,0:T(8,128)}, f32[256,128]{1,0:T(8,128)}, f32[16,2,16,128]{3,2,1,0:T(8,128)S(1)}) custom-call(s32[4]{0:T(128)S(1)} %pad_add_fusion.place, f32[1,2]{1,0:T(1,128)S(1)} %copy-done.13, s32[256,128]{1,0:T(8,128)S(1)} %bitcast.28, s32[256,128]{1,0:T(8,128)S(1)} %bitcast.30, f32[256,128]{1,0:T(8,128)S(1)} %bitcast.32, ...), custom_call_target="tpu_custom_call" | custom-call | tf_op jit(solution)/shard_map/pallas_call | solution.py:47
  32.8 0.0 copy-start.4
  32.8 0.0 copy-start.9
  32.8 0.0 copy-start.10
  32.8 0.0 copy-start.11
  32.8 21.5 %all_to_all.20 = f32[32,16,128]{2,1,0:T(8,128)S(1)} all-to-all(f32[32,16,128]{2,1,0:T(8,128)S(1)} %bitcast.33), channel_id=1, replica_groups=mesh['gx'=16,'gt'=16,'core'=2] {'gt','core'}, dimensions={0} | all-to-all | bytes 524288 | tf_op jit(solution)/shard_map/all_to_all | solution.py:257
  54.3 0.0 copy-done.4
  54.3 0.0 copy-done.9
  54.3 0.0 copy-done.10
  54.3 0.0 copy-done.11
  54.3 0.0 copy-start
  54.3 1.1 shard_map.168
  55.5 0.0 copy-start.5
  55.5 0.0 copy-start.6
  55.5 0.0 copy-start.8
  55.5 31.5 %all_to_all.21 = f32[256,2,128]{2,1,0:T(2,128)S(1)} all-to-all(f32[256,2,128]{2,1,0:T(2,128)S(1)} %bitcast.25), channel_id=1, replica_groups=mesh['gx'=16,'gt'=16,'core'=2] {'gx','gt'}, dimensions={0} | all-to-all | bytes 524288 | tf_op jit(solution)/shard_map/all_to_all | solution.py:257
  87.0 0.0 copy-done
  87.0 0.0 copy-done.5
  87.0 0.0 copy-done.6
  87.0 0.0 copy-done.8
  87.0 0.0 copy-start.7
  87.0 1.8 %shard_map.169.mine = f32[512,128]{1,0:T(8,128)S(1)} custom-call(s32[4]{0:T(128)S(1)} %pad_add_fusion.place, f32[512,128]{1,0:T(8,128)S(1)} %bitcast.26, f32[512,256]{1,0:T(8,128)S(1)} %copy-done, f32[256,256]{1,0:T(8,128)S(1)} %copy-done.8, f32[256,128]{1,0:T(8,128)S(1)} %copy-done.6, f32[256,128]{1,0:T(8,128)S(1)} %copy-done.5), custom_call_target="tpu_custom_call" | custom-call | tf_op jit(solution)/shard_map/pallas_call | solution.py:47
  88.9 3.5 %collective-permute-start.4 = (f32[512,128]{1,0:T(8,128)S(1)}, f32[512,128]{1,0:T(8,128)S(1)}, u32[]{:S(2)}, u32[]{:S(2)}) collective-permute-start(f32[512,128]{1,0:T(8,128)S(1)} %shard_map.169.mine), channel_id=1, source_target_pairs={{0,1},{1,0},{2,3},{3,2},{4,5},{5,4},{6,7},{7,6},{8,9},{9,8},{10,11... | collective-permute-start | bytes 786440 | tf_op jit(solution)/shard_map/ppermute | solution.py:311
  92.4 1.1 collective-permute-done.4.other
  93.5 0.0 copy-done.7
  93.5 2.0 %shard_map.170 = f32[512,128]{1,0:T(8,128)S(1)} custom-call(s32[4]{0:T(128)S(1)} %pad_add_fusion.place, f32[512,128]{1,0:T(8,128)S(1)} %shard_map.169.mine, f32[512,128]{1,0:T(8,128)S(1)} %collective-permute-done.4.other, f32[512,256]{1,0:T(8,128)S(1)} %copy-done, f32[256,256]{1,0:T(8,128)S(1)} %copy-done.7, f32[256,128]{1,0:T(8,128)S(1)} %copy-done.6, ...), custom_call_target="tpu_custom_call" | custom-call | tf_op jit(solution)/shard_map/pallas_call | solution.py:47
  95.5 0.0 copy-start.12
  95.5 23.0 %all_to_all.22 = f32[256,2,128]{2,1,0:T(2,128)S(1)} all-to-all(f32[256,2,128]{2,1,0:T(2,128)S(1)} %bitcast.21), channel_id=1, replica_groups=mesh['gx'=16,'gt'=16,'core'=2] {'gx','gt'}, dimensions={0} | all-to-all | bytes 524288 | tf_op jit(solution)/shard_map/all_to_all | solution.py:257
  118.5 0.0 copy-done.12
  118.5 1.0 shard_map.171
  119.6 16.9 %all_to_all.23 = f32[32,16,128]{2,1,0:T(8,128)S(1)} all-to-all(f32[32,16,128]{2,1,0:T(8,128)S(1)} %bitcast.23), channel_id=1, replica_groups=mesh['gx'=16,'gt'=16,'core'=2] {'gt','core'}, dimensions={0} | all-to-all | bytes 524288 | tf_op jit(solution)/shard_map/all_to_all | solution.py:257
  136.5 0.8 broadcast_subtract_fusion
  (3 shorter events, 0.0 us)
Async XLA Ops:
  0.6 18.2 %copy-start.1 = (s32[1,256,128]{2,1,0:T(8,128)S(1)}, s32[1,256,128]{2,1,0:T(8,128)}, u32[]{:S(2)}) copy-start(s32[1,256,128]{2,1,0:T(8,128)} %param.15) | copy-start | bytes 393220
  2.2 9.6 %collective-permute-start = (f32[3,8,128]{2,1,0:T(8,128)S(1)}, f32[3,8,128]{2,1,0:T(8,128)S(1)}, u32[]{:S(2)}, u32[]{:S(2)}) collective-permute-start(f32[3,8,128]{2,1,0:T(8,128)S(1)} %pad_maximum_fusion), channel_id=1, source_target_pairs={{0,32},{32,64},{64,96},{96,128},{128,160},{160,192},{192,224},{224... | collective-permute-start | bytes 36872 | tf_op jit(solution)/shard_map/ppermute | solution.py:262
  10.5 8.3 %collective-permute-start.1 = (f32[3,8,128]{2,1,0:T(8,128)S(1)}, f32[3,8,128]{2,1,0:T(8,128)S(1)}, u32[]{:S(2)}, u32[]{:S(2)}) collective-permute-start(f32[3,8,128]{2,1,0:T(8,128)S(1)} %pad_maximum_fusion.1), channel_id=1, source_target_pairs={{32,0},{64,32},{96,64},{128,96},{160,128},{192,160},{224,192},{256... | collective-permute-start | bytes 36872 | tf_op jit(solution)/shard_map/ppermute | solution.py:262
  18.8 0.9 copy-start.2
  19.7 0.9 copy-start.3
  20.8 6.3 %collective-permute-start.2 = (f32[3,8,384]{2,1,0:T(8,128)S(1)}, f32[3,8,384]{2,1,0:T(8,128)S(1)}, u32[]{:S(2)}, u32[]{:S(2)}) collective-permute-start(f32[3,8,384]{2,1,0:T(8,128)S(1)} %get-tuple-element.8), channel_id=1, source_target_pairs={{0,1},{1,2},{2,3},{3,4},{4,5},{5,6},{6,7},{7,8},{8,9},{9,10},{10,1... | collective-permute-start | bytes 110600 | tf_op jit(solution)/shard_map/ppermute | solution.py:262
  25.2 5.5 %collective-permute-start.3 = (f32[3,8,384]{2,1,0:T(8,128)S(1)}, f32[3,8,384]{2,1,0:T(8,128)S(1)}, u32[]{:S(2)}, u32[]{:S(2)}) collective-permute-start(f32[3,8,384]{2,1,0:T(8,128)S(1)} %get-tuple-element.9), channel_id=1, source_target_pairs={{1,0},{2,1},{3,2},{4,3},{5,4},{6,5},{7,6},{8,7},{9,8},{10,9},{11,1... | collective-permute-start | bytes 110600 | tf_op jit(solution)/shard_map/ppermute | solution.py:262
  27.1 3.6 %copy-start.13 = (f32[1,2]{1,0:T(1,128)S(1)}, f32[1,2]{1,0:T(1,128)}, u32[]{:S(2)}) copy-start(f32[1,2]{1,0:T(1,128)} %slope.1) | copy-start | bytes 28
  32.8 21.5 %copy-start.4 = (f32[128,256]{1,0:T(8,128)S(1)}, f32[128,256]{1,0:T(8,128)}, u32[]{:S(2)}) copy-start(f32[128,256]{1,0:T(8,128)} %constant.37.clone.second) | copy-start | bytes 393220
  32.8 21.5 %copy-start.9 = (f32[32,128]{1,0:T(8,128)S(1)}, f32[32,128]{1,0:T(8,128)}, u32[]{:S(2)}) copy-start(f32[32,128]{1,0:T(8,128)} %constant.40.clone.twist_sin) | copy-start | bytes 49156
  32.8 21.5 %copy-start.10 = (f32[32,128]{1,0:T(8,128)S(1)}, f32[32,128]{1,0:T(8,128)}, u32[]{:S(2)}) copy-start(f32[32,128]{1,0:T(8,128)} %constant.39.clone.twist_cos) | copy-start | bytes 49156
  32.8 21.5 %copy-start.11 = (f32[64,32]{1,0:T(8,128)S(1)}, f32[64,32]{1,0:T(8,128)}, u32[]{:S(2)}) copy-start(f32[64,32]{1,0:T(8,128)} %constant.36.clone.first) | copy-start | bytes 24580
  54.3 32.7 %copy-start = (f32[512,256]{1,0:T(8,128)S(1)}, f32[512,256]{1,0:T(8,128)}, u32[]{:S(2)}) copy-start(f32[512,256]{1,0:T(8,128)} %constant.41.clone.first) | copy-start | bytes 1572868
  55.5 31.5 %copy-start.5 = (f32[256,128]{1,0:T(8,128)S(1)}, f32[256,128]{1,0:T(8,128)}, u32[]{:S(2)}) copy-start(f32[256,128]{1,0:T(8,128)} %constant.45.clone.twist_sin) | copy-start | bytes 393220
  55.5 31.5 %copy-start.6 = (f32[256,128]{1,0:T(8,128)S(1)}, f32[256,128]{1,0:T(8,128)}, u32[]{:S(2)}) copy-start(f32[256,128]{1,0:T(8,128)} %constant.44.clone.twist_cos) | copy-start | bytes 393220
  55.5 31.5 %copy-start.8 = (f32[256,256]{1,0:T(8,128)S(1)}, f32[256,256]{1,0:T(8,128)}, u32[]{:S(2)}) copy-start(f32[256,256]{1,0:T(8,128)} %constant.42.clone.second) | copy-start | bytes 786436
  87.0 6.5 %copy-start.7 = (f32[256,256]{1,0:T(8,128)S(1)}, f32[256,256]{1,0:T(8,128)}, u32[]{:S(2)}) copy-start(f32[256,256]{1,0:T(8,128)} %constant.43.clone.second) | copy-start | bytes 786436
  88.9 4.7 %collective-permute-start.4 = (f32[512,128]{1,0:T(8,128)S(1)}, f32[512,128]{1,0:T(8,128)S(1)}, u32[]{:S(2)}, u32[]{:S(2)}) collective-permute-start(f32[512,128]{1,0:T(8,128)S(1)} %shard_map.169.mine), channel_id=1, source_target_pairs={{0,1},{1,0},{2,3},{3,2},{4,5},{5,4},{6,7},{7,6},{8,9},{9,8},{10,11... | collective-permute-start | bytes 786440 | tf_op jit(solution)/shard_map/ppermute | solution.py:311
  95.5 23.0 %copy-start.12 = (f32[32,64]{1,0:T(8,128)S(1)}, f32[32,64]{1,0:T(8,128)}, u32[]{:S(2)}) copy-start(f32[32,64]{1,0:T(8,128)} %constant.38.clone.first) | copy-start | bytes 24580

commit v2 on v1

v2 whole, which is shorter than its diff:
```python
import functools
import math

import jax
import jax.numpy as jnp
import numpy as np
from jax import lax
from jax.experimental import pallas as pl
from jax.experimental.pallas import tpu as pltpu
from jax.sharding import Mesh
from jax.sharding import PartitionSpec as P

solid_conduct = 1.7
gas_conduct = 0.026
liquid_conduct = 0.6
reference_conduct = 0.863
step_grad = 0.1
step_well = 0.3
step_drive = 0.2
step_heat = 0.12
latent_heat = 0.5
gradient_gain = 0.5

TILE_ROWS = 256
TILE_COLS = 128
EDGE = 8
SHIFT = 2
TALL = TILE_ROWS + EDGE
WIDE = 384
OUTER = 32
SLAB = 16
CHIPS = 256
COLS = 4096
ROWS = 4096
CORE_MAJOR = np.arange(OUTER).reshape(-1, 2).T.reshape(-1)
VMEM = pl.BlockSpec(memory_space=pltpu.VMEM)
SMEM = pl.BlockSpec(memory_space=pltpu.SMEM)


def halves(array):
    high = array.astype(jnp.bfloat16)
    return high, (array - high.astype(jnp.float32)).astype(jnp.bfloat16)


def dot(left, right, contract=((1,), (0,))):
    def product(x, y):
        return lax.dot_general(x, y, (contract, ((), ())), preferred_element_type=jnp.float32)

    (left_high, left_low), (right_high, right_low) = halves(left), halves(right)
    return product(left_high, right_high) + (
        product(left_high, right_low) + product(left_low, right_high)
    )


def call(kernel, outs, *args, smem=()):
    shapes = [jax.ShapeDtypeStruct(shape, jnp.float32) for shape in outs]
    spaces = [SMEM if i in smem else VMEM for i in range(len(args))]
    return pl.pallas_call(
        kernel,
        out_shape=shapes,
        in_specs=spaces,
        out_specs=[VMEM] * len(outs),
        compiler_params=pltpu.CompilerParams(vmem_limit_bytes=32 * 1024 * 1024),
    )(*args)


def angles(left, right, length):
    product = np.outer(np.arange(left), np.asarray(right)) % length
    return 2.0 * math.pi / length * product


def table(array):
    return jnp.asarray(np.asarray(array, dtype=np.float32))


def column_tables():
    first = angles(OUTER, range(OUTER), OUTER)
    cosine, sine = np.cos(first), np.sin(first)
    tables = []
    for shift in (SHIFT, 0):
        inner = np.arange(128) - shift
        second = angles(64, inner, 128)
        twist = angles(OUTER, inner, COLS)
        if shift:
            stack = np.concatenate([cosine, -sine], axis=0)
        else:
            stack = np.concatenate([cosine, -sine], axis=1)[CORE_MAJOR]
        mix = np.block([[np.cos(second), np.sin(second)], [-np.sin(second), np.cos(second)]])
        tables.append([table(array) for array in (stack, mix, np.cos(twist), np.sin(twist))])
    return tables


def row_tables():
    first = angles(CHIPS, range(CHIPS), CHIPS)
    both = table(np.concatenate([np.cos(first), np.sin(first)], axis=0))
    tables = []
    for shift, sign in ((SHIFT, -1.0), (0, 1.0)):
        inner = np.arange(SLAB) - shift
        second = angles(SLAB, inner, SLAB)
        twist = np.repeat(angles(CHIPS, inner, ROWS), 8, axis=1)
        cosine, sine = np.kron(np.cos(second), np.eye(8)), sign * np.kron(np.sin(second), np.eye(8))
        if shift:
            cosine, sine = cosine.T, sine.T
        mix = np.block([[cosine, sine], [-sine, cosine]])
        tables.append([both] + [table(array) for array in (mix, np.cos(twist), np.sin(twist))])
    return tables


def prepare_kernel(voxel, wetted, heat, porous, phase, heat_out):
    porous[...] = voxel[...].astype(jnp.float32)
    phase[...] = porous[...] * wetted[...].astype(jnp.float32)
    heat_out[...] = heat[...]


def with_above(above, porous, phase, heat):
    tops = (above[0], above[0] * above[1], above[2])
    return [
        jnp.concatenate([top, field[...]], axis=0) for top, field in zip(tops, (porous, phase, heat))
    ]


def edge_kernel(porous, phase, heat, above, strip):
    spare = jnp.zeros((WIDE - TALL, TILE_COLS), jnp.float32)
    for f, tall in enumerate(with_above(above, porous, phase, heat)):
        strip[f] = jnp.concatenate([tall, spare], axis=0).T[TILE_COLS - EDGE :]


def progress(phase, heat, porous, phase_lap, heat_lap):
    well = 2.0 * phase * (1.0 - phase) * (1.0 - 2.0 * phase)
    growth = 30.0 * phase * phase * (1.0 - phase) * (1.0 - phase)
    new_phase = porous * (
        phase + step_grad * phase_lap - step_well * well + step_drive * heat * growth
    )
    new_heat = heat + step_heat * heat_lap - latent_heat * (new_phase - phase)
    return new_phase, new_heat


def stencil_kernel(place, slope, porous, phase, heat, above, left, fields_out, polar_out):
    spare = jnp.zeros((TILE_COLS - EDGE, WIDE), jnp.float32)
    fields = []
    for f, tall in enumerate(with_above(above, porous, phase, heat)):
        side = jnp.concatenate([spare, left[f]], axis=0).T
        fields.append(jnp.concatenate([tall, side[:TALL]], axis=1))
    porous, phase, heat = fields
    wide = porous.shape[1]
    row = lax.broadcasted_iota(jnp.int32, porous.shape, 0) + TALL * place[0]
    column = lax.broadcasted_iota(jnp.int32, porous.shape, 1) + wide * place[1]
    last_row, first_row = row != EDGE - 1, row != EDGE
    last_column, first_column = column != wide - 1, column != 0

    def neighbours(field):
        return (
            jnp.where(last_row, pltpu.roll(field, TALL - 1, 0), 0.0),
            jnp.where(first_row, pltpu.roll(field, 1, 0), 0.0),
            jnp.where(last_column, pltpu.roll(field, wide - 1, 1), 0.0),
            jnp.where(first_column, pltpu.roll(field, 1, 1), 0.0),
        )

    def laplace(around, field):
        return around[0] + around[1] + around[2] + around[3] - 6.0 * field

    def shifted(field):
        field = pltpu.roll(field, SHIFT, 1)[:, :TILE_COLS]
        return pltpu.roll(field, TALL - EDGE + SHIFT, 0)[:TILE_ROWS]

    phase_lap, heat_lap = laplace(neighbours(phase), phase), laplace(neighbours(heat), heat)
    phase, heat = progress(phase, heat, porous, phase_lap, heat_lap)
    heat_around = neighbours(heat)
    phase_lap, heat_lap = laplace(neighbours(phase), phase), laplace(heat_around, heat)
    phase, heat = progress(phase, heat, porous, phase_lap, heat_lap)
    fields_out[0] = shifted(phase)
    fields_out[1] = shifted(heat)
    start_x = slope[0, 0] + gradient_gain * (heat_around[0] - heat_around[1])
    start_y = slope[0, 1] + gradient_gain * (heat_around[2] - heat_around[3])
    conduct = (
        porous * (gas_conduct + (liquid_conduct - gas_conduct) * phase)
        + (1.0 - porous) * solid_conduct
    )
    contrast = conduct - reference_conduct
    blocks = (TILE_ROWS // SLAB, SLAB, TILE_COLS)
    polar_out[:, 0] = shifted(contrast * start_x).reshape(blocks)
    polar_out[:, 1] = shifted(contrast * start_y).reshape(blocks)


def return_rows_kernel(fields, tail, fixed, strip):
    for f in range(2):
        tall = jnp.concatenate([fields[f], tail[f]], axis=0)
        whole = pltpu.roll(tall, TALL - SHIFT, 0)[:TILE_ROWS]
        fixed[f] = whole
        strip[f] = whole.T[:EDGE]


def return_columns_kernel(fixed, side, phase, heat):
    spare = jnp.zeros((TILE_COLS - EDGE, TILE_ROWS), jnp.float32)
    for f, out in enumerate((phase, heat)):
        wide = jnp.concatenate([fixed[f], jnp.concatenate([side[f], spare], axis=0).T], axis=1)
        out[...] = pltpu.roll(wide, 2 * TILE_COLS - SHIFT, 1)[:, :TILE_COLS]


def columns_forward_kernel(data, first, second, twist_cos, twist_sin, out):
    rows = jnp.concatenate([data[pl.ds(s, OUTER, stride=SLAB), :] for s in range(SLAB)], axis=1)
    spread = dot(first[...], rows)
    cosine, sine = twist_cos[...], twist_sin[...]
    real, imag = [], []
    for s in range(SLAB):
        part = slice(s * 128, (s + 1) * 128)
        re, im = spread[:OUTER, part], spread[OUTER:, part]
        real.append(re * cosine + im * sine)
        imag.append(im * cosine - re * sine)
    for g in range(4):
        span = slice(g * 8, (g + 1) * 8)
        re = jnp.concatenate([part[span] for part in real], axis=0)
        im = jnp.concatenate([part[span] for part in imag], axis=0)
        both = jnp.concatenate([re, im], axis=1)
        final = dot(second[...], both, ((1,), (1,)))
        out[pl.ds(2 * g, 64, stride=8), :] = final[:64]
        out[pl.ds(2 * g + 1, 64, stride=8), :] = final[64:]


def columns_backward_kernel(place, slope, data, first, second, twist_cos, twist_sin, out):
    real, imag = [], []
    for g in range(4):
        span = slice(g * 8, (g + 1) * 8)
        both = jnp.concatenate(
            [data[pl.ds(2 * g, 64, stride=8), :], data[pl.ds(2 * g + 1, 64, stride=8), :]], axis=0
        )
        spread = dot(both, second[...], ((0,), (0,)))
        re = spread[:, :128].reshape(SLAB, 8, 128)
        im = spread[:, 128:].reshape(SLAB, 8, 128)
        cosine, sine = twist_cos[span][None], twist_sin[span][None]
        real.append(re * cosine - im * sine)
        imag.append(im * cosine + re * sine)
    stacked = jnp.concatenate(
        [jnp.concatenate([part[s] for part in real + imag], axis=0) for s in range(SLAB)], axis=1
    )
    mean = jnp.where(place[3] == 0, slope[0, 0], slope[0, 1])
    final = mean - dot(first[...], stacked)
    for s in range(SLAB):
        out[pl.ds(s, OUTER, stride=SLAB), :] = final[:, s * 128 : (s + 1) * 128]


def wave_numbers(place):
    shape = (CHIPS, 128)
    kp = lax.broadcasted_iota(jnp.int32, shape, 0)
    lane = lax.broadcasted_iota(jnp.int32, shape, 1)
    row_freq = kp + CHIPS * (lane // 8)
    col_freq = 8 * place[2] + lane % 8
    row_wave = jnp.where(row_freq >= ROWS // 2, row_freq - ROWS, row_freq).astype(jnp.float32)
    return row_freq, col_freq, row_wave, col_freq.astype(jnp.float32)


def rows_forward_kernel(place, data, first, second, twist_cos, twist_sin, out):
    real = data[pl.ds(0, CHIPS, stride=2), :]
    imag = data[pl.ds(1, CHIPS, stride=2), :]
    spread = dot(first[...], jnp.concatenate([real, imag], axis=1))
    re = spread[:CHIPS, :128] + spread[CHIPS:, 128:]
    im = spread[:CHIPS, 128:] - spread[CHIPS:, :128]
    cosine, sine = twist_cos[...], twist_sin[...]
    turned = jnp.concatenate([re * cosine + im * sine, im * cosine - re * sine], axis=1)
    final = dot(turned, second[...])
    _, _, row_wave, col_wave = wave_numbers(place)
    wave = jnp.where(place[3] == 0, row_wave, col_wave)
    out[:CHIPS] = wave * final[:, :128]
    out[CHIPS:] = wave * final[:, 128:]


def rows_backward_kernel(place, mine, other, first, second, twist_cos, twist_sin, out):
    row_freq, col_freq, row_wave, col_wave = wave_numbers(place)
    valid = (
        (row_freq != ROWS // 2)
        & (col_freq != COLS // 2)
        & ((row_freq != 0) | (col_freq != 0))
    )
    denom = reference_conduct * jnp.maximum(row_wave * row_wave + col_wave * col_wave, 1.0)
    weight = jnp.where(col_freq == 0, 1.0, 2.0) / (ROWS * COLS)
    wave = jnp.where(place[3] == 0, row_wave, col_wave)
    coef = jnp.where(valid, weight * wave / denom, 0.0)
    along = mine[...] + other[...]
    green = jnp.concatenate([coef * along[:CHIPS], coef * along[CHIPS:]], axis=1)
    spread = dot(green, second[...])
    re, im = spread[:, :128], spread[:, 128:]
    cosine, sine = twist_cos[...], twist_sin[...]
    turned = jnp.concatenate([re * cosine - im * sine, im * cosine + re * sine], axis=1)
    final = dot(first[...], turned)
    out[pl.ds(0, CHIPS, stride=2), :] = final[:CHIPS, :128] - final[CHIPS:, 128:]
    out[pl.ds(1, CHIPS, stride=2), :] = final[:CHIPS, 128:] + final[CHIPS:, :128]


def exchange(array, axes, count):
    blocks = array.reshape((count, array.size // count // 128, 128))
    return lax.all_to_all(blocks, axes, split_axis=0, concat_axis=0, tiled=True)


def shift(block, axes, count, step):
    return lax.ppermute(block, axes, [(i, (i + step) % count) for i in range(count)])


def bottom_strip(voxel, wetted, heat):
    bottom = [array[:, TILE_ROWS - EDGE :].astype(jnp.float32) for array in (voxel, wetted, heat)]
    which = lax.broadcasted_iota(jnp.int32, (3, EDGE, TILE_COLS), 0)
    return jnp.where(which == 0, bottom[0], jnp.where(which == 1, bottom[1], bottom[2]))


def body(voxel_material, wetted_indicator, starting_deficit_map, applied_thermal_slope):
    gx_size = lax.axis_size("gx")
    gt_size = lax.axis_size("gt")
    core_size = lax.axis_size("core")
    gy_size = gt_size * core_size
    gx_index = lax.axis_index("gx")
    gt_index = lax.axis_index("gt")
    core_index = lax.axis_index("core")
    gy = ("gt", "core")
    chips = ("gx", "gt")
    place = jnp.stack(
        [gx_index, gt_index * core_size + core_index, gx_index * gt_size + gt_index, core_index]
    ).astype(jnp.int32)
    (col_to, col_back), (row_to, row_back) = column_tables(), row_tables()
    tile = (TILE_ROWS, TILE_COLS)
    voxel, wetted, heat = voxel_material[0], wetted_indicator[0], starting_deficit_map[0]
    porous, phase, heat = call(prepare_kernel, [tile] * 3, voxel, wetted, heat)
    above = shift(bottom_strip(voxel_material, wetted_indicator, starting_deficit_map), "gx", gx_size, 1)
    (strip,) = call(edge_kernel, [(3, EDGE, WIDE)], porous, phase, heat, above)
    left = shift(strip, gy, gy_size, 1)
    fields, polar = call(
        stencil_kernel, [(2,) + tile, (TILE_ROWS // SLAB, 2, SLAB, TILE_COLS)],
        place, applied_thermal_slope, porous, phase, heat, above, left, smem=(0, 1),
    )
    slab = exchange(polar, gy, gy_size).reshape(-1, 128)
    slab = exchange(polar, gy, gy_size).reshape(-1, 128)
    (spec,) = call(columns_forward_kernel, [(2 * CHIPS, 128)], slab, *col_to)
    spec = exchange(spec, chips, CHIPS).reshape(-1, 128)
    (mine,) = call(rows_forward_kernel, [(2 * CHIPS, 128)], place, spec, *row_to, smem=(0,))
    other = lax.ppermute(mine, "core", [(0, 1), (1, 0)])
    (green,) = call(rows_backward_kernel, [(2 * CHIPS, 128)], place, mine, other, *row_back, smem=(0,))
    green, head = lax.optimization_barrier((green, fields[:, :EDGE]))
    tail = shift(head, "gx", gx_size, -1)
    fixed, strip = call(return_rows_kernel, [(2,) + tile, (2, EDGE, TILE_ROWS)], fields, tail)
    green = exchange(green, chips, CHIPS).reshape(-1, 128)
    green, strip = lax.optimization_barrier((green, strip))
    side = shift(strip, gy, gy_size, -1)
    phase_two, heat_two = call(return_columns_kernel, [tile, tile], fixed, side)
    (answer,) = call(
        columns_backward_kernel, [(OUTER * SLAB, 128)],
        place, applied_thermal_slope, green, *col_back, smem=(0, 1),
    )
    gradient = exchange(answer, ("core", "gt"), gy_size).reshape(2, 1, TILE_ROWS, TILE_COLS)
    return (phase_two[None], heat_two[None], gradient)


def solution(mesh):
    gx_size, gy_size = mesh.devices.shape
    fine = Mesh(mesh.devices.reshape(gx_size, gy_size // 2, 2), ("gx", "gt", "core"))
    gy = ("gt", "core")
    in_specs = (P(None, "gx", gy), P(None, "gx", gy), P(None, "gx", gy), P())
    out_specs = (P(None, "gx", gy), P(None, "gx", gy), P(None, None, "gx", gy))
    return jax.shard_map(body, mesh=fine, in_specs=in_specs, out_specs=out_specs, check_vma=False)
```

time: 138 us -> 126 us (0.913)
  blocking collectives: 92.9 us -> 47.1 us
  starting transfers between devices: 19.3 us -> 42.2 us
  waiting for transfers between devices: 11.7 us -> 20.6 us
  local copies, waits for them, and re-layouts: 1.89 us -> 4.21 us
  other arithmetic: 2.41 us -> 0.87 us
    all_to_all x4 -> x2, blocking collectives: 92.9 us -> 47.1 us  [exchange(): return lax.all_to_all(blocks, axes, split_axis=0, concat_axis=0, tiled=True)]
    all_to_all x0 -> x2, starting transfers between devices: none -> 15.3 us  [exchange(): return lax.all_to_all(blocks, axes, split_axis=0, concat_axis=0, tiled=True)]
    all_to_all x0 -> x2, waiting for transfers between devices: none -> 7.77 us  [exchange(): return lax.all_to_all(blocks, axes, split_axis=0, concat_axis=0, tiled=True)]
    ppermute x4, starting transfers between devices: 15.8 us -> 23.4 us  [shift(): lax.ppermute(block, axes, [(i, (i + step) % count) for i in range(count)])]
    unnamed x28 -> x39, local copies, waits for them, and re-layouts: 1.88 us -> 3.52 us
    pallas_call x6 -> x9, Pallas kernels: 8.27 us -> 9.35 us  [call(): pl.pallas_call(kernel, out_shape=shapes, in_specs=spaces, out_specs=[VMEM...]
  transfers between devices with their start and end apart: 5 -> 7, of which waited for: 3 -> 7; matrix products, arithmetic and copies ran while one was open for 0% -> 0% of each run, Pallas kernels for 0% -> 1%
where the time goes in v2:
time: 126 us; the launch traced here: 125 us
  blocking collectives  47.1 us (37%)
  starting transfers between devices  42.2 us (33%)
  waiting for transfers between devices  20.6 us (16%)
  Pallas kernels  9.35 us (7%)
  local copies, waits for them, and re-layouts  4.21 us (3%)
    all_to_all x2, blocking collectives, exchange(): return lax.all_to_all(blocks, axes, split_axis=0, concat_axis=0, tiled=True)  47.1 us
    ppermute x4, starting transfers between devices, shift(): lax.ppermute(block, axes, [(i, (i + step) % count) for i in range(count)])  23.4 us
    all_to_all x2, starting transfers between devices, exchange(): return lax.all_to_all(blocks, axes, split_axis=0, concat_axis=0, tiled=True)  15.3 us
    ppermute x4, waiting for transfers between devices, shift(): lax.ppermute(block, axes, [(i, (i + step) % count) for i in range(count)])  11.7 us
    pallas_call x9, Pallas kernels, call(): pl.pallas_call(kernel, out_shape=shapes, in_specs=spaces, out_specs=[VMEM...  9.35 us
    all_to_all x2, waiting for transfers between devices, exchange(): return lax.all_to_all(blocks, axes, split_axis=0, concat_axis=0, tiled=True)  7.77 us
    ppermute x1, starting transfers between devices, body(): other = lax.ppermute(mine, 'core', [(0, 1), (1, 0)])  3.52 us
    unnamed x39, local copies, waits for them, and re-layouts  3.52 us
  transfers between devices with their start and end apart: 7, of which 7 were waited for; matrix products, arithmetic and copies ran while one was open for 0% of the time, Pallas kernels for 1%

profile of v2, /device:TPU:1, one launch (start us, length us, event | category | flops | bytes accessed | tf_op | source)
XLA Modules:
  0.0 125.4 jit_solution(1762633409385885476)
XLA Ops:
  0.6 0.7 slice_bitcast_fusion
  1.3 0.7 convert_bitcast_fusion
  2.0 0.1 select_select_fusion
  2.1 8.3 %collective-permute-start = (f32[3,8,128]{2,1,0:T(8,128)S(1)}, f32[3,8,128]{2,1,0:T(8,128)S(1)}, u32[]{:S(2)}, u32[]{:S(2)}) collective-permute-start(f32[3,8,128]{2,1,0:T(8,128)S(1)} %select_select_fusion), channel_id=1, source_target_pairs={{0,32},{32,64},{64,96},{96,128},{128,160},{160,192},{192,224},{224... | collective-permute-start | bytes 36872 | tf_op jit(solution)/shard_map/ppermute | solution.py:295
  10.4 0.0 copy-start.3
  10.4 0.9 copy-done.3
  11.3 0.9 copy-done.4
  12.2 0.9 copy-done.5
  13.2 6.8 %collective-permute-done.above = f32[3,8,128]{2,1,0:T(8,128)S(1)} collective-permute-done((f32[3,8,128]{2,1,0:T(8,128)S(1)}, f32[3,8,128]{2,1,0:T(8,128)S(1)}, u32[]{:S(2)}, u32[]{:S(2)}) %collective-permute-start) | collective-permute-done | bytes 12320 | tf_op jit(solution)/shard_map/ppermute | solution.py:295
  19.9 0.2 shard_map.203
  20.2 3.7 %collective-permute-start.1 = (f32[3,8,384]{2,1,0:T(8,128)S(1)}, f32[3,8,384]{2,1,0:T(8,128)S(1)}, u32[]{:S(2)}, u32[]{:S(2)}) collective-permute-start(f32[3,8,384]{2,1,0:T(8,128)S(1)} %shard_map.203), channel_id=1, source_target_pairs={{0,1},{1,2},{2,3},{3,4},{4,5},{5,6},{6,7},{7,8},{8,9},{9,10},{10,1... | collective-permute-start | bytes 110600 | tf_op jit(solution)/shard_map/ppermute | solution.py:295
  23.9 0.0 copy-start.18
  23.9 0.1 pad_add_fusion.place
  24.0 0.9 collective-permute-done.1.left
  25.0 0.0 copy-done.18
  25.0 2.0 %shard_map.204 = (f32[2,256,128]{2,1,0:T(8,128)S(1)}, f32[16,2,16,128]{3,2,1,0:T(8,128)S(1)}) custom-call(s32[4]{0:T(128)S(1)} %pad_add_fusion.place, f32[1,2]{1,0:T(1,128)S(1)} %copy-done.18, f32[256,128]{1,0:T(8,128)S(1)} %get-tuple-element.16.porous, f32[256,128]{1,0:T(8,128)S(1)} %get-tuple-element.17.phase, f32[256,128]{1,0:T(8,128)S(1)} %get-tuple-element.18.heat, ...), custom_call_target="tpu_custom_call" | custom-call | tf_op jit(solution)/shard_map/pallas_call | solution.py:58
  27.0 0.0 copy-start.9
  27.0 0.0 copy-start.12
  27.0 0.0 copy-start.16
  27.0 0.0 copy-start.17
  27.0 20.4 %all_to_all.20 = f32[32,16,128]{2,1,0:T(8,128)S(1)} all-to-all(f32[32,16,128]{2,1,0:T(8,128)S(1)} %bitcast.27), channel_id=1, replica_groups=mesh['gx'=16,'gt'=16,'core'=2] {'gt','core'}, dimensions={0} | all-to-all | bytes 524288 | tf_op jit(solution)/shard_map/all_to_all | solution.py:291
  47.4 0.0 copy-done.9
  47.5 0.0 copy-done.12
  47.5 0.0 copy-done.16
  47.5 0.0 copy-done.17
  47.5 0.0 copy-start
  47.5 0.7 shard_map.205
  48.2 0.0 copy-start.2
  48.2 0.0 copy-start.6
  48.3 0.0 copy-start.7
  48.3 26.7 %all_to_all.21 = f32[256,2,128]{2,1,0:T(2,128)S(1)} all-to-all(f32[256,2,128]{2,1,0:T(2,128)S(1)} %bitcast.25), channel_id=1, replica_groups=mesh['gx'=16,'gt'=16,'core'=2] {'gx','gt'}, dimensions={0} | all-to-all | bytes 524288 | tf_op jit(solution)/shard_map/all_to_all | solution.py:291
  75.0 0.0 copy-done
  75.0 0.0 copy-done.2
  75.0 0.0 copy-done.6
  75.0 0.0 copy-done.7
  75.0 0.0 copy-start.1
  75.1 0.0 copy-start.10
  75.1 0.0 copy-start.11
  75.1 1.3 %shard_map.206.mine = f32[512,128]{1,0:T(8,128)S(1)} custom-call(s32[4]{0:T(128)S(1)} %pad_add_fusion.place, f32[512,128]{1,0:T(8,128)S(1)} %bitcast.26, f32[512,256]{1,0:T(8,128)S(1)} %copy-done, f32[256,256]{1,0:T(8,128)S(1)} %copy-done.2, f32[256,128]{1,0:T(8,128)S(1)} %copy-done.6, f32[256,128]{1,0:T(8,128)S(1)} %copy-done.7), custom_call_target="tpu_custom_call" | custom-call | tf_op jit(solution)/shard_map/pallas_call | solution.py:58
  76.4 3.5 %collective-permute-start.2 = (f32[512,128]{1,0:T(8,128)S(1)}, f32[512,128]{1,0:T(8,128)S(1)}, u32[]{:S(2)}, u32[]{:S(2)}) collective-permute-start(f32[512,128]{1,0:T(8,128)S(1)} %shard_map.206.mine), channel_id=1, source_target_pairs={{0,1},{1,0},{2,3},{3,2},{4,5},{5,4},{6,7},{7,6},{8,9},{9,8},{10,11... | collective-permute-start | bytes 786440 | tf_op jit(solution)/shard_map/ppermute | solution.py:333
  79.9 1.1 collective-permute-done.2.other
  81.0 0.0 copy-done.1
  81.0 0.0 copy-done.10
  81.0 0.0 copy-done.11
  81.0 2.1 %shard_map.207 = f32[512,128]{1,0:T(8,128)} custom-call(s32[4]{0:T(128)S(1)} %pad_add_fusion.place, f32[512,128]{1,0:T(8,128)S(1)} %shard_map.206.mine, f32[512,128]{1,0:T(8,128)S(1)} %collective-permute-done.2.other, f32[512,256]{1,0:T(8,128)S(1)} %copy-done, f32[256,256]{1,0:T(8,128)S(1)} %copy-done.1, f32[256,128]{1,0:T(8,128)S(1)} %copy-done.10, ...), custom_call_target="tpu_custom_call" | custom-call | tf_op jit(solution)/shard_map/pallas_call | solution.py:58
  83.1 9.2 %all-to-all-start.2 = ((f32[256,2,128]{2,1,0:T(2,128)}), f32[256,2,128]{2,1,0:T(2,128)S(1)}, u32[]{:S(2)}, u32[]{:S(2)}) async-start(f32[256,2,128]{2,1,0:T(2,128)} %bitcast.14), calls=%async_computation.2 | async-start | bytes 524288 | tf_op jit(solution)/shard_map/all_to_all | solution.py:291
  92.3 0.0 copy-start.8
  92.3 0.0 copy-start.13
  92.3 0.0 copy-start.14
  92.3 0.0 copy-start.15
  92.4 9.3 %collective-permute-start.3 = (f32[2,8,128]{2,1,0:T(8,128)S(1)}, f32[2,8,128]{2,1,0:T(8,128)S(1)}, u32[]{:S(2)}, u32[]{:S(2)}) collective-permute-start(f32[2,8,128]{2,1,0:T(8,128)S(1)} %slice.15), channel_id=1, source_target_pairs={{0,480},{32,0},{64,32},{96,64},{128,96},{160,128},{192,160},{224,1... | collective-permute-start | bytes 24584 | tf_op jit(solution)/shard_map/ppermute | solution.py:295
  101.6 0.8 collective-permute-done.3.tail
  102.4 0.1 shard_map.208
  102.5 3.8 %all-to-all-done.2 = f32[256,2,128]{2,1,0:T(2,128)S(1)} async-done(((f32[256,2,128]{2,1,0:T(2,128)}), f32[256,2,128]{2,1,0:T(2,128)S(1)}, u32[]{:S(2)}, u32[]{:S(2)}) %all-to-all-start.2) | async-done | bytes 262176 | tf_op jit(solution)/shard_map/all_to_all | solution.py:291
  106.3 0.0 copy-done.8
  106.3 0.0 copy-done.13
  106.3 0.0 copy-done.14
  106.3 1.9 %shard_map.210 = f32[512,128]{1,0:T(8,128)} custom-call(s32[4]{0:T(128)S(1)} %pad_add_fusion.place, f32[1,2]{1,0:T(1,128)S(1)} %copy-done.18, f32[512,128]{1,0:T(8,128)S(1)} %bitcast.23, f32[32,64]{1,0:T(8,128)S(1)} %copy-done.13, f32[128,256]{1,0:T(8,128)S(1)} %copy-done.8, f32[32,128]{1,0:T(8,128)S(1)} %copy-done.14, f32[32,128]{1,0:T(8,128)S(1)} %copy-done.15), custom_call_target="tpu_custom_call" | custom-call | tf_op jit(solution)/shard_map/pallas_call | solution.py:58
  108.2 6.1 %all-to-all-start.3 = ((f32[32,16,128]{2,1,0:T(8,128)}), f32[32,16,128]{2,1,0:T(8,128)S(1)}, u32[]{:S(2)}, u32[]{:S(2)}) async-start(f32[32,16,128]{2,1,0:T(8,128)} %bitcast.18), calls=%async_computation.3 | async-start | bytes 524288 | tf_op jit(solution)/shard_map/all_to_all | solution.py:291
  114.3 2.2 %collective-permute-start.4 = (f32[2,8,256]{2,1,0:T(8,128)S(1)}, f32[2,8,256]{2,1,0:T(8,128)S(1)}, u32[]{:S(2)}, u32[]{:S(2)}) collective-permute-start(f32[2,8,256]{2,1,0:T(8,128)S(1)} %get-tuple-element.25), channel_id=1, source_target_pairs={{0,31},{1,0},{2,1},{3,2},{4,3},{5,4},{6,5},{7,6},{8,7},{9,8},{10,9... | collective-permute-start | bytes 49160 | tf_op jit(solution)/shard_map/ppermute | solution.py:295
  116.5 3.2 %collective-permute-done.4.side = f32[2,8,256]{2,1,0:T(8,128)S(1)} collective-permute-done((f32[2,8,256]{2,1,0:T(8,128)S(1)}, f32[2,8,256]{2,1,0:T(8,128)S(1)}, u32[]{:S(2)}, u32[]{:S(2)}) %collective-permute-start.4) | collective-permute-done | bytes 16416 | tf_op jit(solution)/shard_map/ppermute | solution.py:295
  119.7 0.9 shard_map.209
  120.7 4.0 %all-to-all-done.3 = f32[32,16,128]{2,1,0:T(8,128)S(1)} async-done(((f32[32,16,128]{2,1,0:T(8,128)}), f32[32,16,128]{2,1,0:T(8,128)S(1)}, u32[]{:S(2)}, u32[]{:S(2)}) %all-to-all-start.3) | async-done | bytes 262176 | tf_op jit(solution)/shard_map/all_to_all | solution.py:291
  124.7 0.7 copy.23
  (6 shorter events, 0.0 us)
Async XLA Ops:
  2.1 17.8 %collective-permute-start = (f32[3,8,128]{2,1,0:T(8,128)S(1)}, f32[3,8,128]{2,1,0:T(8,128)S(1)}, u32[]{:S(2)}, u32[]{:S(2)}) collective-permute-start(f32[3,8,128]{2,1,0:T(8,128)S(1)} %select_select_fusion), channel_id=1, source_target_pairs={{0,32},{32,64},{64,96},{96,128},{128,160},{160,192},{192,224},{224... | collective-permute-start | bytes 36872 | tf_op jit(solution)/shard_map/ppermute | solution.py:295
  10.4 0.9 copy-start.3
  11.3 0.9 copy-start.4
  12.2 0.9 copy-start.5
  20.2 4.8 %collective-permute-start.1 = (f32[3,8,384]{2,1,0:T(8,128)S(1)}, f32[3,8,384]{2,1,0:T(8,128)S(1)}, u32[]{:S(2)}, u32[]{:S(2)}) collective-permute-start(f32[3,8,384]{2,1,0:T(8,128)S(1)} %shard_map.203), channel_id=1, source_target_pairs={{0,1},{1,2},{2,3},{3,4},{4,5},{5,6},{6,7},{7,8},{8,9},{9,10},{10,1... | collective-permute-start | bytes 110600 | tf_op jit(solution)/shard_map/ppermute | solution.py:295
  23.9 1.0 copy-start.18
  27.0 20.5 %copy-start.9 = (f32[128,256]{1,0:T(8,128)S(1)}, f32[128,256]{1,0:T(8,128)}, u32[]{:S(2)}) copy-start(f32[128,256]{1,0:T(8,128)} %constant.51.clone.second) | copy-start | bytes 393220
  27.0 20.4 %copy-start.12 = (f32[64,32]{1,0:T(8,128)S(1)}, f32[64,32]{1,0:T(8,128)}, u32[]{:S(2)}) copy-start(f32[64,32]{1,0:T(8,128)} %constant.50.clone.first) | copy-start | bytes 24580
  27.0 20.4 %copy-start.16 = (f32[32,128]{1,0:T(8,128)S(1)}, f32[32,128]{1,0:T(8,128)}, u32[]{:S(2)}) copy-start(f32[32,128]{1,0:T(8,128)} %constant.52.clone.twist_cos) | copy-start | bytes 49156
  27.0 20.4 %copy-start.17 = (f32[32,128]{1,0:T(8,128)S(1)}, f32[32,128]{1,0:T(8,128)}, u32[]{:S(2)}) copy-start(f32[32,128]{1,0:T(8,128)} %constant.53.clone.twist_sin) | copy-start | bytes 49156
  47.5 27.6 %copy-start = (f32[512,256]{1,0:T(8,128)S(1)}, f32[512,256]{1,0:T(8,128)}, u32[]{:S(2)}) copy-start(f32[512,256]{1,0:T(8,128)} %constant.58.clone.first) | copy-start | bytes 1572868
  48.2 26.8 %copy-start.2 = (f32[256,256]{1,0:T(8,128)S(1)}, f32[256,256]{1,0:T(8,128)}, u32[]{:S(2)}) copy-start(f32[256,256]{1,0:T(8,128)} %constant.59.clone.second) | copy-start | bytes 786436
  48.2 26.8 %copy-start.6 = (f32[256,128]{1,0:T(8,128)S(1)}, f32[256,128]{1,0:T(8,128)}, u32[]{:S(2)}) copy-start(f32[256,128]{1,0:T(8,128)} %constant.60.clone.twist_cos) | copy-start | bytes 393220
  48.3 26.8 %copy-start.7 = (f32[256,128]{1,0:T(8,128)S(1)}, f32[256,128]{1,0:T(8,128)}, u32[]{:S(2)}) copy-start(f32[256,128]{1,0:T(8,128)} %constant.61.clone.twist_sin) | copy-start | bytes 393220
  75.0 6.0 %copy-start.1 = (f32[256,256]{1,0:T(8,128)S(1)}, f32[256,256]{1,0:T(8,128)}, u32[]{:S(2)}) copy-start(f32[256,256]{1,0:T(8,128)} %constant.62.clone.second) | copy-start | bytes 786436
  75.1 6.0 %copy-start.10 = (f32[256,128]{1,0:T(8,128)S(1)}, f32[256,128]{1,0:T(8,128)}, u32[]{:S(2)}) copy-start(f32[256,128]{1,0:T(8,128)} %constant.63.clone.twist_cos) | copy-start | bytes 393220
  75.1 6.0 %copy-start.11 = (f32[256,128]{1,0:T(8,128)S(1)}, f32[256,128]{1,0:T(8,128)}, u32[]{:S(2)}) copy-start(f32[256,128]{1,0:T(8,128)} %constant.64.clone.twist_sin) | copy-start | bytes 393220
  76.4 4.7 %collective-permute-start.2 = (f32[512,128]{1,0:T(8,128)S(1)}, f32[512,128]{1,0:T(8,128)S(1)}, u32[]{:S(2)}, u32[]{:S(2)}) collective-permute-start(f32[512,128]{1,0:T(8,128)S(1)} %shard_map.206.mine), channel_id=1, source_target_pairs={{0,1},{1,0},{2,3},{3,2},{4,5},{5,4},{6,7},{7,6},{8,9},{9,8},{10,11... | collective-permute-start | bytes 786440 | tf_op jit(solution)/shard_map/ppermute | solution.py:333
  83.1 23.1 %all-to-all-start.2 = ((f32[256,2,128]{2,1,0:T(2,128)}), f32[256,2,128]{2,1,0:T(2,128)S(1)}, u32[]{:S(2)}, u32[]{:S(2)}) async-start(f32[256,2,128]{2,1,0:T(2,128)} %bitcast.14), calls=%async_computation.2 | async-start | bytes 524288 | tf_op jit(solution)/shard_map/all_to_all | solution.py:291
  92.3 14.0 %copy-start.8 = (f32[128,256]{1,0:T(8,128)S(1)}, f32[128,256]{1,0:T(8,128)}, u32[]{:S(2)}) copy-start(f32[128,256]{1,0:T(8,128)} %constant.55.clone.second) | copy-start | bytes 393220
  92.3 14.0 %copy-start.13 = (f32[32,64]{1,0:T(8,128)S(1)}, f32[32,64]{1,0:T(8,128)}, u32[]{:S(2)}) copy-start(f32[32,64]{1,0:T(8,128)} %constant.54.clone.first) | copy-start | bytes 24580
  92.3 14.0 %copy-start.14 = (f32[32,128]{1,0:T(8,128)S(1)}, f32[32,128]{1,0:T(8,128)}, u32[]{:S(2)}) copy-start(f32[32,128]{1,0:T(8,128)} %constant.56.clone.twist_cos) | copy-start | bytes 49156
  92.3 13.9 %copy-start.15 = (f32[32,128]{1,0:T(8,128)S(1)}, f32[32,128]{1,0:T(8,128)}, u32[]{:S(2)}) copy-start(f32[32,128]{1,0:T(8,128)} %constant.57.clone.twist_sin) | copy-start | bytes 49156
  92.4 10.1 %collective-permute-start.3 = (f32[2,8,128]{2,1,0:T(8,128)S(1)}, f32[2,8,128]{2,1,0:T(8,128)S(1)}, u32[]{:S(2)}, u32[]{:S(2)}) collective-permute-start(f32[2,8,128]{2,1,0:T(8,128)S(1)} %slice.15), channel_id=1, source_target_pairs={{0,480},{32,0},{64,32},{96,64},{128,96},{160,128},{192,160},{224,1... | collective-permute-start | bytes 24584 | tf_op jit(solution)/shard_map/ppermute | solution.py:295
  108.2 16.4 %all-to-all-start.3 = ((f32[32,16,128]{2,1,0:T(8,128)}), f32[32,16,128]{2,1,0:T(8,128)S(1)}, u32[]{:S(2)}, u32[]{:S(2)}) async-start(f32[32,16,128]{2,1,0:T(8,128)} %bitcast.18), calls=%async_computation.3 | async-start | bytes 524288 | tf_op jit(solution)/shard_map/all_to_all | solution.py:291
  114.3 5.4 %collective-permute-start.4 = (f32[2,8,256]{2,1,0:T(8,128)S(1)}, f32[2,8,256]{2,1,0:T(8,128)S(1)}, u32[]{:S(2)}, u32[]{:S(2)}) collective-permute-start(f32[2,8,256]{2,1,0:T(8,128)S(1)} %get-tuple-element.25), channel_id=1, source_target_pairs={{0,31},{1,0},{2,1},{3,2},{4,3},{5,4},{6,5},{7,6},{8,7},{9,8},{10,9... | collective-permute-start | bytes 49160 | tf_op jit(solution)/shard_map/ppermute | solution.py:295

commit v3 on v2

v3 whole, which is shorter than its diff:
```python
import functools
import math

import jax
import jax.numpy as jnp
import numpy as np
from jax import lax
from jax.experimental import pallas as pl
from jax.experimental.pallas import tpu as pltpu
from jax.sharding import Mesh
from jax.sharding import PartitionSpec as P

solid_conduct = 1.7
gas_conduct = 0.026
liquid_conduct = 0.6
reference_conduct = 0.863
step_grad = 0.1
step_well = 0.3
step_drive = 0.2
step_heat = 0.12
latent_heat = 0.5
gradient_gain = 0.5

TILE_ROWS = 256
TILE_COLS = 128
EDGE = 8
SHIFT = 2
TALL = TILE_ROWS + EDGE
WIDE = 384
OUTER = 32
SLAB = 16
SPAN = 20
HALF = 64
BLOCK = SLAB + 4
CHIPS = 256
COLS = 4096
ROWS = 4096
CORE_MAJOR = np.arange(OUTER).reshape(-1, 2).T.reshape(-1)
VMEM = pl.BlockSpec(memory_space=pltpu.VMEM)
SMEM = pl.BlockSpec(memory_space=pltpu.SMEM)


def halves(array):
    high = array.astype(jnp.bfloat16)
    return high, (array - high.astype(jnp.float32)).astype(jnp.bfloat16)


def dot(left, right, contract=((1,), (0,))):
    def product(x, y):
        return lax.dot_general(x, y, (contract, ((), ())), preferred_element_type=jnp.float32)

    (left_high, left_low), (right_high, right_low) = left, right
    return product(left_high, right_high) + (
        product(left_high, right_low) + product(left_low, right_high)
    )


def call(kernel, outs, *args, smem=(), scratch=()):
    shapes = [jax.ShapeDtypeStruct(shape, jnp.float32) for shape in outs]
    spaces = [SMEM if i in smem else VMEM for i in range(len(args))]
    return pl.pallas_call(
        kernel,
        out_shape=shapes,
        in_specs=spaces,
        out_specs=[VMEM] * len(outs),
        scratch_shapes=list(scratch),
        compiler_params=pltpu.CompilerParams(vmem_limit_bytes=32 * 1024 * 1024),
    )(*args)


def angles(left, right, length):
    product = np.outer(np.arange(left), np.asarray(right)) % length
    return 2.0 * math.pi / length * product


def table(array):
    return jnp.asarray(np.asarray(array, dtype=np.float32))


def split_table(array):
    array = np.asarray(array, dtype=np.float32)
    high = array.astype(jnp.bfloat16)
    low = (array - high.astype(np.float32)).astype(jnp.bfloat16)
    return jnp.asarray(np.stack([high, low]))


def column_tables():
    first = angles(OUTER, range(OUTER), OUTER)
    cosine, sine = np.cos(first), np.sin(first)
    second = angles(64, range(128), 128)
    twist = angles(OUTER, range(128), COLS)
    mix = np.block([[np.cos(second), np.sin(second)], [-np.sin(second), np.cos(second)]])
    rest = [split_table(mix), table(np.cos(twist)), table(np.sin(twist))]
    slot, s = np.divmod(np.arange(4 * SLAB), SLAB)
    order = np.zeros((128, 128))
    order[np.arange(4 * SLAB), EDGE * s + slot] = 1.0
    stacked = np.concatenate([cosine, -sine], axis=0)
    forward = [split_table(order), split_table(stacked)] + rest
    backward = [split_table(np.concatenate([cosine, -sine], axis=1)[CORE_MAJOR])] + rest
    return forward, backward


def row_tables():
    first = angles(CHIPS, range(CHIPS), CHIPS)
    both = split_table(np.concatenate([np.cos(first), np.sin(first)], axis=0))
    tables = []
    for shift, sign in ((SHIFT, -1.0), (0, 1.0)):
        inner = np.arange(SLAB) - shift
        second = angles(SLAB, inner, SLAB)
        twist = np.repeat(angles(CHIPS, inner, ROWS), 8, axis=1)
        cosine, sine = np.kron(np.cos(second), np.eye(8)), sign * np.kron(np.sin(second), np.eye(8))
        if shift:
            cosine, sine = cosine.T, sine.T
        mix = np.block([[cosine, sine], [-sine, cosine]])
        tables.append([both, split_table(mix), table(np.cos(twist)), table(np.sin(twist))])
    return tables


GX, GY, CHIP, CORE, SLOPE_X, SLOPE_Y, SLOPE = range(7)


def prepare_kernel(place, slope, porous, phase, heat, info, strip):
    values = [place[i].astype(jnp.float32) for i in range(4)] + [slope[0, 0], slope[0, 1]]
    values.append(jnp.where(place[3] == 0, slope[0, 0], slope[0, 1]))
    row = lax.broadcasted_iota(jnp.int32, info.shape, 0)
    filled = jnp.zeros(info.shape, jnp.float32)
    for i, value in enumerate(values):
        filled = jnp.where(row == i, value, filled)
    info[...] = filled
    for f, field in enumerate((porous, phase, heat)):
        strip[f] = field[:EDGE, :]


def known(info, i):
    return info[i : i + 1, :]


def with_above(above, porous, phase, heat):
    tops = (above[0], above[0] * above[1], -above[2])
    return [
        jnp.concatenate([top, field[...]], axis=0) for top, field in zip(tops, (porous, phase, heat))
    ]


def with_both(above, below, porous, phase, heat):
    talls = with_above(above, porous, phase, heat)
    return [jnp.concatenate([tall, below[f]], axis=0) for f, tall in enumerate(talls)]


def edge_kernel(porous, phase, heat, above, below, first, last):
    spare = jnp.zeros((WIDE - TALL - EDGE, TILE_COLS), jnp.float32)
    for f, tall in enumerate(with_both(above, below, porous, phase, heat)):
        flipped = jnp.concatenate([tall, spare], axis=0).T
        first[f] = flipped[:EDGE]
        last[f] = flipped[TILE_COLS - EDGE :]


def progress(phase, heat, porous, phase_lap, heat_lap):
    well = 2.0 * phase * (1.0 - phase) * (1.0 - 2.0 * phase)
    growth = 30.0 * phase * phase * (1.0 - phase) * (1.0 - phase)
    new_phase = porous * (
        phase + step_grad * phase_lap - step_well * well + step_drive * heat * growth
    )
    new_heat = heat + step_heat * heat_lap - latent_heat * (new_phase - phase)
    return new_phase, new_heat


def stencil(porous, phase, heat, neighbours):
    def laplace(around, field):
        return around[0] + around[1] + around[2] + around[3] - 6.0 * field

    phase_lap, heat_lap = laplace(neighbours(phase), phase), laplace(neighbours(heat), heat)
    phase, heat = progress(phase, heat, porous, phase_lap, heat_lap)
    around = neighbours(heat)
    phase_lap, heat_lap = laplace(neighbours(phase), phase), laplace(around, heat)
    phase, heat = progress(phase, heat, porous, phase_lap, heat_lap)
    return phase, heat, around[0] - around[1], around[2] - around[3]


def roll(field, step, axis):
    return pltpu.roll(field, step % field.shape[axis], axis)


def walled(wall, field):
    return field if wall is None else jnp.where(wall, 0.0, field)


def ring_neighbours(walls):
    def neighbours(field):
        moves = ((-1, 0), (1, 0), (-1, 1), (1, 1))
        return [walled(wall, roll(field, *move)) for move, wall in zip(moves, walls)]

    return neighbours


def conductivity_contrast(porous, phase):
    conduct = (
        porous * (gas_conduct + (liquid_conduct - gas_conduct) * phase)
        + (1.0 - porous) * solid_conduct
    )
    return conduct - reference_conduct


def shifted_rows(field):
    return roll(field, SHIFT - EDGE, 0)[:TILE_ROWS]


def row_walls(first, row):
    return first & (row == EDGE - 1), first & (row == EDGE)


def polar_kernel(info, porous, phase, heat, above, out):
    talls = with_above(above, porous, phase, heat)
    row = lax.broadcasted_iota(jnp.int32, talls[0].shape, 0)
    walls = row_walls(known(info, GX) == 0.0, row) + (None, None)
    phase_two, _, along_rows, along_columns = stencil(*talls, ring_neighbours(walls))
    contrast = conductivity_contrast(talls[0], phase_two)
    polars = (
        shifted_rows(contrast * (known(info, SLOPE_X) + gradient_gain * along_rows)),
        shifted_rows(contrast * (known(info, SLOPE_Y) + gradient_gain * along_columns)),
    )
    spare = jnp.zeros((WIDE - TALL, TILE_COLS), jnp.float32)
    sublane = lax.broadcasted_iota(jnp.int32, (EDGE, WIDE), 0)
    lane = lax.broadcasted_iota(jnp.int32, (EDGE, TILE_COLS), 1)
    edges = []
    for tall in talls:
        flipped = jnp.concatenate([tall, spare], axis=0).T
        edges.append(jnp.where(sublane < 4, flipped[:EDGE], flipped[TILE_COLS - EDGE :]))
    for x in range(TILE_ROWS // SLAB):
        first = EDGE - 2 * SHIFT + SLAB * x
        windows = [
            roll(edge, f * SPAN - first, 1)[:, :TILE_COLS] for f, edge in enumerate(edges)
        ]
        packed = jnp.where(
            lane < SPAN, windows[0], jnp.where(lane < 2 * SPAN, windows[1], windows[2])
        )
        packed = jnp.where(lane < HALF, packed, roll(roll(packed, HALF, 1), 4, 0))
        for f in range(2):
            start = (2 * x + f) * BLOCK
            out[start : start + SLAB, :] = polars[f][x * SLAB : (x + 1) * SLAB]
            out[start + SLAB : start + BLOCK, :] = packed[:4]


def fields_kernel(info, porous, phase, heat, above, below, left, right, phase_out, heat_out):
    spare = jnp.zeros((TILE_COLS - 2 * EDGE, WIDE), jnp.float32)
    wides = []
    for f, tall in enumerate(with_both(above, below, porous, phase, heat)):
        side = jnp.concatenate([right[f], spare, left[f]], axis=0).T
        wides.append(jnp.concatenate([tall, side[: TALL + EDGE]], axis=1))
    shape = wides[0].shape
    row = lax.broadcasted_iota(jnp.int32, shape, 0)
    column = lax.broadcasted_iota(jnp.int32, shape, 1)
    gx, gy = (jnp.concatenate([known(info, i)] * 2, axis=1) for i in (GX, GY))
    top, bottom = gx == 0.0, gx == ROWS // TILE_ROWS - 1
    start, end = gy == 0.0, gy == COLS // TILE_COLS - 1
    walls = (
        (top & (row == EDGE - 1)) | (bottom & (row == TALL - 1)),
        (top & (row == EDGE)) | (bottom & (row == TALL)),
        (start & (column == shape[1] - 1)) | (end & (column == TILE_COLS - 1)),
        (start & (column == 0)) | (end & (column == TILE_COLS)),
    )
    phase_two, heat_two, _, _ = stencil(*wides, ring_neighbours(walls))
    phase_out[...] = phase_two[EDGE:TALL, :TILE_COLS]
    heat_out[...] = heat_two[EDGE:TALL, :TILE_COLS]


def edge_polar(info, data):
    raw = jnp.concatenate([data[pl.ds(SLAB + c, OUTER, stride=BLOCK), :] for c in range(4)], axis=0)
    fields = [raw] + [roll(raw, -f * SPAN, 1) for f in (1, 2)]
    lane = lax.broadcasted_iota(jnp.int32, raw.shape, 1)
    row = lane % HALF
    first = known(info, CHIP) == 0.0
    down_wall, up_wall = first & (row == 2 * SHIFT - 1), first & (row == 2 * SHIFT)
    tile = lax.broadcasted_iota(jnp.int32, (OUTER, TILE_COLS), 0)

    def neighbours(field):
        after = walled(tile == OUTER - 1, roll(roll(field[:OUTER], -1, 0), HALF, 1))
        before = walled(tile == 0, roll(roll(field[3 * OUTER :], 1, 0), HALF, 1))
        return (
            walled(down_wall, roll(field, -1, 1)),
            walled(up_wall, roll(field, 1, 1)),
            jnp.concatenate([field[OUTER:], after], axis=0),
            jnp.concatenate([before, field[: 3 * OUTER]], axis=0),
        )

    phase, _, along_rows, along_columns = stencil(*fields, neighbours)
    along = jnp.where(known(info, CORE) == 0.0, along_rows, along_columns)
    polar = conductivity_contrast(raw, phase) * (known(info, SLOPE) + gradient_gain * along)
    return [polar[c * OUTER : (c + 1) * OUTER] for c in range(4)]


def columns_forward_kernel(info, data, order, first, second, twist_cos, twist_sin, out):
    edges = edge_polar(info, data)
    lane = lax.broadcasted_iota(jnp.int32, (OUTER, TILE_COLS), 1)
    packed = jnp.zeros((OUTER, TILE_COLS), jnp.float32)
    for slot, column in enumerate((2, 3, 0, 1)):
        start = SHIFT + (HALF if column >= 2 else 0)
        moved = roll(edges[column], SLAB * slot - start, 1)
        packed = jnp.where(lane // SLAB == slot, moved, packed)
    packed = dot(halves(packed), (order[0], order[1]))
    outer = (lane < SHIFT) | (lane >= TILE_COLS - SHIFT)
    parts = []
    for s in range(SLAB):
        around = roll(packed, -EDGE * s - SHIFT, 1)
        parts.append(jnp.where(outer, around, data[pl.ds(s, OUTER, stride=BLOCK), :]))
    rows = jnp.concatenate(parts, axis=1)
    spread = dot((first[0], first[1]), halves(rows))
    cosine, sine = twist_cos[...], twist_sin[...]
    real, imag = [], []
    for s in range(SLAB):
        part = slice(s * 128, (s + 1) * 128)
        re, im = spread[:OUTER, part], spread[OUTER:, part]
        real.append(re * cosine + im * sine)
        imag.append(im * cosine - re * sine)
    for g in range(4):
        span = slice(g * 8, (g + 1) * 8)
        re = jnp.concatenate([part[span] for part in real], axis=0)
        im = jnp.concatenate([part[span] for part in imag], axis=0)
        both = jnp.concatenate([re, im], axis=1)
        final = dot((second[0], second[1]), halves(both), ((1,), (1,)))
        out[pl.ds(2 * g, 64, stride=8), :] = final[:64]
        out[pl.ds(2 * g + 1, 64, stride=8), :] = final[64:]


def columns_backward_kernel(info, data, first, second, twist_cos, twist_sin, out):
    real, imag = [], []
    for g in range(4):
        span = slice(g * 8, (g + 1) * 8)
        both = jnp.concatenate(
            [data[pl.ds(2 * g, 64, stride=8), :], data[pl.ds(2 * g + 1, 64, stride=8), :]], axis=0
        )
        spread = dot(halves(both.T), (second[0], second[1]))
        re = spread[:, :128].reshape(SLAB, 8, 128)
        im = spread[:, 128:].reshape(SLAB, 8, 128)
        cosine, sine = twist_cos[span][None], twist_sin[span][None]
        real.append(re * cosine - im * sine)
        imag.append(im * cosine + re * sine)
    stacked = jnp.concatenate(
        [jnp.concatenate([part[s] for part in real + imag], axis=0) for s in range(SLAB)], axis=1
    )
    final = dot((first[0], first[1]), halves(stacked))
    for s in range(SLAB):
        part = final[:, s * 128 : (s + 1) * 128]
        out[pl.ds(s, OUTER, stride=SLAB), :] = known(info, SLOPE) - part


def wave_numbers(info):
    shape = (CHIPS, 128)
    lane = lax.broadcasted_iota(jnp.int32, shape, 1)
    row_freq = lax.broadcasted_iota(jnp.int32, shape, 0) + CHIPS * (lane // 8)
    row_wave = jnp.where(row_freq >= ROWS // 2, row_freq - ROWS, row_freq).astype(jnp.float32)
    col_wave = 8.0 * known(info, CHIP) + (lane % 8).astype(jnp.float32)
    wave = jnp.where(known(info, CORE) == 0.0, row_wave, col_wave)
    return row_freq, row_wave, col_wave, wave


def rows_forward_kernel(info, data, first, second, twist_cos, twist_sin, out):
    real = data[pl.ds(0, CHIPS, stride=2), :]
    imag = data[pl.ds(1, CHIPS, stride=2), :]
    spread = dot((first[0], first[1]), halves(jnp.concatenate([real, imag], axis=1)))
    re = spread[:CHIPS, :128] + spread[CHIPS:, 128:]
    im = spread[:CHIPS, 128:] - spread[CHIPS:, :128]
    cosine, sine = twist_cos[...], twist_sin[...]
    turned = jnp.concatenate([re * cosine + im * sine, im * cosine - re * sine], axis=1)
    final = dot(halves(turned), (second[0], second[1]))
    wave = wave_numbers(info)[3]
    out[:CHIPS] = wave * final[:, :128]
    out[CHIPS:] = wave * final[:, 128:]


def rows_backward_kernel(info, mine, other, first, second, twist_cos, twist_sin, out):
    row_freq, row_wave, col_wave, wave = wave_numbers(info)
    valid = (
        (row_freq != ROWS // 2)
        & (col_wave != COLS // 2)
        & ((row_freq != 0) | (col_wave != 0.0))
    )
    denom = reference_conduct * jnp.maximum(row_wave * row_wave + col_wave * col_wave, 1.0)
    weight = jnp.where(col_wave == 0.0, 1.0, 2.0) / (ROWS * COLS)
    coef = jnp.where(valid, weight * wave / denom, 0.0)
    along = mine[...] + other[...]
    green = jnp.concatenate([coef * along[:CHIPS], coef * along[CHIPS:]], axis=1)
    spread = dot(halves(green), (second[0], second[1]))
    re, im = spread[:, :128], spread[:, 128:]
    cosine, sine = twist_cos[...], twist_sin[...]
    turned = jnp.concatenate([re * cosine - im * sine, im * cosine + re * sine], axis=1)
    final = dot((first[0], first[1]), halves(turned))
    out[pl.ds(0, CHIPS, stride=2), :] = final[:CHIPS, :128] - final[CHIPS:, 128:]
    out[pl.ds(1, CHIPS, stride=2), :] = final[:CHIPS, 128:] + final[CHIPS:, :128]


def exchange(array, axes, tile):
    blocks = array.reshape((array.size // tile // 128, tile, 128))
    return lax.all_to_all(blocks, axes, split_axis=0, concat_axis=0, tiled=True)


def shift(block, axes, count, step):
    return lax.ppermute(block, axes, [(i, (i + step) % count) for i in range(count)])


def bottom_strip(voxel, wetted, heat):
    bottom = [array[:, TILE_ROWS - EDGE :] for array in (voxel, wetted, heat)]
    parts = bottom[0].astype(jnp.float32), bottom[1].astype(jnp.float32), -bottom[2]
    which = lax.broadcasted_iota(jnp.int32, (3, EDGE, TILE_COLS), 0)
    return jnp.where(which == 0, parts[0], jnp.where(which == 1, parts[1], parts[2]))


def body(voxel, wetted, heat, slope):
    gx_index, gt_index, core = (lax.axis_index(name) for name in ("gx", "gt", "core"))
    gx_size, gt_size, core_size = (lax.axis_size(name) for name in ("gx", "gt", "core"))
    gy_size = gt_size * core_size
    gy = ("gt", "core")
    chips = ("gx", "gt")
    place = jnp.stack([gx_index, gt_index * core_size + core, gx_index * gt_size + gt_index, core])
    (col_to, col_back), (row_to, row_back) = column_tables(), row_tables()
    tile = (TILE_ROWS, TILE_COLS)
    above = shift(bottom_strip(voxel, wetted, heat), "gx", gx_size, 1)
    porous = voxel[0].astype(jnp.float32)
    phase = porous * wetted[0].astype(jnp.float32)
    heat = heat[0]
    info, top = call(
        prepare_kernel, [(8, 128), (3, EDGE, TILE_COLS)],
        place.astype(jnp.int32), slope, porous, phase, heat, smem=(0, 1),
    )
    (polar,) = call(polar_kernel, [(OUTER * BLOCK, 128)], info, porous, phase, heat, above)
    below = shift(top, "gx", gx_size, -1)
    slab = exchange(polar, gy, 4).reshape(-1, 128)
    slab, below = lax.optimization_barrier((slab, below))
    first, last = call(edge_kernel, [(3, EDGE, WIDE)] * 2, porous, phase, heat, above, below)
    left = shift(last, gy, gy_size, 1)
    (spec,) = call(columns_forward_kernel, [(2 * CHIPS, 128)], info, slab, *col_to)
    spec = exchange(spec, chips, 2).reshape(-1, 128)
    spec, left = lax.optimization_barrier((spec, left))
    (mine,) = call(rows_forward_kernel, [(2 * CHIPS, 128)], info, spec, *row_to)
    other = lax.ppermute(mine, "core", [(0, 1), (1, 0)])
    (green,) = call(rows_backward_kernel, [(2 * CHIPS, 128)], info, mine, other, *row_back)
    green = exchange(green, chips, 2).reshape(-1, 128)
    green, first = lax.optimization_barrier((green, first))
    right = shift(first, gy, gy_size, -1)
    phase_two, heat_two = call(
        fields_kernel, [tile, tile], info, porous, phase, heat, above, below, left, right
    )
    (answer,) = call(columns_backward_kernel, [(OUTER * SLAB, 128)], info, green, *col_back)
    gradient = exchange(answer, ("core", "gt"), 8).reshape(2, 1, TILE_ROWS, TILE_COLS)
    return (phase_two[None], heat_two[None], gradient)


def solution(mesh):
    gx_size, gy_size = mesh.devices.shape
    fine = Mesh(mesh.devices.reshape(gx_size, gy_size // 2, 2), ("gx", "gt", "core"))
    gy = ("gt", "core")
    in_specs = (P(None, "gx", gy), P(None, "gx", gy), P(None, "gx", gy), P())
    out_specs = (P(None, "gx", gy), P(None, "gx", gy), P(None, None, "gx", gy))
    return jax.shard_map(body, mesh=fine, in_specs=in_specs, out_specs=out_specs, check_vma=False)
```

time: 126 us -> 121 us (0.960)
  blocking collectives: 47.1 us -> 24.2 us
  waiting for transfers between devices: 20.6 us -> 30.6 us
  starting transfers between devices: 42.2 us -> 51 us
  local copies, waits for them, and re-layouts: 4.21 us -> 1.58 us
  other arithmetic: 0.87 us -> 2.59 us
    all_to_all x2 -> x1, blocking collectives: 47.1 us -> 24.2 us  [exchange(): return lax.all_to_all(blocks, axes, split_axis=0, concat_axis=0, tiled=True)]
    all_to_all x2 -> x3, starting transfers between devices: 15.3 us -> 25.6 us  [exchange(): return lax.all_to_all(blocks, axes, split_axis=0, concat_axis=0, tiled=True)]
    all_to_all x2 -> x3, waiting for transfers between devices: 7.77 us -> 15.9 us  [exchange(): return lax.all_to_all(blocks, axes, split_axis=0, concat_axis=0, tiled=True)]
    ppermute x4, starting transfers between devices: 23.4 us -> 20.6 us  [shift(): lax.ppermute(block, axes, [(i, (i + step) % count) for i in range(count)])]
    unnamed x39 -> x33, local copies, waits for them, and re-layouts: 3.52 us -> 1.58 us
    ppermute x4, waiting for transfers between devices: 11.7 us -> 13.5 us  [shift(): lax.ppermute(block, axes, [(i, (i + step) % count) for i in range(count)])]
    ppermute x1, starting transfers between devices: 3.52 us -> 4.79 us  [body(): other = lax.ppermute(mine, 'core', [(0, 1), (1, 0)])]
    pallas_call x9 -> x8, Pallas kernels: 9.35 us -> 9.01 us  [call(): pl.pallas_call(kernel, out_shape=shapes, in_specs=spaces, out_specs=[VMEM...]
  transfers between devices with their start and end apart: 7 -> 8, of which waited for: 7 -> 8; matrix products, arithmetic and copies ran while one was open for 0% -> 1% of each run, Pallas kernels for 1% -> 2%
where the time goes in v3:
time: 121 us; the launch traced here: 120 us
  starting transfers between devices  51 us (42%)
  waiting for transfers between devices  30.6 us (25%)
  blocking collectives  24.2 us (20%)
  Pallas kernels  9.01 us (7%)
  other arithmetic  2.59 us (2%)
  local copies, waits for them, and re-layouts  1.58 us (1%)
    all_to_all x3, starting transfers between devices, exchange(): return lax.all_to_all(blocks, axes, split_axis=0, concat_axis=0, tiled=True)  25.6 us
    all_to_all x1, blocking collectives, exchange(): return lax.all_to_all(blocks, axes, split_axis=0, concat_axis=0, tiled=True)  24.2 us
    ppermute x4, starting transfers between devices, shift(): lax.ppermute(block, axes, [(i, (i + step) % count) for i in range(count)])  20.6 us
    all_to_all x3, waiting for transfers between devices, exchange(): return lax.all_to_all(blocks, axes, split_axis=0, concat_axis=0, tiled=True)  15.9 us
    ppermute x4, waiting for transfers between devices, shift(): lax.ppermute(block, axes, [(i, (i + step) % count) for i in range(count)])  13.5 us
    pallas_call x8, Pallas kernels, call(): pl.pallas_call(kernel, out_shape=shapes, in_specs=spaces, out_specs=[VMEM...  9.01 us
    ppermute x1, starting transfers between devices, body(): other = lax.ppermute(mine, 'core', [(0, 1), (1, 0)])  4.79 us
  transfers between devices with their start and end apart: 8, of which 8 were waited for; matrix products, arithmetic and copies ran while one was open for 1% of the time, Pallas kernels for 2%

profile of v3, /device:TPU:1, one launch (start us, length us, event | category | flops | bytes accessed | tf_op | source)
XLA Modules:
  0.0 119.9 jit_solution(17632513339259893094)
XLA Ops:
  0.6 0.7 negate_bitcast_fusion
  1.3 0.7 convert_bitcast_fusion.1
  2.0 0.1 select_select_fusion
  2.1 8.3 %collective-permute-start = (f32[3,8,128]{2,1,0:T(8,128)S(1)}, f32[3,8,128]{2,1,0:T(8,128)S(1)}, u32[]{:S(2)}, u32[]{:S(2)}) collective-permute-start(f32[3,8,128]{2,1,0:T(8,128)S(1)} %select_select_fusion), channel_id=1, source_target_pairs={{0,32},{32,64},{64,96},{96,128},{128,160},{160,192},{192,224},{224... | collective-permute-start | bytes 36872 | tf_op jit(solution)/shard_map/ppermute | solution.py:398
  10.4 0.0 copy-start.15
  10.4 1.0 bitcast_multiply_fusion.phase
  11.4 0.0 copy-done.15
  11.4 0.0 copy-start
  11.5 0.1 pad_add_fusion.place
  11.6 0.0 copy-start.14
  11.6 0.8 copy-done
  12.4 0.0 copy-done.14
  12.4 0.6 shard_map.184
  12.9 7.0 %collective-permute-done.above = f32[3,8,128]{2,1,0:T(8,128)S(1)} collective-permute-done((f32[3,8,128]{2,1,0:T(8,128)S(1)}, f32[3,8,128]{2,1,0:T(8,128)S(1)}, u32[]{:S(2)}, u32[]{:S(2)}) %collective-permute-start) | collective-permute-done | bytes 12320 | tf_op jit(solution)/shard_map/ppermute | solution.py:398
  19.9 1.6 %shard_map.185 = f32[640,128]{1,0:T(8,128)} custom-call(f32[8,128]{1,0:T(8,128)S(1)} %get-tuple-element.15.info, f32[256,128]{1,0:T(8,128)S(1)} %convert_bitcast_fusion.porous, f32[256,128]{1,0:T(8,128)S(1)} %bitcast_multiply_fusion.phase, f32[256,128]{1,0:T(8,128)S(1)} %bitcast.28, f32[3,8,128]{2,1,0:T(8,128)S(1)} %collective-permute-done.above), custom_call_target="tpu_custom_call" | custom-call | tf_op jit(solution)/shard_map/pallas_call | solution.py:61
  21.6 0.0 copy-start.2
  21.6 0.0 copy-start.9
  21.6 0.0 copy-start.10
  21.6 0.0 copy-start.11
  21.6 0.0 copy-start.12
  21.6 6.5 %all-to-all-start = ((f32[160,4,128]{2,1,0:T(4,128)}), f32[160,4,128]{2,1,0:T(4,128)S(1)}, u32[]{:S(2)}, u32[]{:S(2)}) async-start(f32[160,4,128]{2,1,0:T(4,128)} %bitcast.10), calls=%async_computation | async-start | bytes 655360 | tf_op jit(solution)/shard_map/all_to_all | solution.py:394
  28.1 7.5 %collective-permute-start.1 = (f32[3,8,128]{2,1,0:T(8,128)S(1)}, f32[3,8,128]{2,1,0:T(8,128)S(1)}, u32[]{:S(2)}, u32[]{:S(2)}) collective-permute-start(f32[3,8,128]{2,1,0:T(8,128)S(1)} %get-tuple-element.16), channel_id=1, source_target_pairs={{0,480},{32,0},{64,32},{96,64},{128,96},{160,128},{192,160},{224,1... | collective-permute-start | bytes 36872 | tf_op jit(solution)/shard_map/ppermute | solution.py:398
  35.6 0.8 collective-permute-done.1.below
  36.4 4.6 %all-to-all-done = f32[160,4,128]{2,1,0:T(4,128)S(1)} async-done(((f32[160,4,128]{2,1,0:T(4,128)}), f32[160,4,128]{2,1,0:T(4,128)S(1)}, u32[]{:S(2)}, u32[]{:S(2)}) %all-to-all-start) | async-done | bytes 327712 | tf_op jit(solution)/shard_map/all_to_all | solution.py:394
  41.0 0.0 copy-done.2
  41.0 0.0 copy-done.9
  41.0 0.0 copy-done.10
  41.0 0.0 copy-done.11
  41.0 0.0 copy-done.12
  41.0 0.0 copy-start.8
  41.0 2.1 %shard_map.186 = f32[512,128]{1,0:T(8,128)} custom-call(f32[8,128]{1,0:T(8,128)S(1)} %get-tuple-element.15.info, f32[640,128]{1,0:T(8,128)S(1)} %bitcast.31, bf16[2,128,128]{2,1,0:T(8,128)(2,1)S(1)} %copy-done.9, bf16[2,64,32]{2,1,0:T(8,128)(2,1)S(1)} %copy-done.12, bf16[2,128,256]{2,1,0:T(8,128)(2,1)S(1)} %copy-done.2, f32[32,128]{1,0:T(8,128)S(1)} %copy-done.11, ...), custom_call_target="tpu_custom_call" | custom-call | tf_op jit(solution)/shard_map/pallas_call | solution.py:61
  43.1 0.0 copy-start.1
  43.1 12.9 %all-to-all-start.1 = ((f32[256,2,128]{2,1,0:T(2,128)}), f32[256,2,128]{2,1,0:T(2,128)S(1)}, u32[]{:S(2)}, u32[]{:S(2)}) async-start(f32[256,2,128]{2,1,0:T(2,128)} %bitcast.12), calls=%async_computation.1 | async-start | bytes 524288 | tf_op jit(solution)/shard_map/all_to_all | solution.py:394
  56.0 0.0 copy-start.4
  56.1 0.0 copy-start.7
  56.1 0.2 shard_map.187
  56.3 2.6 %collective-permute-start.2 = (f32[3,8,384]{2,1,0:T(8,128)S(1)}, f32[3,8,384]{2,1,0:T(8,128)S(1)}, u32[]{:S(2)}, u32[]{:S(2)}) collective-permute-start(f32[3,8,384]{2,1,0:T(8,128)S(1)} %get-tuple-element.19), channel_id=1, source_target_pairs={{0,1},{1,2},{2,3},{3,4},{4,5},{5,6},{6,7},{7,8},{8,9},{9,10},{10,1... | collective-permute-start | bytes 110600 | tf_op jit(solution)/shard_map/ppermute | solution.py:398
  58.9 2.0 %collective-permute-done.2.left = f32[3,8,384]{2,1,0:T(8,128)S(1)} collective-permute-done((f32[3,8,384]{2,1,0:T(8,128)S(1)}, f32[3,8,384]{2,1,0:T(8,128)S(1)}, u32[]{:S(2)}, u32[]{:S(2)}) %collective-permute-start.2) | collective-permute-done | bytes 36896 | tf_op jit(solution)/shard_map/ppermute | solution.py:398
  60.8 8.5 %all-to-all-done.1 = f32[256,2,128]{2,1,0:T(2,128)S(1)} async-done(((f32[256,2,128]{2,1,0:T(2,128)}), f32[256,2,128]{2,1,0:T(2,128)S(1)}, u32[]{:S(2)}, u32[]{:S(2)}) %all-to-all-start.1) | async-done | bytes 262176 | tf_op jit(solution)/shard_map/all_to_all | solution.py:394
  69.4 0.0 copy-done.8
  69.4 0.0 copy-done.1
  69.4 0.0 copy-done.4
  69.4 0.0 copy-done.7
  69.4 0.0 copy-start.3
  69.4 0.0 copy-start.5
  69.4 0.0 copy-start.6
  69.4 0.7 shard_map.188.mine
  70.2 4.8 %collective-permute-start.3 = (f32[512,128]{1,0:T(8,128)S(1)}, f32[512,128]{1,0:T(8,128)S(1)}, u32[]{:S(2)}, u32[]{:S(2)}) collective-permute-start(f32[512,128]{1,0:T(8,128)S(1)} %shard_map.188.mine), channel_id=1, source_target_pairs={{0,1},{1,0},{2,3},{3,2},{4,5},{5,4},{6,7},{7,6},{8,9},{9,8},{10,11... | collective-permute-start | bytes 786440 | tf_op jit(solution)/shard_map/ppermute | solution.py:435
  75.0 1.1 collective-permute-done.3.other
  76.1 0.0 copy-done.3
  76.1 0.0 copy-done.5
  76.1 0.0 copy-done.6
  76.1 0.8 shard_map.189
  76.9 0.0 copy-start.13
  77.0 24.2 %all_to_all.20 = f32[256,2,128]{2,1,0:T(2,128)S(1)} all-to-all(f32[256,2,128]{2,1,0:T(2,128)S(1)} %bitcast.32), channel_id=1, replica_groups=mesh['gx'=16,'gt'=16,'core'=2] {'gx','gt'}, dimensions={0} | all-to-all | bytes 524288 | tf_op jit(solution)/shard_map/all_to_all | solution.py:394
  101.2 0.0 copy-done.13
  101.2 1.4 %shard_map.191 = f32[512,128]{1,0:T(8,128)} custom-call(f32[8,128]{1,0:T(8,128)S(1)} %get-tuple-element.15.info, f32[512,128]{1,0:T(8,128)S(1)} %bitcast.34, bf16[2,32,64]{2,1,0:T(8,128)(2,1)S(1)} %copy-done.13, bf16[2,128,256]{2,1,0:T(8,128)(2,1)S(1)} %copy-done.2, f32[32,128]{1,0:T(8,128)S(1)} %copy-done.11, f32[32,128]{1,0:T(8,128)S(1)} %copy-done.10), custom_call_target="tpu_custom_call" | custom-call | tf_op jit(solution)/shard_map/pallas_call | solution.py:61
  102.6 6.2 %all-to-all-start.3 = ((f32[64,8,128]{2,1,0:T(8,128)}), f32[64,8,128]{2,1,0:T(8,128)S(1)}, u32[]{:S(2)}, u32[]{:S(2)}) async-start(f32[64,8,128]{2,1,0:T(8,128)} %bitcast.18), calls=%async_computation.3 | async-start | bytes 524288 | tf_op jit(solution)/shard_map/all_to_all | solution.py:394
  108.8 2.2 %collective-permute-start.4 = (f32[3,8,384]{2,1,0:T(8,128)S(1)}, f32[3,8,384]{2,1,0:T(8,128)S(1)}, u32[]{:S(2)}, u32[]{:S(2)}) collective-permute-start(f32[3,8,384]{2,1,0:T(8,128)S(1)} %get-tuple-element.23), channel_id=1, source_target_pairs={{0,31},{1,0},{2,1},{3,2},{4,3},{5,4},{6,5},{7,6},{8,7},{9,8},{10,9... | collective-permute-start | bytes 110600 | tf_op jit(solution)/shard_map/ppermute | solution.py:398
  111.0 3.7 %collective-permute-done.4.right = f32[3,8,384]{2,1,0:T(8,128)S(1)} collective-permute-done((f32[3,8,384]{2,1,0:T(8,128)S(1)}, f32[3,8,384]{2,1,0:T(8,128)S(1)}, u32[]{:S(2)}, u32[]{:S(2)}) %collective-permute-start.4) | collective-permute-done | bytes 36896 | tf_op jit(solution)/shard_map/ppermute | solution.py:398
  114.7 1.6 %shard_map.190 = (f32[256,128]{1,0:T(8,128)}, f32[256,128]{1,0:T(8,128)}) custom-call(f32[8,128]{1,0:T(8,128)S(1)} %get-tuple-element.15.info, f32[256,128]{1,0:T(8,128)S(1)} %convert_bitcast_fusion.porous, f32[256,128]{1,0:T(8,128)S(1)} %bitcast_multiply_fusion.phase, f32[256,128]{1,0:T(8,128)S(1)} %bitcast.30, ...), custom_call_target="tpu_custom_call" | custom-call | tf_op jit(solution)/shard_map/pallas_call | solution.py:61
  116.3 2.8 %all-to-all-done.3 = f32[64,8,128]{2,1,0:T(8,128)S(1)} async-done(((f32[64,8,128]{2,1,0:T(8,128)}), f32[64,8,128]{2,1,0:T(8,128)S(1)}, u32[]{:S(2)}, u32[]{:S(2)}) %all-to-all-start.3) | async-done | bytes 262176 | tf_op jit(solution)/shard_map/all_to_all | solution.py:394
  119.2 0.7 copy.21
  (2 shorter events, 0.0 us)
Async XLA Ops:
  2.1 17.8 %collective-permute-start = (f32[3,8,128]{2,1,0:T(8,128)S(1)}, f32[3,8,128]{2,1,0:T(8,128)S(1)}, u32[]{:S(2)}, u32[]{:S(2)}) collective-permute-start(f32[3,8,128]{2,1,0:T(8,128)S(1)} %select_select_fusion), channel_id=1, source_target_pairs={{0,32},{32,64},{64,96},{96,128},{128,160},{160,192},{192,224},{224... | collective-permute-start | bytes 36872 | tf_op jit(solution)/shard_map/ppermute | solution.py:398
  10.4 1.0 copy-start.15
  11.4 0.9 copy-start
  11.6 0.8 copy-start.14
  21.6 19.4 %copy-start.2 = (bf16[2,128,256]{2,1,0:T(8,128)(2,1)S(1)}, bf16[2,128,256]{2,1,0:T(8,128)(2,1)}, u32[]{:S(2)}) copy-start(bf16[2,128,256]{2,1,0:T(8,128)(2,1)} %constant.46.clone.second) | copy-start | bytes 393220
  21.6 19.4 %copy-start.9 = (bf16[2,128,128]{2,1,0:T(8,128)(2,1)S(1)}, bf16[2,128,128]{2,1,0:T(8,128)(2,1)}, u32[]{:S(2)}) copy-start(bf16[2,128,128]{2,1,0:T(8,128)(2,1)} %constant.49.clone.order) | copy-start | bytes 196612
  21.6 19.4 %copy-start.10 = (f32[32,128]{1,0:T(8,128)S(1)}, f32[32,128]{1,0:T(8,128)}, u32[]{:S(2)}) copy-start(f32[32,128]{1,0:T(8,128)} %constant.48.clone.twist_sin) | copy-start | bytes 49156
  21.6 19.4 %copy-start.11 = (f32[32,128]{1,0:T(8,128)S(1)}, f32[32,128]{1,0:T(8,128)}, u32[]{:S(2)}) copy-start(f32[32,128]{1,0:T(8,128)} %constant.47.clone.twist_cos) | copy-start | bytes 49156
  21.6 19.5 %copy-start.12 = (bf16[2,64,32]{2,1,0:T(8,128)(2,1)S(1)}, bf16[2,64,32]{2,1,0:T(8,128)(2,1)}, u32[]{:S(2)}) copy-start(bf16[2,64,32]{2,1,0:T(8,128)(2,1)} %constant.50.clone.first) | copy-start | bytes 24580
  21.6 19.4 %all-to-all-start = ((f32[160,4,128]{2,1,0:T(4,128)}), f32[160,4,128]{2,1,0:T(4,128)S(1)}, u32[]{:S(2)}, u32[]{:S(2)}) async-start(f32[160,4,128]{2,1,0:T(4,128)} %bitcast.10), calls=%async_computation | async-start | bytes 655360 | tf_op jit(solution)/shard_map/all_to_all | solution.py:394
  28.1 8.4 %collective-permute-start.1 = (f32[3,8,128]{2,1,0:T(8,128)S(1)}, f32[3,8,128]{2,1,0:T(8,128)S(1)}, u32[]{:S(2)}, u32[]{:S(2)}) collective-permute-start(f32[3,8,128]{2,1,0:T(8,128)S(1)} %get-tuple-element.16), channel_id=1, source_target_pairs={{0,480},{32,0},{64,32},{96,64},{128,96},{160,128},{192,160},{224,1... | collective-permute-start | bytes 36872 | tf_op jit(solution)/shard_map/ppermute | solution.py:398
  41.0 28.4 %copy-start.8 = (f32[256,128]{1,0:T(8,128)S(1)}, f32[256,128]{1,0:T(8,128)}, u32[]{:S(2)}) copy-start(f32[256,128]{1,0:T(8,128)} %constant.54.clone.twist_cos) | copy-start | bytes 393220
  43.1 26.3 %copy-start.1 = (bf16[2,512,256]{2,1,0:T(8,128)(2,1)S(1)}, bf16[2,512,256]{2,1,0:T(8,128)(2,1)}, u32[]{:S(2)}) copy-start(bf16[2,512,256]{2,1,0:T(8,128)(2,1)} %constant.52.clone.first) | copy-start | bytes 1572868
  43.1 26.3 %all-to-all-start.1 = ((f32[256,2,128]{2,1,0:T(2,128)}), f32[256,2,128]{2,1,0:T(2,128)S(1)}, u32[]{:S(2)}, u32[]{:S(2)}) async-start(f32[256,2,128]{2,1,0:T(2,128)} %bitcast.12), calls=%async_computation.1 | async-start | bytes 524288 | tf_op jit(solution)/shard_map/all_to_all | solution.py:394
  56.0 13.3 %copy-start.4 = (bf16[2,256,256]{2,1,0:T(8,128)(2,1)S(1)}, bf16[2,256,256]{2,1,0:T(8,128)(2,1)}, u32[]{:S(2)}) copy-start(bf16[2,256,256]{2,1,0:T(8,128)(2,1)} %constant.53.clone.second) | copy-start | bytes 786436
  56.1 13.3 %copy-start.7 = (f32[256,128]{1,0:T(8,128)S(1)}, f32[256,128]{1,0:T(8,128)}, u32[]{:S(2)}) copy-start(f32[256,128]{1,0:T(8,128)} %constant.55.clone.twist_sin) | copy-start | bytes 393220
  56.3 4.6 %collective-permute-start.2 = (f32[3,8,384]{2,1,0:T(8,128)S(1)}, f32[3,8,384]{2,1,0:T(8,128)S(1)}, u32[]{:S(2)}, u32[]{:S(2)}) collective-permute-start(f32[3,8,384]{2,1,0:T(8,128)S(1)} %get-tuple-element.19), channel_id=1, source_target_pairs={{0,1},{1,2},{2,3},{3,4},{4,5},{5,6},{6,7},{7,8},{8,9},{9,10},{10,1... | collective-permute-start | bytes 110600 | tf_op jit(solution)/shard_map/ppermute | solution.py:398
  69.4 6.7 %copy-start.3 = (bf16[2,256,256]{2,1,0:T(8,128)(2,1)S(1)}, bf16[2,256,256]{2,1,0:T(8,128)(2,1)}, u32[]{:S(2)}) copy-start(bf16[2,256,256]{2,1,0:T(8,128)(2,1)} %constant.56.clone.second) | copy-start | bytes 786436
  69.4 6.7 %copy-start.5 = (f32[256,128]{1,0:T(8,128)S(1)}, f32[256,128]{1,0:T(8,128)}, u32[]{:S(2)}) copy-start(f32[256,128]{1,0:T(8,128)} %constant.58.clone.twist_sin) | copy-start | bytes 393220
  69.4 6.7 %copy-start.6 = (f32[256,128]{1,0:T(8,128)S(1)}, f32[256,128]{1,0:T(8,128)}, u32[]{:S(2)}) copy-start(f32[256,128]{1,0:T(8,128)} %constant.57.clone.twist_cos) | copy-start | bytes 393220
  70.2 5.9 %collective-permute-start.3 = (f32[512,128]{1,0:T(8,128)S(1)}, f32[512,128]{1,0:T(8,128)S(1)}, u32[]{:S(2)}, u32[]{:S(2)}) collective-permute-start(f32[512,128]{1,0:T(8,128)S(1)} %shard_map.188.mine), channel_id=1, source_target_pairs={{0,1},{1,0},{2,3},{3,2},{4,5},{5,4},{6,7},{7,6},{8,9},{9,8},{10,11... | collective-permute-start | bytes 786440 | tf_op jit(solution)/shard_map/ppermute | solution.py:435
  76.9 24.2 %copy-start.13 = (bf16[2,32,64]{2,1,0:T(8,128)(2,1)S(1)}, bf16[2,32,64]{2,1,0:T(8,128)(2,1)}, u32[]{:S(2)}) copy-start(bf16[2,32,64]{2,1,0:T(8,128)(2,1)} %constant.51.clone.first) | copy-start | bytes 24580
  102.6 16.6 %all-to-all-start.3 = ((f32[64,8,128]{2,1,0:T(8,128)}), f32[64,8,128]{2,1,0:T(8,128)S(1)}, u32[]{:S(2)}, u32[]{:S(2)}) async-start(f32[64,8,128]{2,1,0:T(8,128)} %bitcast.18), calls=%async_computation.3 | async-start | bytes 524288 | tf_op jit(solution)/shard_map/all_to_all | solution.py:394
  108.8 5.9 %collective-permute-start.4 = (f32[3,8,384]{2,1,0:T(8,128)S(1)}, f32[3,8,384]{2,1,0:T(8,128)S(1)}, u32[]{:S(2)}, u32[]{:S(2)}) collective-permute-start(f32[3,8,384]{2,1,0:T(8,128)S(1)} %get-tuple-element.23), channel_id=1, source_target_pairs={{0,31},{1,0},{2,1},{3,2},{4,3},{5,4},{6,5},{7,6},{8,7},{9,8},{10,9... | collective-permute-start | bytes 110600 | tf_op jit(solution)/shard_map/ppermute | solution.py:398

commit v4 on v3

--- a/solution.py
+++ b/solution.py
@@ -119,7 +119,7 @@
 GX, GY, CHIP, CORE, SLOPE_X, SLOPE_Y, SLOPE = range(7)
 
 
-def prepare_kernel(place, slope, porous, phase, heat, info, strip):
+def prepare_kernel(place, slope, info):
     values = [place[i].astype(jnp.float32) for i in range(4)] + [slope[0, 0], slope[0, 1]]
     values.append(jnp.where(place[3] == 0, slope[0, 0], slope[0, 1]))
     row = lax.broadcasted_iota(jnp.int32, info.shape, 0)
@@ -127,8 +127,6 @@
     for i, value in enumerate(values):
         filled = jnp.where(row == i, value, filled)
     info[...] = filled
-    for f, field in enumerate((porous, phase, heat)):
-        strip[f] = field[:EDGE, :]
 
 
 def known(info, i):
@@ -142,17 +140,23 @@
     ]
 
 
-def with_both(above, below, porous, phase, heat):
-    talls = with_above(above, porous, phase, heat)
-    return [jnp.concatenate([tall, below[f]], axis=0) for f, tall in enumerate(talls)]
-
-
-def edge_kernel(porous, phase, heat, above, below, first, last):
-    spare = jnp.zeros((WIDE - TALL - EDGE, TILE_COLS), jnp.float32)
-    for f, tall in enumerate(with_both(above, below, porous, phase, heat)):
+def edge_kernel(porous, phase, heat, above, first, last):
+    spare = jnp.zeros((WIDE - TALL, TILE_COLS), jnp.float32)
+    for f, tall in enumerate(with_above(above, porous, phase, heat)):
         flipped = jnp.concatenate([tall, spare], axis=0).T
         first[f] = flipped[:EDGE]
         last[f] = flipped[TILE_COLS - EDGE :]
+
+
+def sides(left, right, f, rows):
+    spare = jnp.zeros((TILE_COLS - 2 * EDGE, rows), jnp.float32)
+    return jnp.concatenate([right[f, :, :rows], spare, left[f, :, :rows]], axis=0).T
+
+
+def top_kernel(porous, phase, heat, left, right, out):
+    for f, field in enumerate((porous, phase, heat)):
+        out[f, :, :TILE_COLS] = field[:EDGE, :]
+        out[f, :, TILE_COLS:] = sides(left, right, f, 128)[EDGE : 2 * EDGE]
 
 
 def progress(phase, heat, porous, phase_lap, heat_lap):
@@ -242,11 +246,10 @@
 
 
 def fields_kernel(info, porous, phase, heat, above, below, left, right, phase_out, heat_out):
-    spare = jnp.zeros((TILE_COLS - 2 * EDGE, WIDE), jnp.float32)
     wides = []
-    for f, tall in enumerate(with_both(above, below, porous, phase, heat)):
-        side = jnp.concatenate([right[f], spare, left[f]], axis=0).T
-        wides.append(jnp.concatenate([tall, side[: TALL + EDGE]], axis=1))
+    for f, tall in enumerate(with_above(above, porous, phase, heat)):
+        wide = jnp.concatenate([tall, sides(left, right, f, WIDE)[:TALL]], axis=1)
+        wides.append(jnp.concatenate([wide, below[f]], axis=0))
     shape = wides[0].shape
     row = lax.broadcasted_iota(jnp.int32, shape, 0)
     column = lax.broadcasted_iota(jnp.int32, shape, 1)
@@ -418,25 +421,23 @@
     porous = voxel[0].astype(jnp.float32)
     phase = porous * wetted[0].astype(jnp.float32)
     heat = heat[0]
-    info, top = call(
-        prepare_kernel, [(8, 128), (3, EDGE, TILE_COLS)],
-        place.astype(jnp.int32), slope, porous, phase, heat, smem=(0, 1),
-    )
+    (info,) = call(prepare_kernel, [(8, 128)], place.astype(jnp.int32), slope, smem=(0, 1))
     (polar,) = call(polar_kernel, [(OUTER * BLOCK, 128)], info, porous, phase, heat, above)
-    below = shift(top, "gx", gx_size, -1)
     slab = exchange(polar, gy, 4).reshape(-1, 128)
-    slab, below = lax.optimization_barrier((slab, below))
-    first, last = call(edge_kernel, [(3, EDGE, WIDE)] * 2, porous, phase, heat, above, below)
+    first, last = call(edge_kernel, [(3, EDGE, WIDE)] * 2, porous, phase, heat, above)
     left = shift(last, gy, gy_size, 1)
+    right = shift(first, gy, gy_size, -1)
+    slab, left, right = lax.optimization_barrier((slab, left, right))
     (spec,) = call(columns_forward_kernel, [(2 * CHIPS, 128)], info, slab, *col_to)
     spec = exchange(spec, chips, 2).reshape(-1, 128)
-    spec, left = lax.optimization_barrier((spec, left))
     (mine,) = call(rows_forward_kernel, [(2 * CHIPS, 128)], info, spec, *row_to)
     other = lax.ppermute(mine, "core", [(0, 1), (1, 0)])
     (green,) = call(rows_backward_kernel, [(2 * CHIPS, 128)], info, mine, other, *row_back)
+    green, left, right = lax.optimization_barrier((green, left, right))
+    (top,) = call(top_kernel, [(3, EDGE, 2 * TILE_COLS)], porous, phase, heat, left, right)
+    below = shift(top, "gx", gx_size, -1)
     green = exchange(green, chips, 2).reshape(-1, 128)
-    green, first = lax.optimization_barrier((green, first))
-    right = shift(first, gy, gy_size, -1)
+    green, below = lax.optimization_barrier((green, below))
     phase_two, heat_two = call(
         fields_kernel, [tile, tile], info, porous, phase, heat, above, below, left, right
     )

time: 121 us -> 119 us (0.983)
  starting transfers between devices: 51 us -> 46.2 us
  blocking collectives: 24.2 us -> 28.5 us
    all_to_all x3, starting transfers between devices: 25.6 us -> 21.3 us  [exchange(): return lax.all_to_all(blocks, axes, split_axis=0, concat_axis=0, tiled=True)]
    all_to_all x1, blocking collectives: 24.2 us -> 28.5 us  [exchange(): return lax.all_to_all(blocks, axes, split_axis=0, concat_axis=0, tiled=True)]
    ppermute x1, starting transfers between devices: 4.79 us -> 1.92 us  [body(): other = lax.ppermute(mine, 'core', [(0, 1), (1, 0)])]
    ppermute x4, starting transfers between devices: 20.6 us -> 22.9 us  [shift(): lax.ppermute(block, axes, [(i, (i + step) % count) for i in range(count)])]
    ppermute x4, waiting for transfers between devices: 13.5 us -> 12.2 us  [shift(): lax.ppermute(block, axes, [(i, (i + step) % count) for i in range(count)])]
    pallas_call x8 -> x9, Pallas kernels: 9.01 us -> 9.08 us  [call(): pl.pallas_call(kernel, out_shape=shapes, in_specs=spaces, out_specs=[VMEM...]
where the time goes in v4:
time: 119 us; the launch traced here: 118 us
  starting transfers between devices  46.2 us (39%)
  waiting for transfers between devices  29.6 us (25%)
  blocking collectives  28.5 us (24%)
  Pallas kernels  9.08 us (8%)
  other arithmetic  2.59 us (2%)
  local copies, waits for them, and re-layouts  1.41 us (1%)
    all_to_all x1, blocking collectives, exchange(): return lax.all_to_all(blocks, axes, split_axis=0, concat_axis=0, tiled=True)  28.5 us
    ppermute x4, starting transfers between devices, shift(): lax.ppermute(block, axes, [(i, (i + step) % count) for i in range(count)])  22.9 us
    all_to_all x3, starting transfers between devices, exchange(): return lax.all_to_all(blocks, axes, split_axis=0, concat_axis=0, tiled=True)  21.3 us
    all_to_all x3, waiting for transfers between devices, exchange(): return lax.all_to_all(blocks, axes, split_axis=0, concat_axis=0, tiled=True)  15.9 us
    ppermute x4, waiting for transfers between devices, shift(): lax.ppermute(block, axes, [(i, (i + step) % count) for i in range(count)])  12.2 us
    pallas_call x9, Pallas kernels, call(): pl.pallas_call(kernel, out_shape=shapes, in_specs=spaces, out_specs=[VMEM...  9.08 us
  transfers between devices with their start and end apart: 8, of which 8 were waited for; matrix products, arithmetic and copies ran while one was open for 1% of the time, Pallas kernels for 2%

profile of v4, /device:TPU:1, one launch (start us, length us, event | category | flops | bytes accessed | tf_op | source)
XLA Modules:
  0.0 118.3 jit_solution(4875465120655981397)
XLA Ops:
  0.6 0.7 negate_bitcast_fusion
  1.3 0.7 convert_bitcast_fusion.1
  2.0 0.1 select_select_fusion
  2.1 8.3 %collective-permute-start = (f32[3,8,128]{2,1,0:T(8,128)S(1)}, f32[3,8,128]{2,1,0:T(8,128)S(1)}, u32[]{:S(2)}, u32[]{:S(2)}) collective-permute-start(f32[3,8,128]{2,1,0:T(8,128)S(1)} %select_select_fusion), channel_id=1, source_target_pairs={{0,32},{32,64},{64,96},{96,128},{128,160},{160,192},{192,224},{224... | collective-permute-start | bytes 36872 | tf_op jit(solution)/shard_map/ppermute | solution.py:401
  10.4 0.0 copy-start.15
  10.4 1.0 bitcast_multiply_fusion.phase
  11.4 0.0 copy-done.15
  11.4 0.0 copy-start
  11.5 0.0 copy-start.14
  11.5 0.1 pad_add_fusion.place
  11.6 0.6 copy-done.14
  12.2 0.6 shard_map.184.info
  12.7 7.2 %collective-permute-done.above = f32[3,8,128]{2,1,0:T(8,128)S(1)} collective-permute-done((f32[3,8,128]{2,1,0:T(8,128)S(1)}, f32[3,8,128]{2,1,0:T(8,128)S(1)}, u32[]{:S(2)}, u32[]{:S(2)}) %collective-permute-start) | collective-permute-done | bytes 12320 | tf_op jit(solution)/shard_map/ppermute | solution.py:401
  19.9 0.0 copy-done
  19.9 1.6 %shard_map.185 = f32[640,128]{1,0:T(8,128)} custom-call(f32[8,128]{1,0:T(8,128)S(1)} %shard_map.184.info, f32[256,128]{1,0:T(8,128)S(1)} %convert_bitcast_fusion.porous, f32[256,128]{1,0:T(8,128)S(1)} %bitcast_multiply_fusion.phase, f32[256,128]{1,0:T(8,128)S(1)} %bitcast.27, f32[3,8,128]{2,1,0:T(8,128)S(1)} %collective-permute-done.above), custom_call_target="tpu_custom_call" | custom-call | tf_op jit(solution)/shard_map/pallas_call | solution.py:61
  21.6 6.3 %all-to-all-start = ((f32[160,4,128]{2,1,0:T(4,128)}), f32[160,4,128]{2,1,0:T(4,128)S(1)}, u32[]{:S(2)}, u32[]{:S(2)}) async-start(f32[160,4,128]{2,1,0:T(4,128)} %bitcast.10), calls=%async_computation | async-start | bytes 655360 | tf_op jit(solution)/shard_map/all_to_all | solution.py:397
  27.9 0.0 copy-start.2
  27.9 0.0 copy-start.9
  27.9 0.0 copy-start.10
  27.9 0.0 copy-start.11
  28.0 0.0 copy-start.12
  28.0 0.2 shard_map.186
  28.2 3.5 %collective-permute-start.1 = (f32[3,8,384]{2,1,0:T(8,128)S(1)}, f32[3,8,384]{2,1,0:T(8,128)S(1)}, u32[]{:S(2)}, u32[]{:S(2)}) collective-permute-start(f32[3,8,384]{2,1,0:T(8,128)S(1)} %get-tuple-element.15), channel_id=1, source_target_pairs={{0,1},{1,2},{2,3},{3,4},{4,5},{5,6},{6,7},{7,8},{8,9},{9,10},{10,1... | collective-permute-start | bytes 110600 | tf_op jit(solution)/shard_map/ppermute | solution.py:401
  31.7 1.9 %collective-permute-start.2 = (f32[3,8,384]{2,1,0:T(8,128)S(1)}, f32[3,8,384]{2,1,0:T(8,128)S(1)}, u32[]{:S(2)}, u32[]{:S(2)}) collective-permute-start(f32[3,8,384]{2,1,0:T(8,128)S(1)} %get-tuple-element.16), channel_id=1, source_target_pairs={{0,31},{1,0},{2,1},{3,2},{4,3},{5,4},{6,5},{7,6},{8,7},{9,8},{10,9... | collective-permute-start | bytes 110600 | tf_op jit(solution)/shard_map/ppermute | solution.py:401
  33.7 0.6 collective-permute-done.1.left
  34.2 3.5 %collective-permute-done.2.right = f32[3,8,384]{2,1,0:T(8,128)S(1)} collective-permute-done((f32[3,8,384]{2,1,0:T(8,128)S(1)}, f32[3,8,384]{2,1,0:T(8,128)S(1)}, u32[]{:S(2)}, u32[]{:S(2)}) %collective-permute-start.2) | collective-permute-done | bytes 36896 | tf_op jit(solution)/shard_map/ppermute | solution.py:401
  37.7 3.2 %all-to-all-done = f32[160,4,128]{2,1,0:T(4,128)S(1)} async-done(((f32[160,4,128]{2,1,0:T(4,128)}), f32[160,4,128]{2,1,0:T(4,128)S(1)}, u32[]{:S(2)}, u32[]{:S(2)}) %all-to-all-start) | async-done | bytes 327712 | tf_op jit(solution)/shard_map/all_to_all | solution.py:397
  41.0 0.0 copy-done.2
  41.0 0.0 copy-done.9
  41.0 0.0 copy-done.10
  41.0 0.0 copy-done.11
  41.0 0.0 copy-done.12
  41.0 0.0 copy-start.1
  41.0 1.4 %shard_map.187 = f32[512,128]{1,0:T(8,128)S(1)} custom-call(f32[8,128]{1,0:T(8,128)S(1)} %shard_map.184.info, f32[640,128]{1,0:T(8,128)S(1)} %bitcast.31, bf16[2,128,128]{2,1,0:T(8,128)(2,1)S(1)} %copy-done.9, bf16[2,64,32]{2,1,0:T(8,128)(2,1)S(1)} %copy-done.12, bf16[2,128,256]{2,1,0:T(8,128)(2,1)S(1)} %copy-done.2, f32[32,128]{1,0:T(8,128)S(1)} %copy-done.11, ...), custom_call_target="tpu_custom_call" | custom-call | tf_op jit(solution)/shard_map/pallas_call | solution.py:61
  42.4 0.0 copy-start.4
  42.4 0.0 copy-start.7
  42.4 0.0 copy-start.8
  42.4 28.5 %all_to_all.20 = f32[256,2,128]{2,1,0:T(2,128)S(1)} all-to-all(f32[256,2,128]{2,1,0:T(2,128)S(1)} %bitcast.32), channel_id=1, replica_groups=mesh['gx'=16,'gt'=16,'core'=2] {'gx','gt'}, dimensions={0} | all-to-all | bytes 524288 | tf_op jit(solution)/shard_map/all_to_all | solution.py:397
  70.9 0.0 copy-done.1
  70.9 0.0 copy-done.4
  70.9 0.0 copy-done.7
  70.9 0.0 copy-done.8
  70.9 0.0 copy-start.3
  71.0 0.0 copy-start.5
  71.0 0.0 copy-start.6
  71.0 0.7 shard_map.188.mine
  71.7 1.9 %collective-permute-start.3 = (f32[512,128]{1,0:T(8,128)S(1)}, f32[512,128]{1,0:T(8,128)S(1)}, u32[]{:S(2)}, u32[]{:S(2)}) collective-permute-start(f32[512,128]{1,0:T(8,128)S(1)} %shard_map.188.mine), channel_id=1, source_target_pairs={{0,1},{1,0},{2,3},{3,2},{4,5},{5,4},{6,7},{7,6},{8,9},{9,8},{10,11... | collective-permute-start | bytes 786440 | tf_op jit(solution)/shard_map/ppermute | solution.py:434
  73.7 1.5 %collective-permute-done.3.other = f32[512,128]{1,0:T(8,128)S(1)} collective-permute-done((f32[512,128]{1,0:T(8,128)S(1)}, f32[512,128]{1,0:T(8,128)S(1)}, u32[]{:S(2)}, u32[]{:S(2)}) %collective-permute-start.3) | collective-permute-done | bytes 262176 | tf_op jit(solution)/shard_map/ppermute | solution.py:434
  75.2 0.0 copy-done.3
  75.2 0.0 copy-done.5
  75.2 0.0 copy-done.6
  75.2 1.5 %shard_map.189 = f32[512,128]{1,0:T(8,128)} custom-call(f32[8,128]{1,0:T(8,128)S(1)} %shard_map.184.info, f32[512,128]{1,0:T(8,128)S(1)} %shard_map.188.mine, f32[512,128]{1,0:T(8,128)S(1)} %collective-permute-done.3.other, bf16[2,512,256]{2,1,0:T(8,128)(2,1)S(1)} %copy-done.1, bf16[2,256,256]{2,1,0:T(8,128)(2,1)S(1)} %copy-done.3, ...), custom_call_target="tpu_custom_call" | custom-call | tf_op jit(solution)/shard_map/pallas_call | solution.py:61
  76.7 9.2 %all-to-all-start.2 = ((f32[256,2,128]{2,1,0:T(2,128)}), f32[256,2,128]{2,1,0:T(2,128)S(1)}, u32[]{:S(2)}, u32[]{:S(2)}) async-start(f32[256,2,128]{2,1,0:T(2,128)} %bitcast.14), calls=%async_computation.2 | async-start | bytes 524288 | tf_op jit(solution)/shard_map/all_to_all | solution.py:397
  85.9 0.0 copy-start.13
  85.9 9.2 %collective-permute-start.4 = (f32[3,8,256]{2,1,0:T(8,128)S(1)}, f32[3,8,256]{2,1,0:T(8,128)S(1)}, u32[]{:S(2)}, u32[]{:S(2)}) collective-permute-start(f32[3,8,256]{2,1,0:T(8,128)S(1)} %shard_map.190), channel_id=1, source_target_pairs={{0,480},{32,0},{64,32},{96,64},{128,96},{160,128},{192,160},{224,1... | collective-permute-start | bytes 73736 | tf_op jit(solution)/shard_map/ppermute | solution.py:401
  95.1 0.9 collective-permute-done.4.below
  96.1 4.0 %all-to-all-done.2 = f32[256,2,128]{2,1,0:T(2,128)S(1)} async-done(((f32[256,2,128]{2,1,0:T(2,128)}), f32[256,2,128]{2,1,0:T(2,128)S(1)}, u32[]{:S(2)}, u32[]{:S(2)}) %all-to-all-start.2) | async-done | bytes 262176 | tf_op jit(solution)/shard_map/all_to_all | solution.py:397
  100.1 0.0 copy-done.13
  100.1 1.4 %shard_map.192 = f32[512,128]{1,0:T(8,128)} custom-call(f32[8,128]{1,0:T(8,128)S(1)} %shard_map.184.info, f32[512,128]{1,0:T(8,128)S(1)} %bitcast.33, bf16[2,32,64]{2,1,0:T(8,128)(2,1)S(1)} %copy-done.13, bf16[2,128,256]{2,1,0:T(8,128)(2,1)S(1)} %copy-done.2, f32[32,128]{1,0:T(8,128)S(1)} %copy-done.11, f32[32,128]{1,0:T(8,128)S(1)} %copy-done.10), custom_call_target="tpu_custom_call" | custom-call | tf_op jit(solution)/shard_map/pallas_call | solution.py:61
  101.5 5.8 %all-to-all-start.3 = ((f32[64,8,128]{2,1,0:T(8,128)}), f32[64,8,128]{2,1,0:T(8,128)S(1)}, u32[]{:S(2)}, u32[]{:S(2)}) async-start(f32[64,8,128]{2,1,0:T(8,128)} %bitcast.18), calls=%async_computation.3 | async-start | bytes 524288 | tf_op jit(solution)/shard_map/all_to_all | solution.py:397
  107.3 1.6 %shard_map.191 = (f32[256,128]{1,0:T(8,128)}, f32[256,128]{1,0:T(8,128)}) custom-call(f32[8,128]{1,0:T(8,128)S(1)} %shard_map.184.info, f32[256,128]{1,0:T(8,128)S(1)} %convert_bitcast_fusion.porous, f32[256,128]{1,0:T(8,128)S(1)} %bitcast_multiply_fusion.phase, f32[256,128]{1,0:T(8,128)S(1)} %bitcast.30, f32[3,8,128]{2,1,0:T(8,128)S(1)} %collective-permute-done.above, ...), custom_call_target="tpu_custom_call" | custom-call | tf_op jit(solution)/shard_map/pallas_call | solution.py:61
  108.9 8.6 %all-to-all-done.3 = f32[64,8,128]{2,1,0:T(8,128)S(1)} async-done(((f32[64,8,128]{2,1,0:T(8,128)}), f32[64,8,128]{2,1,0:T(8,128)S(1)}, u32[]{:S(2)}, u32[]{:S(2)}) %all-to-all-start.3) | async-done | bytes 262176 | tf_op jit(solution)/shard_map/all_to_all | solution.py:397
  117.6 0.7 copy.21
  (3 shorter events, 0.1 us)
Async XLA Ops:
  2.1 17.8 %collective-permute-start = (f32[3,8,128]{2,1,0:T(8,128)S(1)}, f32[3,8,128]{2,1,0:T(8,128)S(1)}, u32[]{:S(2)}, u32[]{:S(2)}) collective-permute-start(f32[3,8,128]{2,1,0:T(8,128)S(1)} %select_select_fusion), channel_id=1, source_target_pairs={{0,32},{32,64},{64,96},{96,128},{128,160},{160,192},{192,224},{224... | collective-permute-start | bytes 36872 | tf_op jit(solution)/shard_map/ppermute | solution.py:401
  10.4 1.0 copy-start.15
  11.4 8.5 %copy-start = (f32[1,256,128]{2,1,0:T(8,128)S(1)}, f32[1,256,128]{2,1,0:T(8,128)}, u32[]{:S(2)}) copy-start(f32[1,256,128]{2,1,0:T(8,128)} %param.19) | copy-start | bytes 393220
  11.5 0.7 copy-start.14
  21.6 19.4 %all-to-all-start = ((f32[160,4,128]{2,1,0:T(4,128)}), f32[160,4,128]{2,1,0:T(4,128)S(1)}, u32[]{:S(2)}, u32[]{:S(2)}) async-start(f32[160,4,128]{2,1,0:T(4,128)} %bitcast.10), calls=%async_computation | async-start | bytes 655360 | tf_op jit(solution)/shard_map/all_to_all | solution.py:397
  27.9 13.1 %copy-start.2 = (bf16[2,128,256]{2,1,0:T(8,128)(2,1)S(1)}, bf16[2,128,256]{2,1,0:T(8,128)(2,1)}, u32[]{:S(2)}) copy-start(bf16[2,128,256]{2,1,0:T(8,128)(2,1)} %constant.46.clone.second) | copy-start | bytes 393220
  27.9 13.0 %copy-start.9 = (bf16[2,128,128]{2,1,0:T(8,128)(2,1)S(1)}, bf16[2,128,128]{2,1,0:T(8,128)(2,1)}, u32[]{:S(2)}) copy-start(bf16[2,128,128]{2,1,0:T(8,128)(2,1)} %constant.49.clone.order) | copy-start | bytes 196612
  27.9 13.0 %copy-start.10 = (f32[32,128]{1,0:T(8,128)S(1)}, f32[32,128]{1,0:T(8,128)}, u32[]{:S(2)}) copy-start(f32[32,128]{1,0:T(8,128)} %constant.48.clone.twist_sin) | copy-start | bytes 49156
  27.9 13.0 %copy-start.11 = (f32[32,128]{1,0:T(8,128)S(1)}, f32[32,128]{1,0:T(8,128)}, u32[]{:S(2)}) copy-start(f32[32,128]{1,0:T(8,128)} %constant.47.clone.twist_cos) | copy-start | bytes 49156
  28.0 13.0 %copy-start.12 = (bf16[2,64,32]{2,1,0:T(8,128)(2,1)S(1)}, bf16[2,64,32]{2,1,0:T(8,128)(2,1)}, u32[]{:S(2)}) copy-start(bf16[2,64,32]{2,1,0:T(8,128)(2,1)} %constant.50.clone.first) | copy-start | bytes 24580
  28.2 6.1 %collective-permute-start.1 = (f32[3,8,384]{2,1,0:T(8,128)S(1)}, f32[3,8,384]{2,1,0:T(8,128)S(1)}, u32[]{:S(2)}, u32[]{:S(2)}) collective-permute-start(f32[3,8,384]{2,1,0:T(8,128)S(1)} %get-tuple-element.15), channel_id=1, source_target_pairs={{0,1},{1,2},{2,3},{3,4},{4,5},{5,6},{6,7},{7,8},{8,9},{9,10},{10,1... | collective-permute-start | bytes 110600 | tf_op jit(solution)/shard_map/ppermute | solution.py:401
  31.7 6.0 %collective-permute-start.2 = (f32[3,8,384]{2,1,0:T(8,128)S(1)}, f32[3,8,384]{2,1,0:T(8,128)S(1)}, u32[]{:S(2)}, u32[]{:S(2)}) collective-permute-start(f32[3,8,384]{2,1,0:T(8,128)S(1)} %get-tuple-element.16), channel_id=1, source_target_pairs={{0,31},{1,0},{2,1},{3,2},{4,3},{5,4},{6,5},{7,6},{8,7},{9,8},{10,9... | collective-permute-start | bytes 110600 | tf_op jit(solution)/shard_map/ppermute | solution.py:401
  41.0 29.9 %copy-start.1 = (bf16[2,512,256]{2,1,0:T(8,128)(2,1)S(1)}, bf16[2,512,256]{2,1,0:T(8,128)(2,1)}, u32[]{:S(2)}) copy-start(bf16[2,512,256]{2,1,0:T(8,128)(2,1)} %constant.52.clone.first) | copy-start | bytes 1572868
  42.4 28.5 %copy-start.4 = (bf16[2,256,256]{2,1,0:T(8,128)(2,1)S(1)}, bf16[2,256,256]{2,1,0:T(8,128)(2,1)}, u32[]{:S(2)}) copy-start(bf16[2,256,256]{2,1,0:T(8,128)(2,1)} %constant.53.clone.second) | copy-start | bytes 786436
  42.4 28.5 %copy-start.7 = (f32[256,128]{1,0:T(8,128)S(1)}, f32[256,128]{1,0:T(8,128)}, u32[]{:S(2)}) copy-start(f32[256,128]{1,0:T(8,128)} %constant.55.clone.twist_sin) | copy-start | bytes 393220
  42.4 28.5 %copy-start.8 = (f32[256,128]{1,0:T(8,128)S(1)}, f32[256,128]{1,0:T(8,128)}, u32[]{:S(2)}) copy-start(f32[256,128]{1,0:T(8,128)} %constant.54.clone.twist_cos) | copy-start | bytes 393220
  70.9 4.2 %copy-start.3 = (bf16[2,256,256]{2,1,0:T(8,128)(2,1)S(1)}, bf16[2,256,256]{2,1,0:T(8,128)(2,1)}, u32[]{:S(2)}) copy-start(bf16[2,256,256]{2,1,0:T(8,128)(2,1)} %constant.56.clone.second) | copy-start | bytes 786436
  71.0 4.2 %copy-start.5 = (f32[256,128]{1,0:T(8,128)S(1)}, f32[256,128]{1,0:T(8,128)}, u32[]{:S(2)}) copy-start(f32[256,128]{1,0:T(8,128)} %constant.58.clone.twist_sin) | copy-start | bytes 393220
  71.0 4.2 %copy-start.6 = (f32[256,128]{1,0:T(8,128)S(1)}, f32[256,128]{1,0:T(8,128)}, u32[]{:S(2)}) copy-start(f32[256,128]{1,0:T(8,128)} %constant.57.clone.twist_cos) | copy-start | bytes 393220
  71.7 3.4 %collective-permute-start.3 = (f32[512,128]{1,0:T(8,128)S(1)}, f32[512,128]{1,0:T(8,128)S(1)}, u32[]{:S(2)}, u32[]{:S(2)}) collective-permute-start(f32[512,128]{1,0:T(8,128)S(1)} %shard_map.188.mine), channel_id=1, source_target_pairs={{0,1},{1,0},{2,3},{3,2},{4,5},{5,4},{6,7},{7,6},{8,9},{9,8},{10,11... | collective-permute-start | bytes 786440 | tf_op jit(solution)/shard_map/ppermute | solution.py:434
  76.7 23.4 %all-to-all-start.2 = ((f32[256,2,128]{2,1,0:T(2,128)}), f32[256,2,128]{2,1,0:T(2,128)S(1)}, u32[]{:S(2)}, u32[]{:S(2)}) async-start(f32[256,2,128]{2,1,0:T(2,128)} %bitcast.14), calls=%async_computation.2 | async-start | bytes 524288 | tf_op jit(solution)/shard_map/all_to_all | solution.py:397
  85.9 14.2 %copy-start.13 = (bf16[2,32,64]{2,1,0:T(8,128)(2,1)S(1)}, bf16[2,32,64]{2,1,0:T(8,128)(2,1)}, u32[]{:S(2)}) copy-start(bf16[2,32,64]{2,1,0:T(8,128)(2,1)} %constant.51.clone.first) | copy-start | bytes 24580
  85.9 10.1 %collective-permute-start.4 = (f32[3,8,256]{2,1,0:T(8,128)S(1)}, f32[3,8,256]{2,1,0:T(8,128)S(1)}, u32[]{:S(2)}, u32[]{:S(2)}) collective-permute-start(f32[3,8,256]{2,1,0:T(8,128)S(1)} %shard_map.190), channel_id=1, source_target_pairs={{0,480},{32,0},{64,32},{96,64},{128,96},{160,128},{192,160},{224,1... | collective-permute-start | bytes 73736 | tf_op jit(solution)/shard_map/ppermute | solution.py:401
  101.5 16.1 %all-to-all-start.3 = ((f32[64,8,128]{2,1,0:T(8,128)}), f32[64,8,128]{2,1,0:T(8,128)S(1)}, u32[]{:S(2)}, u32[]{:S(2)}) async-start(f32[64,8,128]{2,1,0:T(8,128)} %bitcast.18), calls=%async_computation.3 | async-start | bytes 524288 | tf_op jit(solution)/shard_map/all_to_all | solution.py:397

commit v5 on v4

--- a/solution.py
+++ b/solution.py
@@ -32,6 +32,7 @@
 SPAN = 20
 HALF = 64
 BLOCK = SLAB + 4
+BACK = SLAB + 2
 CHIPS = 256
 COLS = 4096
 ROWS = 4096
@@ -97,7 +98,9 @@
     stacked = np.concatenate([cosine, -sine], axis=0)
     forward = [split_table(order), split_table(stacked)] + rest
     backward = [split_table(np.concatenate([cosine, -sine], axis=1)[CORE_MAJOR])] + rest
-    return forward, backward
+    columns = np.zeros((128, 128))
+    columns[np.arange(4 * SLAB), (slot - SHIFT) % TILE_COLS] = 1.0
+    return forward, backward, jnp.asarray(columns.astype(jnp.bfloat16))
 
 
 def row_tables():
@@ -140,25 +143,6 @@
     ]
 
 
-def edge_kernel(porous, phase, heat, above, first, last):
-    spare = jnp.zeros((WIDE - TALL, TILE_COLS), jnp.float32)
-    for f, tall in enumerate(with_above(above, porous, phase, heat)):
-        flipped = jnp.concatenate([tall, spare], axis=0).T
-        first[f] = flipped[:EDGE]
-        last[f] = flipped[TILE_COLS - EDGE :]
-
-
-def sides(left, right, f, rows):
-    spare = jnp.zeros((TILE_COLS - 2 * EDGE, rows), jnp.float32)
-    return jnp.concatenate([right[f, :, :rows], spare, left[f, :, :rows]], axis=0).T
-
-
-def top_kernel(porous, phase, heat, left, right, out):
-    for f, field in enumerate((porous, phase, heat)):
-        out[f, :, :TILE_COLS] = field[:EDGE, :]
-        out[f, :, TILE_COLS:] = sides(left, right, f, 128)[EDGE : 2 * EDGE]
-
-
 def progress(phase, heat, porous, phase_lap, heat_lap):
     well = 2.0 * phase * (1.0 - phase) * (1.0 - 2.0 * phase)
     growth = 30.0 * phase * phase * (1.0 - phase) * (1.0 - phase)
@@ -213,11 +197,13 @@
     return first & (row == EDGE - 1), first & (row == EDGE)
 
 
-def polar_kernel(info, porous, phase, heat, above, out):
+def polar_kernel(info, porous, phase, heat, above, out, fields):
     talls = with_above(above, porous, phase, heat)
     row = lax.broadcasted_iota(jnp.int32, talls[0].shape, 0)
     walls = row_walls(known(info, GX) == 0.0, row) + (None, None)
-    phase_two, _, along_rows, along_columns = stencil(*talls, ring_neighbours(walls))
+    phase_two, heat_two, along_rows, along_columns = stencil(*talls, ring_neighbours(walls))
+    fields[0] = shifted_rows(phase_two)
+    fields[1] = shifted_rows(heat_two)
     contrast = conductivity_contrast(talls[0], phase_two)
     polars = (
         shifted_rows(contrast * (known(info, SLOPE_X) + gradient_gain * along_rows)),
@@ -226,6 +212,7 @@
     spare = jnp.zeros((WIDE - TALL, TILE_COLS), jnp.float32)
     sublane = lax.broadcasted_iota(jnp.int32, (EDGE, WIDE), 0)
     lane = lax.broadcasted_iota(jnp.int32, (EDGE, TILE_COLS), 1)
+    low = lax.broadcasted_iota(jnp.int32, (EDGE, TILE_COLS), 0) < 4
     edges = []
     for tall in talls:
         flipped = jnp.concatenate([tall, spare], axis=0).T
@@ -238,33 +225,31 @@
         packed = jnp.where(
             lane < SPAN, windows[0], jnp.where(lane < 2 * SPAN, windows[1], windows[2])
         )
-        packed = jnp.where(lane < HALF, packed, roll(roll(packed, HALF, 1), 4, 0))
-        for f in range(2):
-            start = (2 * x + f) * BLOCK
-            out[start : start + SLAB, :] = polars[f][x * SLAB : (x + 1) * SLAB]
-            out[start + SLAB : start + BLOCK, :] = packed[:4]
-
-
-def fields_kernel(info, porous, phase, heat, above, below, left, right, phase_out, heat_out):
-    wides = []
-    for f, tall in enumerate(with_above(above, porous, phase, heat)):
-        wide = jnp.concatenate([tall, sides(left, right, f, WIDE)[:TALL]], axis=1)
-        wides.append(jnp.concatenate([wide, below[f]], axis=0))
-    shape = wides[0].shape
-    row = lax.broadcasted_iota(jnp.int32, shape, 0)
-    column = lax.broadcasted_iota(jnp.int32, shape, 1)
-    gx, gy = (jnp.concatenate([known(info, i)] * 2, axis=1) for i in (GX, GY))
-    top, bottom = gx == 0.0, gx == ROWS // TILE_ROWS - 1
-    start, end = gy == 0.0, gy == COLS // TILE_COLS - 1
-    walls = (
-        (top & (row == EDGE - 1)) | (bottom & (row == TALL - 1)),
-        (top & (row == EDGE)) | (bottom & (row == TALL)),
-        (start & (column == shape[1] - 1)) | (end & (column == TILE_COLS - 1)),
-        (start & (column == 0)) | (end & (column == TILE_COLS)),
-    )
-    phase_two, heat_two, _, _ = stencil(*wides, ring_neighbours(walls))
-    phase_out[...] = phase_two[EDGE:TALL, :TILE_COLS]
-    heat_out[...] = heat_two[EDGE:TALL, :TILE_COLS]
+        swapped = roll(packed, 4, 0)
+        lower, upper = jnp.where(low, packed, swapped), jnp.where(low, swapped, packed)
+        both = jnp.where(lane < HALF, lower, roll(upper, HALF, 1))
+        rows = slice(x * SLAB, (x + 1) * SLAB)
+        start = 2 * x * BLOCK
+        out[start : start + SLAB, :] = polars[0][rows]
+        rest = roll(jnp.concatenate([both, polars[1][rows]], axis=0), -4, 0)
+        out[start + SLAB : start + 2 * BLOCK, :] = rest
+
+
+def tail_kernel(info, porous, phase, heat, fields, parcel, out):
+    ends = [
+        jnp.concatenate([field[TILE_ROWS - 2 * EDGE :, :], parcel[f * EDGE : (f + 1) * EDGE, :]])
+        for f, field in enumerate((porous, phase, heat))
+    ]
+    row = lax.broadcasted_iota(jnp.int32, ends[0].shape, 0)
+    last = known(info, GX) == ROWS // TILE_ROWS - 1
+    walls = (last & (row == 2 * EDGE - 1), last & (row == 2 * EDGE), None, None)
+    late = lax.broadcasted_iota(jnp.int32, (EDGE, TILE_COLS), 0) >= EDGE - SHIFT
+    for f, end in enumerate(stencil(*ends, ring_neighbours(walls))[:2]):
+        whole = roll(fields[f], -SHIFT, 0)
+        out[f, : TILE_ROWS - EDGE, :] = whole[: TILE_ROWS - EDGE]
+        out[f, TILE_ROWS - EDGE :, :] = jnp.where(
+            late, end[EDGE : 2 * EDGE], whole[TILE_ROWS - EDGE :]
+        )
 
 
 def edge_polar(info, data):
@@ -286,21 +271,33 @@
             jnp.concatenate([before, field[: 3 * OUTER]], axis=0),
         )
 
-    phase, _, along_rows, along_columns = stencil(*fields, neighbours)
-    along = jnp.where(known(info, CORE) == 0.0, along_rows, along_columns)
+    phase, heat, along_rows, along_columns = stencil(*fields, neighbours)
+    first = known(info, CORE) == 0.0
+    along = jnp.where(first, along_rows, along_columns)
+    value = jnp.where(first, phase, heat)
     polar = conductivity_contrast(raw, phase) * (known(info, SLOPE) + gradient_gain * along)
-    return [polar[c * OUTER : (c + 1) * OUTER] for c in range(4)]
-
-
-def columns_forward_kernel(info, data, order, first, second, twist_cos, twist_sin, out):
-    edges = edge_polar(info, data)
+    return [[array[c * OUTER : (c + 1) * OUTER] for c in range(4)] for array in (polar, value)]
+
+
+def pack(columns):
     lane = lax.broadcasted_iota(jnp.int32, (OUTER, TILE_COLS), 1)
     packed = jnp.zeros((OUTER, TILE_COLS), jnp.float32)
     for slot, column in enumerate((2, 3, 0, 1)):
         start = SHIFT + (HALF if column >= 2 else 0)
-        moved = roll(edges[column], SLAB * slot - start, 1)
+        moved = roll(columns[column], SLAB * slot - start, 1)
         packed = jnp.where(lane // SLAB == slot, moved, packed)
-    packed = dot(halves(packed), (order[0], order[1]))
+    return packed
+
+
+def columns_forward_kernel(
+    info, data, porous, phase, heat, order, first, second, twist_cos, twist_sin, out, parcel
+):
+    polar, value = edge_polar(info, data)
+    for f, field in enumerate((porous, phase, heat)):
+        parcel[f * EDGE : (f + 1) * EDGE, :] = field[:EDGE, :]
+    parcel[3 * EDGE :, :] = pack(value)
+    packed = dot(halves(pack(polar)), (order[0], order[1]))
+    lane = lax.broadcasted_iota(jnp.int32, (OUTER, TILE_COLS), 1)
     outer = (lane < SHIFT) | (lane >= TILE_COLS - SHIFT)
     parts = []
     for s in range(SLAB):
@@ -325,7 +322,7 @@
         out[pl.ds(2 * g + 1, 64, stride=8), :] = final[64:]
 
 
-def columns_backward_kernel(info, data, first, second, twist_cos, twist_sin, out):
+def columns_backward_kernel(info, data, mine, below, first, second, twist_cos, twist_sin, out):
     real, imag = [], []
     for g in range(4):
         span = slice(g * 8, (g + 1) * 8)
@@ -344,7 +341,43 @@
     final = dot((first[0], first[1]), halves(stacked))
     for s in range(SLAB):
         part = final[:, s * 128 : (s + 1) * 128]
-        out[pl.ds(s, OUTER, stride=SLAB), :] = known(info, SLOPE) - part
+        out[pl.ds(s, OUTER, stride=BACK), :] = known(info, SLOPE) - part
+    lane = lax.broadcasted_iota(jnp.int32, (SLAB, TILE_COLS), 1)
+    slab = known(info, CHIP) - SLAB * known(info, GX)
+    late = (slab == 0.0) & (lane % SLAB < SHIFT)
+    for core in range(2):
+        rows = pl.ds(3 * EDGE + core, SLAB, stride=2)
+        start = core * SLAB * BACK + SLAB
+        out[pl.ds(start, SLAB, stride=BACK), :] = jnp.where(late, below[rows, :], mine[rows, :])
+        out[pl.ds(start + 1, SLAB, stride=BACK), :] = jnp.zeros((SLAB, TILE_COLS), jnp.float32)
+
+
+def place_kernel(data, fields, columns, phase, heat, gradient):
+    lane = lax.broadcasted_iota(jnp.int32, (SLAB, TILE_COLS), 1)
+    row = lax.broadcasted_iota(jnp.int32, (SLAB, TILE_COLS), 0)
+    own = (lane % SLAB == row) & (lane < 4 * SLAB)
+    lane = lax.broadcasted_iota(jnp.int32, (TILE_ROWS, TILE_COLS), 1)
+    outer = (lane < SHIFT) | (lane >= TILE_COLS - SHIFT)
+    for f, out in enumerate((phase, heat)):
+        start = f * SLAB * BACK
+        values = data[pl.ds(start + SLAB, SLAB, stride=BACK), :]
+        spread = jnp.concatenate(
+            [jnp.where(own, values[x : x + 1], 0.0) for x in range(SLAB)], axis=0
+        )
+        high, rest = halves(spread)
+        low = (spread - high.astype(jnp.float32) - rest.astype(jnp.float32)).astype(jnp.bfloat16)
+        parts = [
+            lax.dot_general(
+                part, columns[...], (((1,), (0,)), ((), ())), preferred_element_type=jnp.float32
+            )
+            for part in (high, rest, low)
+        ]
+        edge = roll(parts[0] + (parts[1] + parts[2]), -SHIFT, 0)
+        out[...] = jnp.where(outer, edge, fields[f])
+        for s in range(SLAB):
+            gradient[pl.ds(f * TILE_ROWS + s, SLAB, stride=SLAB), :] = data[
+                pl.ds(start + s, SLAB, stride=BACK), :
+            ]
 
 
 def wave_numbers(info):
@@ -415,35 +448,38 @@
     gy = ("gt", "core")
     chips = ("gx", "gt")
     place = jnp.stack([gx_index, gt_index * core_size + core, gx_index * gt_size + gt_index, core])
-    (col_to, col_back), (row_to, row_back) = column_tables(), row_tables()
+    (col_to, col_back, columns), (row_to, row_back) = column_tables(), row_tables()
     tile = (TILE_ROWS, TILE_COLS)
     above = shift(bottom_strip(voxel, wetted, heat), "gx", gx_size, 1)
     porous = voxel[0].astype(jnp.float32)
     phase = porous * wetted[0].astype(jnp.float32)
     heat = heat[0]
     (info,) = call(prepare_kernel, [(8, 128)], place.astype(jnp.int32), slope, smem=(0, 1))
-    (polar,) = call(polar_kernel, [(OUTER * BLOCK, 128)], info, porous, phase, heat, above)
+    polar, fields = call(
+        polar_kernel, [(OUTER * BLOCK, 128), (2,) + tile], info, porous, phase, heat, above
+    )
     slab = exchange(polar, gy, 4).reshape(-1, 128)
-    first, last = call(edge_kernel, [(3, EDGE, WIDE)] * 2, porous, phase, heat, above)
-    left = shift(last, gy, gy_size, 1)
-    right = shift(first, gy, gy_size, -1)
-    slab, left, right = lax.optimization_barrier((slab, left, right))
-    (spec,) = call(columns_forward_kernel, [(2 * CHIPS, 128)], info, slab, *col_to)
+    spec, parcel = call(
+        columns_forward_kernel, [(2 * CHIPS, 128), (3 * EDGE + OUTER, 128)],
+        info, slab, porous, phase, heat, *col_to,
+    )
     spec = exchange(spec, chips, 2).reshape(-1, 128)
     (mine,) = call(rows_forward_kernel, [(2 * CHIPS, 128)], info, spec, *row_to)
     other = lax.ppermute(mine, "core", [(0, 1), (1, 0)])
     (green,) = call(rows_backward_kernel, [(2 * CHIPS, 128)], info, mine, other, *row_back)
-    green, left, right = lax.optimization_barrier((green, left, right))
-    (top,) = call(top_kernel, [(3, EDGE, 2 * TILE_COLS)], porous, phase, heat, left, right)
-    below = shift(top, "gx", gx_size, -1)
+    green, parcel = lax.optimization_barrier((green, parcel))
+    below = shift(parcel, "gx", gx_size, -1)
     green = exchange(green, chips, 2).reshape(-1, 128)
-    green, below = lax.optimization_barrier((green, below))
-    phase_two, heat_two = call(
-        fields_kernel, [tile, tile], info, porous, phase, heat, above, below, left, right
-    )
-    (answer,) = call(columns_backward_kernel, [(OUTER * SLAB, 128)], info, green, *col_back)
-    gradient = exchange(answer, ("core", "gt"), 8).reshape(2, 1, TILE_ROWS, TILE_COLS)
-    return (phase_two[None], heat_two[None], gradient)
+    (fields,) = call(tail_kernel, [(2,) + tile], info, porous, phase, heat, fields, below)
+    green, below, fields = lax.optimization_barrier((green, below, fields))
+    (answer,) = call(
+        columns_backward_kernel, [(OUTER * BACK, 128)], info, green, parcel, below, *col_back
+    )
+    answer = exchange(answer, ("core", "gt"), 2).reshape(-1, 128)
+    phase, heat, gradient = call(
+        place_kernel, [tile, tile, (2 * TILE_ROWS, TILE_COLS)], answer, fields, columns
+    )
+    return (phase[None], heat[None], gradient.reshape((2, 1) + tile))
 
 
 def solution(mesh):

time: 119 us -> 118 us (level)
  blocking collectives: 28.5 us -> 62.2 us
  waiting for transfers between devices: 29.6 us -> 13 us
  starting transfers between devices: 46.2 us -> 30.7 us
  Pallas kernels: 9.08 us -> 6.95 us
    all_to_all x1 -> x3, blocking collectives: 28.5 us -> 62.2 us  [exchange(): return lax.all_to_all(blocks, axes, split_axis=0, concat_axis=0, tiled=True)]
    all_to_all x3 -> x1, waiting for transfers between devices: 15.9 us -> 3.69 us  [exchange(): return lax.all_to_all(blocks, axes, split_axis=0, concat_axis=0, tiled=True)]
    all_to_all x3 -> x1, starting transfers between devices: 21.3 us -> 9.17 us  [exchange(): return lax.all_to_all(blocks, axes, split_axis=0, concat_axis=0, tiled=True)]
    ppermute x4 -> x2, starting transfers between devices: 22.9 us -> 17.4 us  [shift(): lax.ppermute(block, axes, [(i, (i + step) % count) for i in range(count)])]
    ppermute x4 -> x2, waiting for transfers between devices: 12.2 us -> 8.17 us  [shift(): lax.ppermute(block, axes, [(i, (i + step) % count) for i in range(count)])]
    ppermute x1, starting transfers between devices: 1.92 us -> 4.14 us  [body(): other = lax.ppermute(mine, 'core', [(0, 1), (1, 0)])]
    pallas_call x9 -> x8, Pallas kernels: 9.08 us -> 6.95 us  [call(): pl.pallas_call(kernel, out_shape=shapes, in_specs=spaces, out_specs=[VMEM...]
  transfers between devices with their start and end apart: 8 -> 4, of which waited for: 8 -> 4; matrix products, arithmetic and copies ran while one was open for 1% -> 1% of each run, Pallas kernels for 2% -> 1%
where the time goes in v5:
time: 118 us; the launch traced here: 117 us
  blocking collectives  62.2 us (53%)
  starting transfers between devices  30.7 us (26%)
  waiting for transfers between devices  13 us (11%)
  Pallas kernels  6.95 us (6%)
  other arithmetic  2.59 us (2%)
    all_to_all x3, blocking collectives, exchange(): return lax.all_to_all(blocks, axes, split_axis=0, concat_axis=0, tiled=True)  62.2 us
    ppermute x2, starting transfers between devices, shift(): lax.ppermute(block, axes, [(i, (i + step) % count) for i in range(count)])  17.4 us
    all_to_all x1, starting transfers between devices, exchange(): return lax.all_to_all(blocks, axes, split_axis=0, concat_axis=0, tiled=True)  9.17 us
    ppermute x2, waiting for transfers between devices, shift(): lax.ppermute(block, axes, [(i, (i + step) % count) for i in range(count)])  8.17 us
    pallas_call x8, Pallas kernels, call(): pl.pallas_call(kernel, out_shape=shapes, in_specs=spaces, out_specs=[VMEM...  6.95 us
    ppermute x1, starting transfers between devices, body(): other = lax.ppermute(mine, 'core', [(0, 1), (1, 0)])  4.14 us
    all_to_all x1, waiting for transfers between devices, exchange(): return lax.all_to_all(blocks, axes, split_axis=0, concat_axis=0, tiled=True)  3.69 us
  transfers between devices with their start and end apart: 4, of which 4 were waited for; matrix products, arithmetic and copies ran while one was open for 1% of the time, Pallas kernels for 1%

profile of v5, /device:TPU:1, one launch (start us, length us, event | category | flops | bytes accessed | tf_op | source)
XLA Modules:
  0.0 117.0 jit_solution(15026239179795349383)
XLA Ops:
  0.6 0.7 negate_bitcast_fusion
  1.3 0.7 convert_bitcast_fusion.1
  2.0 0.1 select_select_fusion
  2.1 8.3 %collective-permute-start = (f32[3,8,128]{2,1,0:T(8,128)S(1)}, f32[3,8,128]{2,1,0:T(8,128)S(1)}, u32[]{:S(2)}, u32[]{:S(2)}) collective-permute-start(f32[3,8,128]{2,1,0:T(8,128)S(1)} %select_select_fusion), channel_id=1, source_target_pairs={{0,32},{32,64},{64,96},{96,128},{128,160},{160,192},{192,224},{224... | collective-permute-start | bytes 36872 | tf_op jit(solution)/shard_map/ppermute | solution.py:434
  10.4 0.0 copy-start.16
  10.4 1.0 bitcast_multiply_fusion.phase
  11.4 0.0 copy-done.16
  11.4 0.0 copy-start.1
  11.5 0.0 copy-start.15
  11.5 0.1 pad_add_fusion.place
  11.6 0.6 copy-done.15
  12.2 0.6 shard_map.193.info
  12.7 7.2 %collective-permute-done.above = f32[3,8,128]{2,1,0:T(8,128)S(1)} collective-permute-done((f32[3,8,128]{2,1,0:T(8,128)S(1)}, f32[3,8,128]{2,1,0:T(8,128)S(1)}, u32[]{:S(2)}, u32[]{:S(2)}) %collective-permute-start) | collective-permute-done | bytes 12320 | tf_op jit(solution)/shard_map/ppermute | solution.py:434
  19.9 0.0 copy-done.1
  19.9 0.9 shard_map.194
  20.8 0.0 copy-start.2
  20.9 0.0 copy-start.9
  20.9 0.0 copy-start.10
  20.9 0.0 copy-start.11
  20.9 0.0 copy-start.13
  20.9 18.9 %all_to_all.20 = f32[160,4,128]{2,1,0:T(4,128)S(1)} all-to-all(f32[160,4,128]{2,1,0:T(4,128)S(1)} %bitcast.38), channel_id=1, replica_groups=mesh['gx'=16,'gt'=16,'core'=2] {'gt','core'}, dimensions={0} | all-to-all | bytes 655360 | tf_op jit(solution)/shard_map/all_to_all | solution.py:430
  39.8 0.0 copy-done.2
  39.8 0.0 copy-done.9
  39.8 0.0 copy-done.10
  39.9 0.0 copy-done.11
  39.9 0.0 copy-done.13
  39.9 0.0 copy-start
  39.9 1.4 %shard_map.195 = (f32[512,128]{1,0:T(8,128)S(1)}, f32[56,128]{1,0:T(8,128)S(1)}) custom-call(f32[8,128]{1,0:T(8,128)S(1)} %shard_map.193.info, f32[640,128]{1,0:T(8,128)S(1)} %bitcast.30, f32[256,128]{1,0:T(8,128)S(1)} %convert_bitcast_fusion.porous, f32[256,128]{1,0:T(8,128)S(1)} %bitcast_multiply_fusion.phase, f32[256,128]{1,0:T(8,128)S(1)} %bitcast.32, ...), custom_call_target="tpu_custom_call" | custom-call | tf_op jit(solution)/shard_map/pallas_call | solution.py:62
  41.3 0.0 copy-start.4
  41.3 0.0 copy-start.7
  41.3 0.0 copy-start.8
  41.3 26.5 %all_to_all.21 = f32[256,2,128]{2,1,0:T(2,128)S(1)} all-to-all(f32[256,2,128]{2,1,0:T(2,128)S(1)} %bitcast.39), channel_id=1, replica_groups=mesh['gx'=16,'gt'=16,'core'=2] {'gx','gt'}, dimensions={0} | all-to-all | bytes 524288 | tf_op jit(solution)/shard_map/all_to_all | solution.py:430
  67.8 0.0 copy-done
  67.8 0.0 copy-done.4
  67.8 0.0 copy-done.7
  67.8 0.0 copy-done.8
  67.8 0.0 copy-start.3
  67.8 0.0 copy-start.5
  67.8 0.0 copy-start.6
  67.8 0.7 shard_map.196.mine
  68.6 4.1 %collective-permute-start.1 = (f32[512,128]{1,0:T(8,128)S(1)}, f32[512,128]{1,0:T(8,128)S(1)}, u32[]{:S(2)}, u32[]{:S(2)}) collective-permute-start(f32[512,128]{1,0:T(8,128)S(1)} %shard_map.196.mine), channel_id=1, source_target_pairs={{0,1},{1,0},{2,3},{3,2},{4,5},{5,4},{6,7},{7,6},{8,9},{9,8},{10,11... | collective-permute-start | bytes 786440 | tf_op jit(solution)/shard_map/ppermute | solution.py:468
  72.7 1.1 collective-permute-done.1.other
  73.9 0.0 copy-done.3
  73.9 0.0 copy-done.5
  73.9 0.0 copy-done.6
  73.9 1.5 %shard_map.197 = f32[512,128]{1,0:T(8,128)} custom-call(f32[8,128]{1,0:T(8,128)S(1)} %shard_map.193.info, f32[512,128]{1,0:T(8,128)S(1)} %shard_map.196.mine, f32[512,128]{1,0:T(8,128)S(1)} %collective-permute-done.1.other, bf16[2,512,256]{2,1,0:T(8,128)(2,1)S(1)} %copy-done, bf16[2,256,256]{2,1,0:T(8,128)(2,1)S(1)} %copy-done.3, f32[256,128]{1,0:T(8,128)S(1)} %copy-done.6, ...), custom_call_target="tpu_custom_call" | custom-call | tf_op jit(solution)/shard_map/pallas_call | solution.py:62
  75.4 9.2 %all-to-all-start.2 = ((f32[256,2,128]{2,1,0:T(2,128)}), f32[256,2,128]{2,1,0:T(2,128)S(1)}, u32[]{:S(2)}, u32[]{:S(2)}) async-start(f32[256,2,128]{2,1,0:T(2,128)} %bitcast.14), calls=%async_computation.2 | async-start | bytes 524288 | tf_op jit(solution)/shard_map/all_to_all | solution.py:430
  84.6 9.1 %collective-permute-start.2 = (f32[56,128]{1,0:T(8,128)S(1)}, f32[56,128]{1,0:T(8,128)S(1)}, u32[]{:S(2)}, u32[]{:S(2)}) collective-permute-start(f32[56,128]{1,0:T(8,128)S(1)} %get-tuple-element.19.mine), channel_id=1, source_target_pairs={{0,480},{32,0},{64,32},{96,64},{128,96},{160,128},{192,160},{224,1... | collective-permute-start | bytes 86024 | tf_op jit(solution)/shard_map/ppermute | solution.py:434
  93.7 1.0 collective-permute-done.2.parcel.below
  94.7 0.0 copy-start.14
  94.7 0.2 shard_map.198.fields
  94.9 3.7 %all-to-all-done.2 = f32[256,2,128]{2,1,0:T(2,128)S(1)} async-done(((f32[256,2,128]{2,1,0:T(2,128)}), f32[256,2,128]{2,1,0:T(2,128)S(1)}, u32[]{:S(2)}, u32[]{:S(2)}) %all-to-all-start.2) | async-done | bytes 262176 | tf_op jit(solution)/shard_map/all_to_all | solution.py:430
  98.5 0.0 copy-done.14
  98.5 0.7 shard_map.199
  99.2 0.0 copy-start.12
  99.2 16.8 %all_to_all.22 = f32[288,2,128]{2,1,0:T(2,128)S(1)} all-to-all(f32[288,2,128]{2,1,0:T(2,128)S(1)} %bitcast.34), channel_id=1, replica_groups=mesh['gx'=16,'gt'=16,'core'=2] {'core','gt'}, dimensions={0} | all-to-all | bytes 589824 | tf_op jit(solution)/shard_map/all_to_all | solution.py:430
  116.0 0.0 copy-done.12
  116.0 1.1 shard_map.200
  (2 shorter events, 0.0 us)
Async XLA Ops:
  2.1 17.8 %collective-permute-start = (f32[3,8,128]{2,1,0:T(8,128)S(1)}, f32[3,8,128]{2,1,0:T(8,128)S(1)}, u32[]{:S(2)}, u32[]{:S(2)}) collective-permute-start(f32[3,8,128]{2,1,0:T(8,128)S(1)} %select_select_fusion), channel_id=1, source_target_pairs={{0,32},{32,64},{64,96},{96,128},{128,160},{160,192},{192,224},{224... | collective-permute-start | bytes 36872 | tf_op jit(solution)/shard_map/ppermute | solution.py:434
  10.4 1.0 copy-start.16
  11.4 8.5 %copy-start.1 = (f32[1,256,128]{2,1,0:T(8,128)S(1)}, f32[1,256,128]{2,1,0:T(8,128)}, u32[]{:S(2)}) copy-start(f32[1,256,128]{2,1,0:T(8,128)} %param.20) | copy-start | bytes 393220
  11.5 0.7 copy-start.15
  20.8 19.0 %copy-start.2 = (bf16[2,128,256]{2,1,0:T(8,128)(2,1)S(1)}, bf16[2,128,256]{2,1,0:T(8,128)(2,1)}, u32[]{:S(2)}) copy-start(bf16[2,128,256]{2,1,0:T(8,128)(2,1)} %constant.48.clone.second) | copy-start | bytes 393220
  20.9 19.0 %copy-start.9 = (f32[32,128]{1,0:T(8,128)S(1)}, f32[32,128]{1,0:T(8,128)}, u32[]{:S(2)}) copy-start(f32[32,128]{1,0:T(8,128)} %constant.50.clone.twist_sin) | copy-start | bytes 49156
  20.9 19.0 %copy-start.10 = (f32[32,128]{1,0:T(8,128)S(1)}, f32[32,128]{1,0:T(8,128)}, u32[]{:S(2)}) copy-start(f32[32,128]{1,0:T(8,128)} %constant.49.clone.twist_cos) | copy-start | bytes 49156
  20.9 19.0 %copy-start.11 = (bf16[2,128,128]{2,1,0:T(8,128)(2,1)S(1)}, bf16[2,128,128]{2,1,0:T(8,128)(2,1)}, u32[]{:S(2)}) copy-start(bf16[2,128,128]{2,1,0:T(8,128)(2,1)} %constant.51.clone.order) | copy-start | bytes 196612
  20.9 19.0 %copy-start.13 = (bf16[2,64,32]{2,1,0:T(8,128)(2,1)S(1)}, bf16[2,64,32]{2,1,0:T(8,128)(2,1)}, u32[]{:S(2)}) copy-start(bf16[2,64,32]{2,1,0:T(8,128)(2,1)} %constant.52.clone.first) | copy-start | bytes 24580
  39.9 27.9 %copy-start = (bf16[2,512,256]{2,1,0:T(8,128)(2,1)S(1)}, bf16[2,512,256]{2,1,0:T(8,128)(2,1)}, u32[]{:S(2)}) copy-start(bf16[2,512,256]{2,1,0:T(8,128)(2,1)} %constant.55.clone.first) | copy-start | bytes 1572868
  41.3 26.5 %copy-start.4 = (bf16[2,256,256]{2,1,0:T(8,128)(2,1)S(1)}, bf16[2,256,256]{2,1,0:T(8,128)(2,1)}, u32[]{:S(2)}) copy-start(bf16[2,256,256]{2,1,0:T(8,128)(2,1)} %constant.56.clone.second) | copy-start | bytes 786436
  41.3 26.5 %copy-start.7 = (f32[256,128]{1,0:T(8,128)S(1)}, f32[256,128]{1,0:T(8,128)}, u32[]{:S(2)}) copy-start(f32[256,128]{1,0:T(8,128)} %constant.58.clone.twist_sin) | copy-start | bytes 393220
  41.3 26.5 %copy-start.8 = (f32[256,128]{1,0:T(8,128)S(1)}, f32[256,128]{1,0:T(8,128)}, u32[]{:S(2)}) copy-start(f32[256,128]{1,0:T(8,128)} %constant.57.clone.twist_cos) | copy-start | bytes 393220
  67.8 6.1 %copy-start.3 = (bf16[2,256,256]{2,1,0:T(8,128)(2,1)S(1)}, bf16[2,256,256]{2,1,0:T(8,128)(2,1)}, u32[]{:S(2)}) copy-start(bf16[2,256,256]{2,1,0:T(8,128)(2,1)} %constant.59.clone.second) | copy-start | bytes 786436
  67.8 6.1 %copy-start.5 = (f32[256,128]{1,0:T(8,128)S(1)}, f32[256,128]{1,0:T(8,128)}, u32[]{:S(2)}) copy-start(f32[256,128]{1,0:T(8,128)} %constant.61.clone.twist_sin) | copy-start | bytes 393220
  67.8 6.1 %copy-start.6 = (f32[256,128]{1,0:T(8,128)S(1)}, f32[256,128]{1,0:T(8,128)}, u32[]{:S(2)}) copy-start(f32[256,128]{1,0:T(8,128)} %constant.60.clone.twist_cos) | copy-start | bytes 393220
  68.6 5.3 %collective-permute-start.1 = (f32[512,128]{1,0:T(8,128)S(1)}, f32[512,128]{1,0:T(8,128)S(1)}, u32[]{:S(2)}, u32[]{:S(2)}) collective-permute-start(f32[512,128]{1,0:T(8,128)S(1)} %shard_map.196.mine), channel_id=1, source_target_pairs={{0,1},{1,0},{2,3},{3,2},{4,5},{5,4},{6,7},{7,6},{8,9},{9,8},{10,11... | collective-permute-start | bytes 786440 | tf_op jit(solution)/shard_map/ppermute | solution.py:468
  75.4 23.1 %all-to-all-start.2 = ((f32[256,2,128]{2,1,0:T(2,128)}), f32[256,2,128]{2,1,0:T(2,128)S(1)}, u32[]{:S(2)}, u32[]{:S(2)}) async-start(f32[256,2,128]{2,1,0:T(2,128)} %bitcast.14), calls=%async_computation.2 | async-start | bytes 524288 | tf_op jit(solution)/shard_map/all_to_all | solution.py:430
  84.6 10.1 %collective-permute-start.2 = (f32[56,128]{1,0:T(8,128)S(1)}, f32[56,128]{1,0:T(8,128)S(1)}, u32[]{:S(2)}, u32[]{:S(2)}) collective-permute-start(f32[56,128]{1,0:T(8,128)S(1)} %get-tuple-element.19.mine), channel_id=1, source_target_pairs={{0,480},{32,0},{64,32},{96,64},{128,96},{160,128},{192,160},{224,1... | collective-permute-start | bytes 86024 | tf_op jit(solution)/shard_map/ppermute | solution.py:434
  94.7 3.9 %copy-start.14 = (bf16[2,32,64]{2,1,0:T(8,128)(2,1)S(1)}, bf16[2,32,64]{2,1,0:T(8,128)(2,1)}, u32[]{:S(2)}) copy-start(bf16[2,32,64]{2,1,0:T(8,128)(2,1)} %constant.53.clone.first) | copy-start | bytes 24580
  99.2 16.8 %copy-start.12 = (bf16[128,128]{1,0:T(8,128)(2,1)S(1)}, bf16[128,128]{1,0:T(8,128)(2,1)}, u32[]{:S(2)}) copy-start(bf16[128,128]{1,0:T(8,128)(2,1)} %constant.54.clone.columns) | copy-start | bytes 98308

commit v6 on v5

--- a/solution.py
+++ b/solution.py
@@ -32,7 +32,7 @@
 SPAN = 20
 HALF = 64
 BLOCK = SLAB + 4
-BACK = SLAB + 2
+BACK = SLAB + 1
 CHIPS = 256
 COLS = 4096
 ROWS = 4096
@@ -91,16 +91,17 @@
     second = angles(64, range(128), 128)
     twist = angles(OUTER, range(128), COLS)
     mix = np.block([[np.cos(second), np.sin(second)], [-np.sin(second), np.cos(second)]])
-    rest = [split_table(mix), table(np.cos(twist)), table(np.sin(twist))]
     slot, s = np.divmod(np.arange(4 * SLAB), SLAB)
     order = np.zeros((128, 128))
     order[np.arange(4 * SLAB), EDGE * s + slot] = 1.0
-    stacked = np.concatenate([cosine, -sine], axis=0)
-    forward = [split_table(order), split_table(stacked)] + rest
-    backward = [split_table(np.concatenate([cosine, -sine], axis=1)[CORE_MAJOR])] + rest
+    every = np.zeros((128 + 2 * OUTER + OUTER, 256))
+    every[:128] = mix
+    every[128 : 128 + 2 * OUTER, :OUTER] = np.concatenate([cosine, -sine], axis=0)
+    every[128 + 2 * OUTER :, : 2 * OUTER] = np.concatenate([cosine, -sine], axis=1)[CORE_MAJOR]
+    shared = [split_table(every), table(np.cos(twist)), table(np.sin(twist))]
     columns = np.zeros((128, 128))
     columns[np.arange(4 * SLAB), (slot - SHIFT) % TILE_COLS] = 1.0
-    return forward, backward, jnp.asarray(columns.astype(jnp.bfloat16))
+    return shared, split_table(order), jnp.asarray(columns.astype(jnp.bfloat16))
 
 
 def row_tables():
@@ -290,7 +291,7 @@
 
 
 def columns_forward_kernel(
-    info, data, porous, phase, heat, order, first, second, twist_cos, twist_sin, out, parcel
+    info, data, porous, phase, heat, order, every, twist_cos, twist_sin, out, parcel
 ):
     polar, value = edge_polar(info, data)
     for f, field in enumerate((porous, phase, heat)):
@@ -304,7 +305,8 @@
         around = roll(packed, -EDGE * s - SHIFT, 1)
         parts.append(jnp.where(outer, around, data[pl.ds(s, OUTER, stride=BLOCK), :]))
     rows = jnp.concatenate(parts, axis=1)
-    spread = dot((first[0], first[1]), halves(rows))
+    first = slice(128, 128 + 2 * OUTER)
+    spread = dot((every[0, first, :OUTER], every[1, first, :OUTER]), halves(rows))
     cosine, sine = twist_cos[...], twist_sin[...]
     real, imag = [], []
     for s in range(SLAB):
@@ -317,19 +319,19 @@
         re = jnp.concatenate([part[span] for part in real], axis=0)
         im = jnp.concatenate([part[span] for part in imag], axis=0)
         both = jnp.concatenate([re, im], axis=1)
-        final = dot((second[0], second[1]), halves(both), ((1,), (1,)))
+        final = dot((every[0, :128], every[1, :128]), halves(both), ((1,), (1,)))
         out[pl.ds(2 * g, 64, stride=8), :] = final[:64]
         out[pl.ds(2 * g + 1, 64, stride=8), :] = final[64:]
 
 
-def columns_backward_kernel(info, data, mine, below, first, second, twist_cos, twist_sin, out):
+def columns_backward_kernel(info, data, mine, below, every, twist_cos, twist_sin, out):
     real, imag = [], []
     for g in range(4):
         span = slice(g * 8, (g + 1) * 8)
         both = jnp.concatenate(
             [data[pl.ds(2 * g, 64, stride=8), :], data[pl.ds(2 * g + 1, 64, stride=8), :]], axis=0
         )
-        spread = dot(halves(both.T), (second[0], second[1]))
+        spread = dot(halves(both.T), (every[0, :128], every[1, :128]))
         re = spread[:, :128].reshape(SLAB, 8, 128)
         im = spread[:, 128:].reshape(SLAB, 8, 128)
         cosine, sine = twist_cos[span][None], twist_sin[span][None]
@@ -338,7 +340,8 @@
     stacked = jnp.concatenate(
         [jnp.concatenate([part[s] for part in real + imag], axis=0) for s in range(SLAB)], axis=1
     )
-    final = dot((first[0], first[1]), halves(stacked))
+    first = slice(128 + 2 * OUTER, 128 + 3 * OUTER)
+    final = dot((every[0, first, : 2 * OUTER], every[1, first, : 2 * OUTER]), halves(stacked))
     for s in range(SLAB):
         part = final[:, s * 128 : (s + 1) * 128]
         out[pl.ds(s, OUTER, stride=BACK), :] = known(info, SLOPE) - part
@@ -349,7 +352,6 @@
         rows = pl.ds(3 * EDGE + core, SLAB, stride=2)
         start = core * SLAB * BACK + SLAB
         out[pl.ds(start, SLAB, stride=BACK), :] = jnp.where(late, below[rows, :], mine[rows, :])
-        out[pl.ds(start + 1, SLAB, stride=BACK), :] = jnp.zeros((SLAB, TILE_COLS), jnp.float32)
 
 
 def place_kernel(data, fields, columns, phase, heat, gradient):
@@ -448,7 +450,7 @@
     gy = ("gt", "core")
     chips = ("gx", "gt")
     place = jnp.stack([gx_index, gt_index * core_size + core, gx_index * gt_size + gt_index, core])
-    (col_to, col_back, columns), (row_to, row_back) = column_tables(), row_tables()
+    (shared, order, columns), (row_to, row_back) = column_tables(), row_tables()
     tile = (TILE_ROWS, TILE_COLS)
     above = shift(bottom_strip(voxel, wetted, heat), "gx", gx_size, 1)
     porous = voxel[0].astype(jnp.float32)
@@ -461,7 +463,7 @@
     slab = exchange(polar, gy, 4).reshape(-1, 128)
     spec, parcel = call(
         columns_forward_kernel, [(2 * CHIPS, 128), (3 * EDGE + OUTER, 128)],
-        info, slab, porous, phase, heat, *col_to,
+        info, slab, porous, phase, heat, order, *shared,
     )
     spec = exchange(spec, chips, 2).reshape(-1, 128)
     (mine,) = call(rows_forward_kernel, [(2 * CHIPS, 128)], info, spec, *row_to)
@@ -473,9 +475,9 @@
     (fields,) = call(tail_kernel, [(2,) + tile], info, porous, phase, heat, fields, below)
     green, below, fields = lax.optimization_barrier((green, below, fields))
     (answer,) = call(
-        columns_backward_kernel, [(OUTER * BACK, 128)], info, green, parcel, below, *col_back
-    )
-    answer = exchange(answer, ("core", "gt"), 2).reshape(-1, 128)
+        columns_backward_kernel, [(OUTER * BACK, 128)], info, green, parcel, below, *shared
+    )
+    answer = exchange(answer, ("core", "gt"), 1).reshape(-1, 128)
     phase, heat, gradient = call(
         place_kernel, [tile, tile, (2 * TILE_ROWS, TILE_COLS)], answer, fields, columns
     )

time: 118 us -> 117 us (level)
  no operation moved by 1% of the time
where the time goes in v6:
time: 117 us
  blocking collectives  61.9 us (53%)
  starting transfers between devices  30.7 us (26%)
  waiting for transfers between devices  13 us (11%)
  Pallas kernels  6.93 us (6%)
  other arithmetic  2.59 us (2%)
    all_to_all x3, blocking collectives, exchange(): return lax.all_to_all(blocks, axes, split_axis=0, concat_axis=0, tiled=True)  61.9 us
    ppermute x2, starting transfers between devices, shift(): lax.ppermute(block, axes, [(i, (i + step) % count) for i in range(count)])  17.4 us
    all_to_all x1, starting transfers between devices, exchange(): return lax.all_to_all(blocks, axes, split_axis=0, concat_axis=0, tiled=True)  9.17 us
    ppermute x2, waiting for transfers between devices, shift(): lax.ppermute(block, axes, [(i, (i + step) % count) for i in range(count)])  8.17 us
    pallas_call x8, Pallas kernels, call(): pl.pallas_call(kernel, out_shape=shapes, in_specs=spaces, out_specs=[VMEM...  6.93 us
    ppermute x1, starting transfers between devices, body(): other = lax.ppermute(mine, 'core', [(0, 1), (1, 0)])  4.14 us
    all_to_all x1, waiting for transfers between devices, exchange(): return lax.all_to_all(blocks, axes, split_axis=0, concat_axis=0, tiled=True)  3.68 us
  transfers between devices with their start and end apart: 4, of which 4 were waited for; matrix products, arithmetic and copies ran while one was open for 1% of the time, Pallas kernels for 1%

profile of v6, /device:TPU:1, one launch (start us, length us, event | category | flops | bytes accessed | tf_op | source)
XLA Modules:
  0.0 116.7 jit_solution(3190438973728122186)
XLA Ops:
  0.6 0.7 negate_bitcast_fusion
  1.3 0.7 convert_bitcast_fusion.1
  2.0 0.1 select_select_fusion
  2.1 8.3 %collective-permute-start = (f32[3,8,128]{2,1,0:T(8,128)S(1)}, f32[3,8,128]{2,1,0:T(8,128)S(1)}, u32[]{:S(2)}, u32[]{:S(2)}) collective-permute-start(f32[3,8,128]{2,1,0:T(8,128)S(1)} %select_select_fusion), channel_id=1, source_target_pairs={{0,32},{32,64},{64,96},{96,128},{128,160},{160,192},{192,224},{224... | collective-permute-start | bytes 36872 | tf_op jit(solution)/shard_map/ppermute | solution.py:436
  10.4 0.0 copy-start.14
  10.4 1.0 bitcast_multiply_fusion.phase
  11.4 0.0 copy-done.14
  11.4 0.0 copy-start.1
  11.5 0.0 copy-start.13
  11.5 0.1 pad_add_fusion.place
  11.6 0.6 copy-done.13
  12.2 0.6 shard_map.175.info
  12.7 7.2 %collective-permute-done.above = f32[3,8,128]{2,1,0:T(8,128)S(1)} collective-permute-done((f32[3,8,128]{2,1,0:T(8,128)S(1)}, f32[3,8,128]{2,1,0:T(8,128)S(1)}, u32[]{:S(2)}, u32[]{:S(2)}) %collective-permute-start) | collective-permute-done | bytes 12320 | tf_op jit(solution)/shard_map/ppermute | solution.py:436
  19.9 0.0 copy-done.1
  19.9 0.9 shard_map.176
  20.8 0.0 copy-start.2
  20.9 0.0 copy-start.9
  20.9 0.0 copy-start.10
  20.9 0.0 copy-start.11
  20.9 18.9 %all_to_all.20 = f32[160,4,128]{2,1,0:T(4,128)S(1)} all-to-all(f32[160,4,128]{2,1,0:T(4,128)S(1)} %bitcast.40), channel_id=1, replica_groups=mesh['gx'=16,'gt'=16,'core'=2] {'gt','core'}, dimensions={0} | all-to-all | bytes 655360 | tf_op jit(solution)/shard_map/all_to_all | solution.py:432
  39.8 0.0 copy-done.2
  39.8 0.0 copy-done.9
  39.8 0.0 copy-done.10
  39.8 0.0 copy-done.11
  39.8 0.0 copy-start.4
  39.9 0.0 copy-start.7
  39.9 0.0 copy-start.8
  39.9 1.4 %shard_map.177 = (f32[512,128]{1,0:T(8,128)S(1)}, f32[56,128]{1,0:T(8,128)S(1)}) custom-call(f32[8,128]{1,0:T(8,128)S(1)} %shard_map.175.info, f32[640,128]{1,0:T(8,128)S(1)} %bitcast.32, f32[256,128]{1,0:T(8,128)S(1)} %convert_bitcast_fusion.porous, f32[256,128]{1,0:T(8,128)S(1)} %bitcast_multiply_fusion.phase, f32[256,128]{1,0:T(8,128)S(1)} %bitcast.34, ...), custom_call_target="tpu_custom_call" | custom-call | tf_op jit(solution)/shard_map/pallas_call | solution.py:62
  41.3 0.0 copy-start
  41.3 26.5 %all_to_all.21 = f32[256,2,128]{2,1,0:T(2,128)S(1)} all-to-all(f32[256,2,128]{2,1,0:T(2,128)S(1)} %bitcast.41), channel_id=1, replica_groups=mesh['gx'=16,'gt'=16,'core'=2] {'gx','gt'}, dimensions={0} | all-to-all | bytes 524288 | tf_op jit(solution)/shard_map/all_to_all | solution.py:432
  67.7 0.0 copy-done.4
  67.7 0.0 copy-done.7
  67.7 0.0 copy-done.8
  67.8 0.0 copy-done
  67.8 0.0 copy-start.3
  67.8 0.0 copy-start.5
  67.8 0.0 copy-start.6
  67.8 0.7 shard_map.178.mine
  68.5 4.1 %collective-permute-start.1 = (f32[512,128]{1,0:T(8,128)S(1)}, f32[512,128]{1,0:T(8,128)S(1)}, u32[]{:S(2)}, u32[]{:S(2)}) collective-permute-start(f32[512,128]{1,0:T(8,128)S(1)} %shard_map.178.mine), channel_id=1, source_target_pairs={{0,1},{1,0},{2,3},{3,2},{4,5},{5,4},{6,7},{7,6},{8,9},{9,8},{10,11... | collective-permute-start | bytes 786440 | tf_op jit(solution)/shard_map/ppermute | solution.py:470
  72.7 1.1 collective-permute-done.1.other
  73.8 0.0 copy-done.3
  73.8 0.0 copy-done.5
  73.8 0.0 copy-done.6
  73.8 1.5 %shard_map.179 = f32[512,128]{1,0:T(8,128)} custom-call(f32[8,128]{1,0:T(8,128)S(1)} %shard_map.175.info, f32[512,128]{1,0:T(8,128)S(1)} %shard_map.178.mine, f32[512,128]{1,0:T(8,128)S(1)} %collective-permute-done.1.other, bf16[2,512,256]{2,1,0:T(8,128)(2,1)S(1)} %copy-done, bf16[2,256,256]{2,1,0:T(8,128)(2,1)S(1)} %copy-done.3, f32[256,128]{1,0:T(8,128)S(1)} %copy-done.6, ...), custom_call_target="tpu_custom_call" | custom-call | tf_op jit(solution)/shard_map/pallas_call | solution.py:62
  75.4 9.2 %all-to-all-start.2 = ((f32[256,2,128]{2,1,0:T(2,128)}), f32[256,2,128]{2,1,0:T(2,128)S(1)}, u32[]{:S(2)}, u32[]{:S(2)}) async-start(f32[256,2,128]{2,1,0:T(2,128)} %bitcast.14), calls=%async_computation.2 | async-start | bytes 524288 | tf_op jit(solution)/shard_map/all_to_all | solution.py:432
  84.5 9.1 %collective-permute-start.2 = (f32[56,128]{1,0:T(8,128)S(1)}, f32[56,128]{1,0:T(8,128)S(1)}, u32[]{:S(2)}, u32[]{:S(2)}) collective-permute-start(f32[56,128]{1,0:T(8,128)S(1)} %get-tuple-element.19.mine), channel_id=1, source_target_pairs={{0,480},{32,0},{64,32},{96,64},{128,96},{160,128},{192,160},{224,1... | collective-permute-start | bytes 86024 | tf_op jit(solution)/shard_map/ppermute | solution.py:436
  93.7 1.0 collective-permute-done.2.parcel.below
  94.7 0.2 shard_map.180.fields
  94.8 3.7 %all-to-all-done.2 = f32[256,2,128]{2,1,0:T(2,128)S(1)} async-done(((f32[256,2,128]{2,1,0:T(2,128)}), f32[256,2,128]{2,1,0:T(2,128)S(1)}, u32[]{:S(2)}, u32[]{:S(2)}) %all-to-all-start.2) | async-done | bytes 262176 | tf_op jit(solution)/shard_map/all_to_all | solution.py:432
  98.5 0.6 shard_map.181
  99.2 0.0 copy-start.12
  99.2 16.5 %all_to_all.22 = f32[544,1,128]{2,1,0:T(1,128)S(1)} all-to-all(f32[544,1,128]{2,1,0:T(1,128)S(1)} %bitcast.37), channel_id=1, replica_groups=mesh['gx'=16,'gt'=16,'core'=2] {'core','gt'}, dimensions={0} | all-to-all | bytes 557056 | tf_op jit(solution)/shard_map/all_to_all | solution.py:432
  115.7 0.0 copy-done.12
  115.7 1.0 shard_map.182
  (2 shorter events, 0.0 us)
Async XLA Ops:
  2.1 17.8 %collective-permute-start = (f32[3,8,128]{2,1,0:T(8,128)S(1)}, f32[3,8,128]{2,1,0:T(8,128)S(1)}, u32[]{:S(2)}, u32[]{:S(2)}) collective-permute-start(f32[3,8,128]{2,1,0:T(8,128)S(1)} %select_select_fusion), channel_id=1, source_target_pairs={{0,32},{32,64},{64,96},{96,128},{128,160},{160,192},{192,224},{224... | collective-permute-start | bytes 36872 | tf_op jit(solution)/shard_map/ppermute | solution.py:436
  10.4 1.0 copy-start.14
  11.4 8.5 %copy-start.1 = (f32[1,256,128]{2,1,0:T(8,128)S(1)}, f32[1,256,128]{2,1,0:T(8,128)}, u32[]{:S(2)}) copy-start(f32[1,256,128]{2,1,0:T(8,128)} %param.18) | copy-start | bytes 393220
  11.5 0.7 copy-start.13
  20.8 19.0 %copy-start.2 = (bf16[2,224,256]{2,1,0:T(8,128)(2,1)S(1)}, bf16[2,224,256]{2,1,0:T(8,128)(2,1)}, u32[]{:S(2)}) copy-start(bf16[2,224,256]{2,1,0:T(8,128)(2,1)} %constant.44.clone.every) | copy-start | bytes 688132
  20.9 19.0 %copy-start.9 = (bf16[2,128,128]{2,1,0:T(8,128)(2,1)S(1)}, bf16[2,128,128]{2,1,0:T(8,128)(2,1)}, u32[]{:S(2)}) copy-start(bf16[2,128,128]{2,1,0:T(8,128)(2,1)} %constant.47.clone.order) | copy-start | bytes 196612
  20.9 19.0 %copy-start.10 = (f32[32,128]{1,0:T(8,128)S(1)}, f32[32,128]{1,0:T(8,128)}, u32[]{:S(2)}) copy-start(f32[32,128]{1,0:T(8,128)} %constant.46.clone.twist_sin) | copy-start | bytes 49156
  20.9 19.0 %copy-start.11 = (f32[32,128]{1,0:T(8,128)S(1)}, f32[32,128]{1,0:T(8,128)}, u32[]{:S(2)}) copy-start(f32[32,128]{1,0:T(8,128)} %constant.45.clone.twist_cos) | copy-start | bytes 49156
  39.8 27.9 %copy-start.4 = (bf16[2,256,256]{2,1,0:T(8,128)(2,1)S(1)}, bf16[2,256,256]{2,1,0:T(8,128)(2,1)}, u32[]{:S(2)}) copy-start(bf16[2,256,256]{2,1,0:T(8,128)(2,1)} %constant.50.clone.second) | copy-start | bytes 786436
  39.9 27.9 %copy-start.7 = (f32[256,128]{1,0:T(8,128)S(1)}, f32[256,128]{1,0:T(8,128)}, u32[]{:S(2)}) copy-start(f32[256,128]{1,0:T(8,128)} %constant.52.clone.twist_sin) | copy-start | bytes 393220
  39.9 27.9 %copy-start.8 = (f32[256,128]{1,0:T(8,128)S(1)}, f32[256,128]{1,0:T(8,128)}, u32[]{:S(2)}) copy-start(f32[256,128]{1,0:T(8,128)} %constant.51.clone.twist_cos) | copy-start | bytes 393220
  41.3 26.5 %copy-start = (bf16[2,512,256]{2,1,0:T(8,128)(2,1)S(1)}, bf16[2,512,256]{2,1,0:T(8,128)(2,1)}, u32[]{:S(2)}) copy-start(bf16[2,512,256]{2,1,0:T(8,128)(2,1)} %constant.49.clone.first) | copy-start | bytes 1572868
  67.8 6.1 %copy-start.3 = (bf16[2,256,256]{2,1,0:T(8,128)(2,1)S(1)}, bf16[2,256,256]{2,1,0:T(8,128)(2,1)}, u32[]{:S(2)}) copy-start(bf16[2,256,256]{2,1,0:T(8,128)(2,1)} %constant.53.clone.second) | copy-start | bytes 786436
  67.8 6.1 %copy-start.5 = (f32[256,128]{1,0:T(8,128)S(1)}, f32[256,128]{1,0:T(8,128)}, u32[]{:S(2)}) copy-start(f32[256,128]{1,0:T(8,128)} %constant.55.clone.twist_sin) | copy-start | bytes 393220
  67.8 6.0 %copy-start.6 = (f32[256,128]{1,0:T(8,128)S(1)}, f32[256,128]{1,0:T(8,128)}, u32[]{:S(2)}) copy-start(f32[256,128]{1,0:T(8,128)} %constant.54.clone.twist_cos) | copy-start | bytes 393220
  68.5 5.3 %collective-permute-start.1 = (f32[512,128]{1,0:T(8,128)S(1)}, f32[512,128]{1,0:T(8,128)S(1)}, u32[]{:S(2)}, u32[]{:S(2)}) collective-permute-start(f32[512,128]{1,0:T(8,128)S(1)} %shard_map.178.mine), channel_id=1, source_target_pairs={{0,1},{1,0},{2,3},{3,2},{4,5},{5,4},{6,7},{7,6},{8,9},{9,8},{10,11... | collective-permute-start | bytes 786440 | tf_op jit(solution)/shard_map/ppermute | solution.py:470
  75.4 23.1 %all-to-all-start.2 = ((f32[256,2,128]{2,1,0:T(2,128)}), f32[256,2,128]{2,1,0:T(2,128)S(1)}, u32[]{:S(2)}, u32[]{:S(2)}) async-start(f32[256,2,128]{2,1,0:T(2,128)} %bitcast.14), calls=%async_computation.2 | async-start | bytes 524288 | tf_op jit(solution)/shard_map/all_to_all | solution.py:432
  84.5 10.1 %collective-permute-start.2 = (f32[56,128]{1,0:T(8,128)S(1)}, f32[56,128]{1,0:T(8,128)S(1)}, u32[]{:S(2)}, u32[]{:S(2)}) collective-permute-start(f32[56,128]{1,0:T(8,128)S(1)} %get-tuple-element.19.mine), channel_id=1, source_target_pairs={{0,480},{32,0},{64,32},{96,64},{128,96},{160,128},{192,160},{224,1... | collective-permute-start | bytes 86024 | tf_op jit(solution)/shard_map/ppermute | solution.py:436
  99.2 16.5 %copy-start.12 = (bf16[128,128]{1,0:T(8,128)(2,1)S(1)}, bf16[128,128]{1,0:T(8,128)(2,1)}, u32[]{:S(2)}) copy-start(bf16[128,128]{1,0:T(8,128)(2,1)} %constant.48.clone.columns) | copy-start | bytes 98308

commit v7 on v6

--- a/solution.py
+++ b/solution.py
@@ -37,6 +37,10 @@
 COLS = 4096
 ROWS = 4096
 CORE_MAJOR = np.arange(OUTER).reshape(-1, 2).T.reshape(-1)
+SIZES = {"z": 8, "y_hi": 2, "x": 4, "y_lo": 4, "core": 2}
+GX_AXES, GY_AXES = ("z", "y_hi"), ("x", "y_lo", "core")
+CHIP_AXES = ("y_lo", "x", "y_hi", "z")
+CHIP_ORDER = np.arange(CHIPS).reshape(8, 2, 4, 4).transpose(3, 2, 1, 0).reshape(-1)
 VMEM = pl.BlockSpec(memory_space=pltpu.VMEM)
 SMEM = pl.BlockSpec(memory_space=pltpu.SMEM)
 
@@ -106,9 +110,10 @@
 
 def row_tables():
     first = angles(CHIPS, range(CHIPS), CHIPS)
-    both = split_table(np.concatenate([np.cos(first), np.sin(first)], axis=0))
+    cosine, sine = np.cos(first)[:, CHIP_ORDER], np.sin(first)[:, CHIP_ORDER]
+    starts = (np.concatenate([cosine, sine], axis=0), np.concatenate([cosine.T, sine.T], axis=0))
     tables = []
-    for shift, sign in ((SHIFT, -1.0), (0, 1.0)):
+    for shift, sign, start in ((SHIFT, -1.0, starts[0]), (0, 1.0, starts[1])):
         inner = np.arange(SLAB) - shift
         second = angles(SLAB, inner, SLAB)
         twist = np.repeat(angles(CHIPS, inner, ROWS), 8, axis=1)
@@ -116,15 +121,16 @@
         if shift:
             cosine, sine = cosine.T, sine.T
         mix = np.block([[cosine, sine], [-sine, cosine]])
-        tables.append([both, split_table(mix), table(np.cos(twist)), table(np.sin(twist))])
+        rest = [split_table(mix), table(np.cos(twist)), table(np.sin(twist))]
+        tables.append([split_table(start)] + rest)
     return tables
 
 
-GX, GY, CHIP, CORE, SLOPE_X, SLOPE_Y, SLOPE = range(7)
+GX, GY, CHIP, CORE, PLACE, SLOPE_X, SLOPE_Y, SLOPE = range(8)
 
 
 def prepare_kernel(place, slope, info):
-    values = [place[i].astype(jnp.float32) for i in range(4)] + [slope[0, 0], slope[0, 1]]
+    values = [place[i].astype(jnp.float32) for i in range(5)] + [slope[0, 0], slope[0, 1]]
     values.append(jnp.where(place[3] == 0, slope[0, 0], slope[0, 1]))
     row = lax.broadcasted_iota(jnp.int32, info.shape, 0)
     filled = jnp.zeros(info.shape, jnp.float32)
@@ -346,8 +352,7 @@
         part = final[:, s * 128 : (s + 1) * 128]
         out[pl.ds(s, OUTER, stride=BACK), :] = known(info, SLOPE) - part
     lane = lax.broadcasted_iota(jnp.int32, (SLAB, TILE_COLS), 1)
-    slab = known(info, CHIP) - SLAB * known(info, GX)
-    late = (slab == 0.0) & (lane % SLAB < SHIFT)
+    late = (known(info, PLACE) == 0.0) & (lane % SLAB < SHIFT)
     for core in range(2):
         rows = pl.ds(3 * EDGE + core, SLAB, stride=2)
         start = core * SLAB * BACK + SLAB
@@ -444,15 +449,12 @@
 
 
 def body(voxel, wetted, heat, slope):
-    gx_index, gt_index, core = (lax.axis_index(name) for name in ("gx", "gt", "core"))
-    gx_size, gt_size, core_size = (lax.axis_size(name) for name in ("gx", "gt", "core"))
-    gy_size = gt_size * core_size
-    gy = ("gt", "core")
-    chips = ("gx", "gt")
-    place = jnp.stack([gx_index, gt_index * core_size + core, gx_index * gt_size + gt_index, core])
+    gx_size, gy_size = ROWS // TILE_ROWS, COLS // TILE_COLS
+    indices = (GX_AXES, GY_AXES, CHIP_AXES, "core", ("x", "y_lo"))
+    place = jnp.stack([lax.axis_index(axes) for axes in indices])
     (shared, order, columns), (row_to, row_back) = column_tables(), row_tables()
     tile = (TILE_ROWS, TILE_COLS)
-    above = shift(bottom_strip(voxel, wetted, heat), "gx", gx_size, 1)
+    above = shift(bottom_strip(voxel, wetted, heat), GX_AXES, gx_size, 1)
     porous = voxel[0].astype(jnp.float32)
     phase = porous * wetted[0].astype(jnp.float32)
     heat = heat[0]
@@ -460,24 +462,24 @@
     polar, fields = call(
         polar_kernel, [(OUTER * BLOCK, 128), (2,) + tile], info, porous, phase, heat, above
     )
-    slab = exchange(polar, gy, 4).reshape(-1, 128)
+    slab = exchange(polar, GY_AXES, 4).reshape(-1, 128)
     spec, parcel = call(
         columns_forward_kernel, [(2 * CHIPS, 128), (3 * EDGE + OUTER, 128)],
         info, slab, porous, phase, heat, order, *shared,
     )
-    spec = exchange(spec, chips, 2).reshape(-1, 128)
+    spec = exchange(spec, CHIP_AXES, 2).reshape(-1, 128)
     (mine,) = call(rows_forward_kernel, [(2 * CHIPS, 128)], info, spec, *row_to)
     other = lax.ppermute(mine, "core", [(0, 1), (1, 0)])
     (green,) = call(rows_backward_kernel, [(2 * CHIPS, 128)], info, mine, other, *row_back)
     green, parcel = lax.optimization_barrier((green, parcel))
-    below = shift(parcel, "gx", gx_size, -1)
-    green = exchange(green, chips, 2).reshape(-1, 128)
+    below = shift(parcel, GX_AXES, gx_size, -1)
+    green = exchange(green, CHIP_AXES, 2).reshape(-1, 128)
     (fields,) = call(tail_kernel, [(2,) + tile], info, porous, phase, heat, fields, below)
     green, below, fields = lax.optimization_barrier((green, below, fields))
     (answer,) = call(
         columns_backward_kernel, [(OUTER * BACK, 128)], info, green, parcel, below, *shared
     )
-    answer = exchange(answer, ("core", "gt"), 1).reshape(-1, 128)
+    answer = exchange(answer, ("core", "x", "y_lo"), 1).reshape(-1, 128)
     phase, heat, gradient = call(
         place_kernel, [tile, tile, (2 * TILE_ROWS, TILE_COLS)], answer, fields, columns
     )
@@ -485,9 +487,7 @@
 
 
 def solution(mesh):
-    gx_size, gy_size = mesh.devices.shape
-    fine = Mesh(mesh.devices.reshape(gx_size, gy_size // 2, 2), ("gx", "gt", "core"))
-    gy = ("gt", "core")
-    in_specs = (P(None, "gx", gy), P(None, "gx", gy), P(None, "gx", gy), P())
-    out_specs = (P(None, "gx", gy), P(None, "gx", gy), P(None, None, "gx", gy))
+    fine = Mesh(mesh.devices.reshape(tuple(SIZES.values())), tuple(SIZES))
+    in_specs = (P(None, GX_AXES, GY_AXES),) * 3 + (P(),)
+    out_specs = (P(None, GX_AXES, GY_AXES),) * 2 + (P(None, None, GX_AXES, GY_AXES),)
     return jax.shard_map(body, mesh=fine, in_specs=in_specs, out_specs=out_specs, check_vma=False)

time: 117 us -> 116 us (level)
    ppermute x2, starting transfers between devices: 17.4 us -> 16 us  [shift(): lax.ppermute(block, axes, [(i, (i + step) % count) for i in range(count)])]
where the time goes in v7:
time: 116 us
  blocking collectives  62 us (53%)
  starting transfers between devices  29.8 us (26%)
  waiting for transfers between devices  12.7 us (11%)
  Pallas kernels  6.95 us (6%)
  other arithmetic  2.48 us (2%)
    all_to_all x3, blocking collectives, exchange(): return lax.all_to_all(blocks, axes, split_axis=0, concat_axis=0, tiled=True)  62 us
    ppermute x2, starting transfers between devices, shift(): lax.ppermute(block, axes, [(i, (i + step) % count) for i in range(count)])  16 us
    all_to_all x1, starting transfers between devices, exchange(): return lax.all_to_all(blocks, axes, split_axis=0, concat_axis=0, tiled=True)  9.83 us
    ppermute x2, waiting for transfers between devices, shift(): lax.ppermute(block, axes, [(i, (i + step) % count) for i in range(count)])  8.95 us
    pallas_call x8, Pallas kernels, call(): pl.pallas_call(kernel, out_shape=shapes, in_specs=spaces, out_specs=[VMEM...  6.95 us
    ppermute x1, starting transfers between devices, body(): other = lax.ppermute(mine, 'core', [(0, 1), (1, 0)])  3.95 us
    all_to_all x1, waiting for transfers between devices, exchange(): return lax.all_to_all(blocks, axes, split_axis=0, concat_axis=0, tiled=True)  2.65 us
  transfers between devices with their start and end apart: 4, of which 4 were waited for; matrix products, arithmetic and copies ran while one was open for 1% of the time, Pallas kernels for 1%

profile of v7, /device:TPU:1, one launch (start us, length us, event | category | flops | bytes accessed | tf_op | source)
XLA Modules:
  0.0 115.6 jit_solution(13747686275822465705)
XLA Ops:
  0.6 0.7 negate_bitcast_fusion
  1.3 0.7 convert_bitcast_fusion.1
  2.0 0.1 select_select_fusion
  2.1 0.0 copy-start.15
  2.1 8.4 %collective-permute-start = (f32[3,8,128]{2,1,0:T(8,128)S(1)}, f32[3,8,128]{2,1,0:T(8,128)S(1)}, u32[]{:S(2)}, u32[]{:S(2)}) collective-permute-start(f32[3,8,128]{2,1,0:T(8,128)S(1)} %select_select_fusion), channel_id=1, source_target_pairs={{0,32},{32,64},{64,96},{96,128},{128,160},{160,192},{192,224},{224... | collective-permute-start | bytes 36872 | tf_op jit(solution)/shard_map/ppermute | solution.py:441
  10.5 1.0 bitcast_multiply_fusion.phase
  11.5 0.0 copy-done.15
  11.5 0.0 copy-start
  11.6 0.0 copy-start.14
  11.6 0.1 stack.23.place
  11.7 0.6 copy-done.14
  12.3 0.6 shard_map.184.info
  12.8 7.2 %collective-permute-done.above = f32[3,8,128]{2,1,0:T(8,128)S(1)} collective-permute-done((f32[3,8,128]{2,1,0:T(8,128)S(1)}, f32[3,8,128]{2,1,0:T(8,128)S(1)}, u32[]{:S(2)}, u32[]{:S(2)}) %collective-permute-start) | collective-permute-done | bytes 12320 | tf_op jit(solution)/shard_map/ppermute | solution.py:441
  20.1 0.0 copy-done
  20.1 0.9 shard_map.185
  21.0 0.0 copy-start.1
  21.0 0.0 copy-start.10
  21.0 0.0 copy-start.11
  21.0 0.0 copy-start.12
  21.0 18.9 %all_to_all.20 = f32[160,4,128]{2,1,0:T(4,128)S(1)} all-to-all(f32[160,4,128]{2,1,0:T(4,128)S(1)} %bitcast.41), channel_id=1, replica_groups=mesh['z'=8,'y_hi'=2,'x'=4,'y_lo'=4,'core'=2] {'x','y_lo','core'}, dimensions={0} | all-to-all | bytes 655360 | tf_op jit(solution)/shard_map/all_to_all | solution.py:437
  40.0 0.0 copy-done.1
  40.0 0.0 copy-done.10
  40.0 0.0 copy-done.11
  40.0 0.0 copy-done.12
  40.0 0.0 copy-start.5
  40.0 0.0 copy-start.8
  40.0 0.0 copy-start.9
  40.0 1.4 %shard_map.186 = (f32[512,128]{1,0:T(8,128)S(1)}, f32[56,128]{1,0:T(8,128)S(1)}) custom-call(f32[8,128]{1,0:T(8,128)S(1)} %shard_map.184.info, f32[640,128]{1,0:T(8,128)S(1)} %bitcast.33, f32[256,128]{1,0:T(8,128)S(1)} %convert_bitcast_fusion.porous, f32[256,128]{1,0:T(8,128)S(1)} %bitcast_multiply_fusion.phase, f32[256,128]{1,0:T(8,128)S(1)} %bitcast.35, ...), custom_call_target="tpu_custom_call" | custom-call | tf_op jit(solution)/shard_map/pallas_call | solution.py:66
  41.4 0.0 copy-start.3
  41.4 25.2 %all_to_all.21 = f32[256,2,128]{2,1,0:T(2,128)S(1)} all-to-all(f32[256,2,128]{2,1,0:T(2,128)S(1)} %bitcast.42), channel_id=1, replica_groups=mesh['z'=8,'y_hi'=2,'x'=4,'y_lo'=4,'core'=2] {'y_lo','x','y_hi','z'}, dimensions={0} | all-to-all | bytes 524288 | tf_op jit(solution)/shard_map/all_to_all | solution.py:437
  66.6 0.0 copy-done.5
  66.6 0.0 copy-done.8
  66.6 0.0 copy-done.9
  66.6 0.0 copy-done.3
  66.6 0.0 copy-start.2
  66.6 0.0 copy-start.4
  66.6 0.0 copy-start.6
  66.6 0.0 copy-start.7
  66.6 0.7 shard_map.187.mine
  67.4 4.0 %collective-permute-start.1 = (f32[512,128]{1,0:T(8,128)S(1)}, f32[512,128]{1,0:T(8,128)S(1)}, u32[]{:S(2)}, u32[]{:S(2)}) collective-permute-start(f32[512,128]{1,0:T(8,128)S(1)} %shard_map.187.mine), channel_id=1, source_target_pairs={{0,1},{1,0},{2,3},{3,2},{4,5},{5,4},{6,7},{7,6},{8,9},{9,8},{10,11... | collective-permute-start | bytes 786440 | tf_op jit(solution)/shard_map/ppermute | solution.py:472
  71.3 1.1 collective-permute-done.1.other
  72.5 0.0 copy-done.2
  72.5 0.0 copy-done.4
  72.5 0.0 copy-done.6
  72.5 0.0 copy-done.7
  72.5 1.5 %shard_map.188 = f32[512,128]{1,0:T(8,128)} custom-call(f32[8,128]{1,0:T(8,128)S(1)} %shard_map.184.info, f32[512,128]{1,0:T(8,128)S(1)} %shard_map.187.mine, f32[512,128]{1,0:T(8,128)S(1)} %collective-permute-done.1.other, bf16[2,512,256]{2,1,0:T(8,128)(2,1)S(1)} %copy-done.2, bf16[2,256,256]{2,1,0:T(8,128)(2,1)S(1)} %copy-done.4, ...), custom_call_target="tpu_custom_call" | custom-call | tf_op jit(solution)/shard_map/pallas_call | solution.py:66
  74.0 9.8 %all-to-all-start.2 = ((f32[256,2,128]{2,1,0:T(2,128)}), f32[256,2,128]{2,1,0:T(2,128)S(1)}, u32[]{:S(2)}, u32[]{:S(2)}) async-start(f32[256,2,128]{2,1,0:T(2,128)} %bitcast.15), calls=%async_computation.2 | async-start | bytes 524288 | tf_op jit(solution)/shard_map/all_to_all | solution.py:437
  83.9 7.6 %collective-permute-start.2 = (f32[56,128]{1,0:T(8,128)S(1)}, f32[56,128]{1,0:T(8,128)S(1)}, u32[]{:S(2)}, u32[]{:S(2)}) collective-permute-start(f32[56,128]{1,0:T(8,128)S(1)} %get-tuple-element.19.mine), channel_id=1, source_target_pairs={{0,480},{32,0},{64,32},{96,64},{128,96},{160,128},{192,160},{224,1... | collective-permute-start | bytes 86024 | tf_op jit(solution)/shard_map/ppermute | solution.py:441
  91.5 1.7 %collective-permute-done.2.parcel.below = f32[56,128]{1,0:T(8,128)S(1)} collective-permute-done((f32[56,128]{1,0:T(8,128)S(1)}, f32[56,128]{1,0:T(8,128)S(1)}, u32[]{:S(2)}, u32[]{:S(2)}) %collective-permute-start.2) | collective-permute-done | bytes 28704 | tf_op jit(solution)/shard_map/ppermute | solution.py:441
  93.2 0.2 shard_map.189.fields
  93.4 2.7 %all-to-all-done.2 = f32[256,2,128]{2,1,0:T(2,128)S(1)} async-done(((f32[256,2,128]{2,1,0:T(2,128)}), f32[256,2,128]{2,1,0:T(2,128)S(1)}, u32[]{:S(2)}, u32[]{:S(2)}) %all-to-all-start.2) | async-done | bytes 262176 | tf_op jit(solution)/shard_map/all_to_all | solution.py:437
  96.0 0.7 shard_map.190
  96.7 0.0 copy-start.13
  96.7 17.9 %all_to_all.22 = f32[544,1,128]{2,1,0:T(1,128)S(1)} all-to-all(f32[544,1,128]{2,1,0:T(1,128)S(1)} %bitcast.38), channel_id=1, replica_groups=mesh['z'=8,'y_hi'=2,'x'=4,'y_lo'=4,'core'=2] {'core','x','y_lo'}, dimensions={0} | all-to-all | bytes 557056 | tf_op jit(solution)/shard_map/all_to_all | solution.py:437
  114.6 0.0 copy-done.13
  114.6 1.0 shard_map.191
  (2 shorter events, 0.0 us)
Async XLA Ops:
  2.1 9.4 %copy-start.15 = (s32[1,256,128]{2,1,0:T(8,128)S(1)}, s32[1,256,128]{2,1,0:T(8,128)}, u32[]{:S(2)}) copy-start(s32[1,256,128]{2,1,0:T(8,128)} %param.17) | copy-start | bytes 393220
  2.1 18.0 %collective-permute-start = (f32[3,8,128]{2,1,0:T(8,128)S(1)}, f32[3,8,128]{2,1,0:T(8,128)S(1)}, u32[]{:S(2)}, u32[]{:S(2)}) collective-permute-start(f32[3,8,128]{2,1,0:T(8,128)S(1)} %select_select_fusion), channel_id=1, source_target_pairs={{0,32},{32,64},{64,96},{96,128},{128,160},{160,192},{192,224},{224... | collective-permute-start | bytes 36872 | tf_op jit(solution)/shard_map/ppermute | solution.py:441
  11.5 8.5 %copy-start = (f32[1,256,128]{2,1,0:T(8,128)S(1)}, f32[1,256,128]{2,1,0:T(8,128)}, u32[]{:S(2)}) copy-start(f32[1,256,128]{2,1,0:T(8,128)} %param.19) | copy-start | bytes 393220
  11.6 0.7 copy-start.14
  21.0 19.0 %copy-start.1 = (bf16[2,224,256]{2,1,0:T(8,128)(2,1)S(1)}, bf16[2,224,256]{2,1,0:T(8,128)(2,1)}, u32[]{:S(2)}) copy-start(bf16[2,224,256]{2,1,0:T(8,128)(2,1)} %constant.60.clone.every) | copy-start | bytes 688132
  21.0 19.0 %copy-start.10 = (bf16[2,128,128]{2,1,0:T(8,128)(2,1)S(1)}, bf16[2,128,128]{2,1,0:T(8,128)(2,1)}, u32[]{:S(2)}) copy-start(bf16[2,128,128]{2,1,0:T(8,128)(2,1)} %constant.63.clone.order) | copy-start | bytes 196612
  21.0 19.0 %copy-start.11 = (f32[32,128]{1,0:T(8,128)S(1)}, f32[32,128]{1,0:T(8,128)}, u32[]{:S(2)}) copy-start(f32[32,128]{1,0:T(8,128)} %constant.62.clone.twist_sin) | copy-start | bytes 49156
  21.0 19.0 %copy-start.12 = (f32[32,128]{1,0:T(8,128)S(1)}, f32[32,128]{1,0:T(8,128)}, u32[]{:S(2)}) copy-start(f32[32,128]{1,0:T(8,128)} %constant.61.clone.twist_cos) | copy-start | bytes 49156
  40.0 26.6 %copy-start.5 = (bf16[2,256,256]{2,1,0:T(8,128)(2,1)S(1)}, bf16[2,256,256]{2,1,0:T(8,128)(2,1)}, u32[]{:S(2)}) copy-start(bf16[2,256,256]{2,1,0:T(8,128)(2,1)} %constant.65.clone.second) | copy-start | bytes 786436
  40.0 26.6 %copy-start.8 = (f32[256,128]{1,0:T(8,128)S(1)}, f32[256,128]{1,0:T(8,128)}, u32[]{:S(2)}) copy-start(f32[256,128]{1,0:T(8,128)} %constant.67.clone.twist_sin) | copy-start | bytes 393220
  40.0 26.6 %copy-start.9 = (f32[256,128]{1,0:T(8,128)S(1)}, f32[256,128]{1,0:T(8,128)}, u32[]{:S(2)}) copy-start(f32[256,128]{1,0:T(8,128)} %constant.66.clone.twist_cos) | copy-start | bytes 393220
  41.4 25.2 %copy-start.3 = (bf16[2,512,256]{2,1,0:T(8,128)(2,1)S(1)}, bf16[2,512,256]{2,1,0:T(8,128)(2,1)}, u32[]{:S(2)}) copy-start(bf16[2,512,256]{2,1,0:T(8,128)(2,1)} %constant.68.clone.first) | copy-start | bytes 1572868
  66.6 5.9 %copy-start.2 = (bf16[2,512,256]{2,1,0:T(8,128)(2,1)S(1)}, bf16[2,512,256]{2,1,0:T(8,128)(2,1)}, u32[]{:S(2)}) copy-start(bf16[2,512,256]{2,1,0:T(8,128)(2,1)} %constant.72.clone.first) | copy-start | bytes 1572868
  66.6 5.9 %copy-start.4 = (bf16[2,256,256]{2,1,0:T(8,128)(2,1)S(1)}, bf16[2,256,256]{2,1,0:T(8,128)(2,1)}, u32[]{:S(2)}) copy-start(bf16[2,256,256]{2,1,0:T(8,128)(2,1)} %constant.69.clone.second) | copy-start | bytes 786436
  66.6 5.9 %copy-start.6 = (f32[256,128]{1,0:T(8,128)S(1)}, f32[256,128]{1,0:T(8,128)}, u32[]{:S(2)}) copy-start(f32[256,128]{1,0:T(8,128)} %constant.71.clone.twist_sin) | copy-start | bytes 393220
  66.6 5.9 %copy-start.7 = (f32[256,128]{1,0:T(8,128)S(1)}, f32[256,128]{1,0:T(8,128)}, u32[]{:S(2)}) copy-start(f32[256,128]{1,0:T(8,128)} %constant.70.clone.twist_cos) | copy-start | bytes 393220
  67.4 5.1 %collective-permute-start.1 = (f32[512,128]{1,0:T(8,128)S(1)}, f32[512,128]{1,0:T(8,128)S(1)}, u32[]{:S(2)}, u32[]{:S(2)}) collective-permute-start(f32[512,128]{1,0:T(8,128)S(1)} %shard_map.187.mine), channel_id=1, source_target_pairs={{0,1},{1,0},{2,3},{3,2},{4,5},{5,4},{6,7},{7,6},{8,9},{9,8},{10,11... | collective-permute-start | bytes 786440 | tf_op jit(solution)/shard_map/ppermute | solution.py:472
  74.0 22.0 %all-to-all-start.2 = ((f32[256,2,128]{2,1,0:T(2,128)}), f32[256,2,128]{2,1,0:T(2,128)S(1)}, u32[]{:S(2)}, u32[]{:S(2)}) async-start(f32[256,2,128]{2,1,0:T(2,128)} %bitcast.15), calls=%async_computation.2 | async-start | bytes 524288 | tf_op jit(solution)/shard_map/all_to_all | solution.py:437
  83.9 9.3 %collective-permute-start.2 = (f32[56,128]{1,0:T(8,128)S(1)}, f32[56,128]{1,0:T(8,128)S(1)}, u32[]{:S(2)}, u32[]{:S(2)}) collective-permute-start(f32[56,128]{1,0:T(8,128)S(1)} %get-tuple-element.19.mine), channel_id=1, source_target_pairs={{0,480},{32,0},{64,32},{96,64},{128,96},{160,128},{192,160},{224,1... | collective-permute-start | bytes 86024 | tf_op jit(solution)/shard_map/ppermute | solution.py:441
  96.7 17.9 %copy-start.13 = (bf16[128,128]{1,0:T(8,128)(2,1)S(1)}, bf16[128,128]{1,0:T(8,128)(2,1)}, u32[]{:S(2)}) copy-start(bf16[128,128]{1,0:T(8,128)(2,1)} %constant.64.clone.columns) | copy-start | bytes 98308

commit v8 on v7

--- a/solution.py
+++ b/solution.py
@@ -60,7 +60,7 @@
     )
 
 
-def call(kernel, outs, *args, smem=(), scratch=()):
+def call(kernel, outs, *args, smem=(), scratch=(), aliases=()):
     shapes = [jax.ShapeDtypeStruct(shape, jnp.float32) for shape in outs]
     spaces = [SMEM if i in smem else VMEM for i in range(len(args))]
     return pl.pallas_call(
@@ -69,6 +69,7 @@
         in_specs=spaces,
         out_specs=[VMEM] * len(outs),
         scratch_shapes=list(scratch),
+        input_output_aliases=dict(aliases),
         compiler_params=pltpu.CompilerParams(vmem_limit_bytes=32 * 1024 * 1024),
     )(*args)
 
@@ -197,34 +198,35 @@
 
 
 def shifted_rows(field):
-    return roll(field, SHIFT - EDGE, 0)[:TILE_ROWS]
+    return roll(field, SHIFT - EDGE, 0)[: field.shape[0] - EDGE]
 
 
 def row_walls(first, row):
     return first & (row == EDGE - 1), first & (row == EDGE)
 
 
-def polar_kernel(info, porous, phase, heat, above, out, fields):
-    talls = with_above(above, porous, phase, heat)
+def polar_blocks(info, talls, slabs, rows, out, fields):
     row = lax.broadcasted_iota(jnp.int32, talls[0].shape, 0)
     walls = row_walls(known(info, GX) == 0.0, row) + (None, None)
     phase_two, heat_two, along_rows, along_columns = stencil(*talls, ring_neighbours(walls))
-    fields[0] = shifted_rows(phase_two)
-    fields[1] = shifted_rows(heat_two)
+    fields[0, :rows] = shifted_rows(phase_two)[:rows]
+    fields[1, :rows] = shifted_rows(heat_two)[:rows]
     contrast = conductivity_contrast(talls[0], phase_two)
     polars = (
         shifted_rows(contrast * (known(info, SLOPE_X) + gradient_gain * along_rows)),
         shifted_rows(contrast * (known(info, SLOPE_Y) + gradient_gain * along_columns)),
     )
-    spare = jnp.zeros((WIDE - TALL, TILE_COLS), jnp.float32)
-    sublane = lax.broadcasted_iota(jnp.int32, (EDGE, WIDE), 0)
+    tall = talls[0].shape[0]
+    wide = WIDE if tall == TALL else TILE_COLS
+    spare = jnp.zeros((wide - tall, TILE_COLS), jnp.float32)
+    sublane = lax.broadcasted_iota(jnp.int32, (EDGE, wide), 0)
     lane = lax.broadcasted_iota(jnp.int32, (EDGE, TILE_COLS), 1)
     low = lax.broadcasted_iota(jnp.int32, (EDGE, TILE_COLS), 0) < 4
     edges = []
     for tall in talls:
         flipped = jnp.concatenate([tall, spare], axis=0).T
         edges.append(jnp.where(sublane < 4, flipped[:EDGE], flipped[TILE_COLS - EDGE :]))
-    for x in range(TILE_ROWS // SLAB):
+    for x in slabs:
         first = EDGE - 2 * SHIFT + SLAB * x
         windows = [
             roll(edge, f * SPAN - first, 1)[:, :TILE_COLS] for f, edge in enumerate(edges)
@@ -240,6 +242,18 @@
         out[start : start + SLAB, :] = polars[0][rows]
         rest = roll(jnp.concatenate([both, polars[1][rows]], axis=0), -4, 0)
         out[start + SLAB : start + 2 * BLOCK, :] = rest
+
+
+def polar_kernel(info, porous, phase, heat, out, fields):
+    nothing = jnp.zeros((3, EDGE, TILE_COLS), jnp.float32)
+    talls = with_above(nothing, porous, phase, heat)
+    polar_blocks(info, talls, range(1, TILE_ROWS // SLAB), TILE_ROWS, out, fields)
+
+
+def first_slab_kernel(info, porous, phase, heat, above, blocks, rows, out, fields):
+    del blocks, rows
+    talls = [tall[: 4 * EDGE] for tall in with_above(above, porous, phase, heat)]
+    polar_blocks(info, talls, range(1), EDGE, out, fields)
 
 
 def tail_kernel(info, porous, phase, heat, fields, parcel, out):
@@ -459,8 +473,11 @@
     phase = porous * wetted[0].astype(jnp.float32)
     heat = heat[0]
     (info,) = call(prepare_kernel, [(8, 128)], place.astype(jnp.int32), slope, smem=(0, 1))
+    shapes = [(OUTER * BLOCK, 128), (2,) + tile]
+    polar, fields = call(polar_kernel, shapes, info, porous, phase, heat)
     polar, fields = call(
-        polar_kernel, [(OUTER * BLOCK, 128), (2,) + tile], info, porous, phase, heat, above
+        first_slab_kernel, shapes, info, porous, phase, heat, above, polar, fields,
+        aliases=((5, 0), (6, 1)),
     )
     slab = exchange(polar, GY_AXES, 4).reshape(-1, 128)
     spec, parcel = call(

time: 116 us -> 116 us (level)
    pallas_call x8 -> x9, Pallas kernels: 6.95 us -> 7.14 us  [call(): pl.pallas_call(kernel, out_shape=shapes, in_specs=spaces, out_specs=[VMEM...]
where the time goes in v8:
time: 116 us; the launch traced here: 115 us
  blocking collectives  62 us (53%)
  starting transfers between devices  29.8 us (26%)
  waiting for transfers between devices  11.9 us (10%)
  Pallas kernels  7.14 us (6%)
  other arithmetic  2.48 us (2%)
    all_to_all x3, blocking collectives, exchange(): return lax.all_to_all(blocks, axes, split_axis=0, concat_axis=0, tiled=True)  62 us
    ppermute x2, starting transfers between devices, shift(): lax.ppermute(block, axes, [(i, (i + step) % count) for i in range(count)])  16 us
    all_to_all x1, starting transfers between devices, exchange(): return lax.all_to_all(blocks, axes, split_axis=0, concat_axis=0, tiled=True)  9.83 us
    ppermute x2, waiting for transfers between devices, shift(): lax.ppermute(block, axes, [(i, (i + step) % count) for i in range(count)])  8.1 us
    pallas_call x9, Pallas kernels, call(): pl.pallas_call(kernel, out_shape=shapes, in_specs=spaces, out_specs=[VMEM...  7.14 us
    ppermute x1, starting transfers between devices, body(): other = lax.ppermute(mine, 'core', [(0, 1), (1, 0)])  3.96 us
    all_to_all x1, waiting for transfers between devices, exchange(): return lax.all_to_all(blocks, axes, split_axis=0, concat_axis=0, tiled=True)  2.65 us
  transfers between devices with their start and end apart: 4, of which 4 were waited for; matrix products, arithmetic and copies ran while one was open for 1% of the time, Pallas kernels for 1%

profile of v8, /device:TPU:1, one launch (start us, length us, event | category | flops | bytes accessed | tf_op | source)
XLA Modules:
  0.0 115.0 jit_solution(13281205498507688204)
XLA Ops:
  0.6 0.7 negate_bitcast_fusion
  1.3 0.7 convert_bitcast_fusion.1
  2.0 0.1 select_select_fusion
  2.1 0.0 copy-start.15
  2.1 8.4 %collective-permute-start = (f32[3,8,128]{2,1,0:T(8,128)S(1)}, f32[3,8,128]{2,1,0:T(8,128)S(1)}, u32[]{:S(2)}, u32[]{:S(2)}) collective-permute-start(f32[3,8,128]{2,1,0:T(8,128)S(1)} %select_select_fusion), channel_id=1, source_target_pairs={{0,32},{32,64},{64,96},{96,128},{128,160},{160,192},{192,224},{224... | collective-permute-start | bytes 36872 | tf_op jit(solution)/shard_map/ppermute | solution.py:455
  10.5 1.0 bitcast_multiply_fusion.phase
  11.5 0.0 copy-done.15
  11.5 0.0 copy-start
  11.6 0.0 copy-start.14
  11.6 0.1 stack.23.place
  11.7 0.6 copy-done.14
  12.3 0.6 shard_map.184.info
  12.8 0.0 copy-done
  12.8 0.8 shard_map.185
  13.7 6.4 %collective-permute-done.above = f32[3,8,128]{2,1,0:T(8,128)S(1)} collective-permute-done((f32[3,8,128]{2,1,0:T(8,128)S(1)}, f32[3,8,128]{2,1,0:T(8,128)S(1)}, u32[]{:S(2)}, u32[]{:S(2)}) %collective-permute-start) | collective-permute-done | bytes 12320 | tf_op jit(solution)/shard_map/ppermute | solution.py:455
  20.1 0.3 shard_map.186
  20.3 0.0 copy-start.1
  20.4 0.0 copy-start.10
  20.4 0.0 copy-start.11
  20.4 0.0 copy-start.12
  20.4 18.9 %all_to_all.20 = f32[160,4,128]{2,1,0:T(4,128)S(1)} all-to-all(f32[160,4,128]{2,1,0:T(4,128)S(1)} %bitcast.37), channel_id=1, replica_groups=mesh['z'=8,'y_hi'=2,'x'=4,'y_lo'=4,'core'=2] {'x','y_lo','core'}, dimensions={0} | all-to-all | bytes 655360 | tf_op jit(solution)/shard_map/all_to_all | solution.py:451
  39.3 0.0 copy-done.1
  39.3 0.0 copy-done.10
  39.3 0.0 copy-done.11
  39.3 0.0 copy-done.12
  39.3 0.0 copy-start.5
  39.4 0.0 copy-start.8
  39.4 0.0 copy-start.9
  39.4 1.4 %shard_map.187 = (f32[512,128]{1,0:T(8,128)S(1)}, f32[56,128]{1,0:T(8,128)S(1)}) custom-call(f32[8,128]{1,0:T(8,128)S(1)} %shard_map.184.info, f32[640,128]{1,0:T(8,128)S(1)} %bitcast.38, f32[256,128]{1,0:T(8,128)S(1)} %convert_bitcast_fusion.porous, f32[256,128]{1,0:T(8,128)S(1)} %bitcast_multiply_fusion.phase, f32[256,128]{1,0:T(8,128)S(1)} %bitcast.35, ...), custom_call_target="tpu_custom_call" | custom-call | tf_op jit(solution)/shard_map/pallas_call | solution.py:66
  40.7 0.0 copy-start.3
  40.8 25.2 %all_to_all.21 = f32[256,2,128]{2,1,0:T(2,128)S(1)} all-to-all(f32[256,2,128]{2,1,0:T(2,128)S(1)} %bitcast.43), channel_id=1, replica_groups=mesh['z'=8,'y_hi'=2,'x'=4,'y_lo'=4,'core'=2] {'y_lo','x','y_hi','z'}, dimensions={0} | all-to-all | bytes 524288 | tf_op jit(solution)/shard_map/all_to_all | solution.py:451
  65.9 0.0 copy-done.5
  65.9 0.0 copy-done.8
  65.9 0.0 copy-done.9
  65.9 0.0 copy-done.3
  66.0 0.0 copy-start.2
  66.0 0.0 copy-start.4
  66.0 0.0 copy-start.6
  66.0 0.0 copy-start.7
  66.0 0.7 shard_map.188.mine
  66.7 4.0 %collective-permute-start.1 = (f32[512,128]{1,0:T(8,128)S(1)}, f32[512,128]{1,0:T(8,128)S(1)}, u32[]{:S(2)}, u32[]{:S(2)}) collective-permute-start(f32[512,128]{1,0:T(8,128)S(1)} %shard_map.188.mine), channel_id=1, source_target_pairs={{0,1},{1,0},{2,3},{3,2},{4,5},{5,4},{6,7},{7,6},{8,9},{9,8},{10,11... | collective-permute-start | bytes 786440 | tf_op jit(solution)/shard_map/ppermute | solution.py:489
  70.7 1.1 collective-permute-done.1.other
  71.8 0.0 copy-done.2
  71.8 0.0 copy-done.4
  71.8 0.0 copy-done.6
  71.9 0.0 copy-done.7
  71.9 1.5 %shard_map.189 = f32[512,128]{1,0:T(8,128)} custom-call(f32[8,128]{1,0:T(8,128)S(1)} %shard_map.184.info, f32[512,128]{1,0:T(8,128)S(1)} %shard_map.188.mine, f32[512,128]{1,0:T(8,128)S(1)} %collective-permute-done.1.other, bf16[2,512,256]{2,1,0:T(8,128)(2,1)S(1)} %copy-done.2, bf16[2,256,256]{2,1,0:T(8,128)(2,1)S(1)} %copy-done.4, ...), custom_call_target="tpu_custom_call" | custom-call | tf_op jit(solution)/shard_map/pallas_call | solution.py:66
  73.4 9.8 %all-to-all-start.2 = ((f32[256,2,128]{2,1,0:T(2,128)}), f32[256,2,128]{2,1,0:T(2,128)S(1)}, u32[]{:S(2)}, u32[]{:S(2)}) async-start(f32[256,2,128]{2,1,0:T(2,128)} %bitcast.15), calls=%async_computation.2 | async-start | bytes 524288 | tf_op jit(solution)/shard_map/all_to_all | solution.py:451
  83.2 7.6 %collective-permute-start.2 = (f32[56,128]{1,0:T(8,128)S(1)}, f32[56,128]{1,0:T(8,128)S(1)}, u32[]{:S(2)}, u32[]{:S(2)}) collective-permute-start(f32[56,128]{1,0:T(8,128)S(1)} %get-tuple-element.23.mine), channel_id=1, source_target_pairs={{0,480},{32,0},{64,32},{96,64},{128,96},{160,128},{192,160},{224,1... | collective-permute-start | bytes 86024 | tf_op jit(solution)/shard_map/ppermute | solution.py:455
  90.9 1.7 %collective-permute-done.2.parcel.below = f32[56,128]{1,0:T(8,128)S(1)} collective-permute-done((f32[56,128]{1,0:T(8,128)S(1)}, f32[56,128]{1,0:T(8,128)S(1)}, u32[]{:S(2)}, u32[]{:S(2)}) %collective-permute-start.2) | collective-permute-done | bytes 28704 | tf_op jit(solution)/shard_map/ppermute | solution.py:455
  92.6 0.2 shard_map.190.fields
  92.7 2.7 %all-to-all-done.2 = f32[256,2,128]{2,1,0:T(2,128)S(1)} async-done(((f32[256,2,128]{2,1,0:T(2,128)}), f32[256,2,128]{2,1,0:T(2,128)S(1)}, u32[]{:S(2)}, u32[]{:S(2)}) %all-to-all-start.2) | async-done | bytes 262176 | tf_op jit(solution)/shard_map/all_to_all | solution.py:451
  95.4 0.7 shard_map.191
  96.0 0.0 copy-start.13
  96.0 17.9 %all_to_all.22 = f32[544,1,128]{2,1,0:T(1,128)S(1)} all-to-all(f32[544,1,128]{2,1,0:T(1,128)S(1)} %bitcast.40), channel_id=1, replica_groups=mesh['z'=8,'y_hi'=2,'x'=4,'y_lo'=4,'core'=2] {'core','x','y_lo'}, dimensions={0} | all-to-all | bytes 557056 | tf_op jit(solution)/shard_map/all_to_all | solution.py:451
  113.9 0.0 copy-done.13
  113.9 1.0 shard_map.192
  (2 shorter events, 0.0 us)
Async XLA Ops:
  2.1 9.4 %copy-start.15 = (s32[1,256,128]{2,1,0:T(8,128)S(1)}, s32[1,256,128]{2,1,0:T(8,128)}, u32[]{:S(2)}) copy-start(s32[1,256,128]{2,1,0:T(8,128)} %param.17) | copy-start | bytes 393220
  2.1 18.0 %collective-permute-start = (f32[3,8,128]{2,1,0:T(8,128)S(1)}, f32[3,8,128]{2,1,0:T(8,128)S(1)}, u32[]{:S(2)}, u32[]{:S(2)}) collective-permute-start(f32[3,8,128]{2,1,0:T(8,128)S(1)} %select_select_fusion), channel_id=1, source_target_pairs={{0,32},{32,64},{64,96},{96,128},{128,160},{160,192},{192,224},{224... | collective-permute-start | bytes 36872 | tf_op jit(solution)/shard_map/ppermute | solution.py:455
  11.5 1.3 %copy-start = (f32[1,256,128]{2,1,0:T(8,128)S(1)}, f32[1,256,128]{2,1,0:T(8,128)}, u32[]{:S(2)}) copy-start(f32[1,256,128]{2,1,0:T(8,128)} %param.19) | copy-start | bytes 393220
  11.6 0.7 copy-start.14
  20.3 19.0 %copy-start.1 = (bf16[2,224,256]{2,1,0:T(8,128)(2,1)S(1)}, bf16[2,224,256]{2,1,0:T(8,128)(2,1)}, u32[]{:S(2)}) copy-start(bf16[2,224,256]{2,1,0:T(8,128)(2,1)} %constant.60.clone.every) | copy-start | bytes 688132
  20.4 19.0 %copy-start.10 = (bf16[2,128,128]{2,1,0:T(8,128)(2,1)S(1)}, bf16[2,128,128]{2,1,0:T(8,128)(2,1)}, u32[]{:S(2)}) copy-start(bf16[2,128,128]{2,1,0:T(8,128)(2,1)} %constant.63.clone.order) | copy-start | bytes 196612
  20.4 19.0 %copy-start.11 = (f32[32,128]{1,0:T(8,128)S(1)}, f32[32,128]{1,0:T(8,128)}, u32[]{:S(2)}) copy-start(f32[32,128]{1,0:T(8,128)} %constant.62.clone.twist_sin) | copy-start | bytes 49156
  20.4 19.0 %copy-start.12 = (f32[32,128]{1,0:T(8,128)S(1)}, f32[32,128]{1,0:T(8,128)}, u32[]{:S(2)}) copy-start(f32[32,128]{1,0:T(8,128)} %constant.61.clone.twist_cos) | copy-start | bytes 49156
  39.3 26.6 %copy-start.5 = (bf16[2,256,256]{2,1,0:T(8,128)(2,1)S(1)}, bf16[2,256,256]{2,1,0:T(8,128)(2,1)}, u32[]{:S(2)}) copy-start(bf16[2,256,256]{2,1,0:T(8,128)(2,1)} %constant.65.clone.second) | copy-start | bytes 786436
  39.4 26.6 %copy-start.8 = (f32[256,128]{1,0:T(8,128)S(1)}, f32[256,128]{1,0:T(8,128)}, u32[]{:S(2)}) copy-start(f32[256,128]{1,0:T(8,128)} %constant.67.clone.twist_sin) | copy-start | bytes 393220
  39.4 26.6 %copy-start.9 = (f32[256,128]{1,0:T(8,128)S(1)}, f32[256,128]{1,0:T(8,128)}, u32[]{:S(2)}) copy-start(f32[256,128]{1,0:T(8,128)} %constant.66.clone.twist_cos) | copy-start | bytes 393220
  40.7 25.2 %copy-start.3 = (bf16[2,512,256]{2,1,0:T(8,128)(2,1)S(1)}, bf16[2,512,256]{2,1,0:T(8,128)(2,1)}, u32[]{:S(2)}) copy-start(bf16[2,512,256]{2,1,0:T(8,128)(2,1)} %constant.68.clone.first) | copy-start | bytes 1572868
  66.0 5.9 %copy-start.2 = (bf16[2,512,256]{2,1,0:T(8,128)(2,1)S(1)}, bf16[2,512,256]{2,1,0:T(8,128)(2,1)}, u32[]{:S(2)}) copy-start(bf16[2,512,256]{2,1,0:T(8,128)(2,1)} %constant.72.clone.first) | copy-start | bytes 1572868
  66.0 5.9 %copy-start.4 = (bf16[2,256,256]{2,1,0:T(8,128)(2,1)S(1)}, bf16[2,256,256]{2,1,0:T(8,128)(2,1)}, u32[]{:S(2)}) copy-start(bf16[2,256,256]{2,1,0:T(8,128)(2,1)} %constant.69.clone.second) | copy-start | bytes 786436
  66.0 5.9 %copy-start.6 = (f32[256,128]{1,0:T(8,128)S(1)}, f32[256,128]{1,0:T(8,128)}, u32[]{:S(2)}) copy-start(f32[256,128]{1,0:T(8,128)} %constant.71.clone.twist_sin) | copy-start | bytes 393220
  66.0 5.9 %copy-start.7 = (f32[256,128]{1,0:T(8,128)S(1)}, f32[256,128]{1,0:T(8,128)}, u32[]{:S(2)}) copy-start(f32[256,128]{1,0:T(8,128)} %constant.70.clone.twist_cos) | copy-start | bytes 393220
  66.7 5.1 %collective-permute-start.1 = (f32[512,128]{1,0:T(8,128)S(1)}, f32[512,128]{1,0:T(8,128)S(1)}, u32[]{:S(2)}, u32[]{:S(2)}) collective-permute-start(f32[512,128]{1,0:T(8,128)S(1)} %shard_map.188.mine), channel_id=1, source_target_pairs={{0,1},{1,0},{2,3},{3,2},{4,5},{5,4},{6,7},{7,6},{8,9},{9,8},{10,11... | collective-permute-start | bytes 786440 | tf_op jit(solution)/shard_map/ppermute | solution.py:489
  73.4 22.0 %all-to-all-start.2 = ((f32[256,2,128]{2,1,0:T(2,128)}), f32[256,2,128]{2,1,0:T(2,128)S(1)}, u32[]{:S(2)}, u32[]{:S(2)}) async-start(f32[256,2,128]{2,1,0:T(2,128)} %bitcast.15), calls=%async_computation.2 | async-start | bytes 524288 | tf_op jit(solution)/shard_map/all_to_all | solution.py:451
  83.2 9.3 %collective-permute-start.2 = (f32[56,128]{1,0:T(8,128)S(1)}, f32[56,128]{1,0:T(8,128)S(1)}, u32[]{:S(2)}, u32[]{:S(2)}) collective-permute-start(f32[56,128]{1,0:T(8,128)S(1)} %get-tuple-element.23.mine), channel_id=1, source_target_pairs={{0,480},{32,0},{64,32},{96,64},{128,96},{160,128},{192,160},{224,1... | collective-permute-start | bytes 86024 | tf_op jit(solution)/shard_map/ppermute | solution.py:455
  96.0 17.9 %copy-start.13 = (bf16[128,128]{1,0:T(8,128)(2,1)S(1)}, bf16[128,128]{1,0:T(8,128)(2,1)}, u32[]{:S(2)}) copy-start(bf16[128,128]{1,0:T(8,128)(2,1)} %constant.64.clone.columns) | copy-start | bytes 98308

commit v9 on v8

--- a/solution.py
+++ b/solution.py
@@ -60,7 +60,7 @@
     )
 
 
-def call(kernel, outs, *args, smem=(), scratch=(), aliases=()):
+def call(kernel, outs, *args, smem=(), scratch=()):
     shapes = [jax.ShapeDtypeStruct(shape, jnp.float32) for shape in outs]
     spaces = [SMEM if i in smem else VMEM for i in range(len(args))]
     return pl.pallas_call(
@@ -69,7 +69,6 @@
         in_specs=spaces,
         out_specs=[VMEM] * len(outs),
         scratch_shapes=list(scratch),
-        input_output_aliases=dict(aliases),
         compiler_params=pltpu.CompilerParams(vmem_limit_bytes=32 * 1024 * 1024),
     )(*args)
 
@@ -251,7 +250,9 @@
 
 
 def first_slab_kernel(info, porous, phase, heat, above, blocks, rows, out, fields):
-    del blocks, rows
+    done = 2 * BLOCK
+    out[done:, :] = blocks[done:, :]
+    fields[:, EDGE:] = rows[:, EDGE:]
     talls = [tall[: 4 * EDGE] for tall in with_above(above, porous, phase, heat)]
     polar_blocks(info, talls, range(1), EDGE, out, fields)
 
@@ -476,8 +477,7 @@
     shapes = [(OUTER * BLOCK, 128), (2,) + tile]
     polar, fields = call(polar_kernel, shapes, info, porous, phase, heat)
     polar, fields = call(
-        first_slab_kernel, shapes, info, porous, phase, heat, above, polar, fields,
-        aliases=((5, 0), (6, 1)),
+        first_slab_kernel, shapes, info, porous, phase, heat, above, polar, fields
     )
     slab = exchange(polar, GY_AXES, 4).reshape(-1, 128)
     spec, parcel = call(

time: 116 us -> 116 us (level)
  no operation moved by 1% of the time
where the time goes in v9:
time: 116 us; the launch traced here: 115 us
  blocking collectives  62 us (53%)
  starting transfers between devices  29.8 us (26%)
  waiting for transfers between devices  11.9 us (10%)
  Pallas kernels  7.14 us (6%)
  other arithmetic  2.48 us (2%)
    all_to_all x3, blocking collectives, exchange(): return lax.all_to_all(blocks, axes, split_axis=0, concat_axis=0, tiled=True)  62 us
    ppermute x2, starting transfers between devices, shift(): lax.ppermute(block, axes, [(i, (i + step) % count) for i in range(count)])  16 us
    all_to_all x1, starting transfers between devices, exchange(): return lax.all_to_all(blocks, axes, split_axis=0, concat_axis=0, tiled=True)  9.83 us
    ppermute x2, waiting for transfers between devices, shift(): lax.ppermute(block, axes, [(i, (i + step) % count) for i in range(count)])  8.1 us
    pallas_call x9, Pallas kernels, call(): pl.pallas_call(kernel, out_shape=shapes, in_specs=spaces, out_specs=[VMEM...  7.14 us
    ppermute x1, starting transfers between devices, body(): other = lax.ppermute(mine, 'core', [(0, 1), (1, 0)])  3.95 us
    all_to_all x1, waiting for transfers between devices, exchange(): return lax.all_to_all(blocks, axes, split_axis=0, concat_axis=0, tiled=True)  2.65 us
  transfers between devices with their start and end apart: 4, of which 4 were waited for; matrix products, arithmetic and copies ran while one was open for 1% of the time, Pallas kernels for 1%

profile of v9, /device:TPU:1, one launch (start us, length us, event | category | flops | bytes accessed | tf_op | source)
XLA Modules:
  0.0 115.0 jit_solution(872418222319787966)
XLA Ops:
  0.6 0.7 negate_bitcast_fusion
  1.3 0.7 convert_bitcast_fusion.1
  2.0 0.1 select_select_fusion
  2.1 0.0 copy-start.15
  2.1 8.4 %collective-permute-start = (f32[3,8,128]{2,1,0:T(8,128)S(1)}, f32[3,8,128]{2,1,0:T(8,128)S(1)}, u32[]{:S(2)}, u32[]{:S(2)}) collective-permute-start(f32[3,8,128]{2,1,0:T(8,128)S(1)} %select_select_fusion), channel_id=1, source_target_pairs={{0,32},{32,64},{64,96},{96,128},{128,160},{160,192},{192,224},{224... | collective-permute-start | bytes 36872 | tf_op jit(solution)/shard_map/ppermute | solution.py:456
  10.5 1.0 bitcast_multiply_fusion.phase
  11.5 0.0 copy-done.15
  11.5 0.0 copy-start
  11.6 0.0 copy-start.14
  11.6 0.1 stack.23.place
  11.7 0.6 copy-done.14
  12.3 0.6 shard_map.184.info
  12.8 0.0 copy-done
  12.8 0.8 shard_map.185
  13.7 6.4 %collective-permute-done.above = f32[3,8,128]{2,1,0:T(8,128)S(1)} collective-permute-done((f32[3,8,128]{2,1,0:T(8,128)S(1)}, f32[3,8,128]{2,1,0:T(8,128)S(1)}, u32[]{:S(2)}, u32[]{:S(2)}) %collective-permute-start) | collective-permute-done | bytes 12320 | tf_op jit(solution)/shard_map/ppermute | solution.py:456
  20.1 0.3 shard_map.186
  20.3 0.0 copy-start.1
  20.4 0.0 copy-start.10
  20.4 0.0 copy-start.11
  20.4 0.0 copy-start.12
  20.4 18.9 %all_to_all.20 = f32[160,4,128]{2,1,0:T(4,128)S(1)} all-to-all(f32[160,4,128]{2,1,0:T(4,128)S(1)} %bitcast.42), channel_id=1, replica_groups=mesh['z'=8,'y_hi'=2,'x'=4,'y_lo'=4,'core'=2] {'x','y_lo','core'}, dimensions={0} | all-to-all | bytes 655360 | tf_op jit(solution)/shard_map/all_to_all | solution.py:452
  39.3 0.0 copy-done.1
  39.3 0.0 copy-done.10
  39.3 0.0 copy-done.11
  39.3 0.0 copy-done.12
  39.3 0.0 copy-start.5
  39.4 0.0 copy-start.8
  39.4 0.0 copy-start.9
  39.4 1.4 %shard_map.187 = (f32[512,128]{1,0:T(8,128)S(1)}, f32[56,128]{1,0:T(8,128)S(1)}) custom-call(f32[8,128]{1,0:T(8,128)S(1)} %shard_map.184.info, f32[640,128]{1,0:T(8,128)S(1)} %bitcast.37, f32[256,128]{1,0:T(8,128)S(1)} %convert_bitcast_fusion.porous, f32[256,128]{1,0:T(8,128)S(1)} %bitcast_multiply_fusion.phase, f32[256,128]{1,0:T(8,128)S(1)} %bitcast.35, ...), custom_call_target="tpu_custom_call" | custom-call | tf_op jit(solution)/shard_map/pallas_call | solution.py:66
  40.7 0.0 copy-start.3
  40.8 25.2 %all_to_all.21 = f32[256,2,128]{2,1,0:T(2,128)S(1)} all-to-all(f32[256,2,128]{2,1,0:T(2,128)S(1)} %bitcast.43), channel_id=1, replica_groups=mesh['z'=8,'y_hi'=2,'x'=4,'y_lo'=4,'core'=2] {'y_lo','x','y_hi','z'}, dimensions={0} | all-to-all | bytes 524288 | tf_op jit(solution)/shard_map/all_to_all | solution.py:452
  65.9 0.0 copy-done.5
  65.9 0.0 copy-done.8
  65.9 0.0 copy-done.9
  65.9 0.0 copy-done.3
  66.0 0.0 copy-start.2
  66.0 0.0 copy-start.4
  66.0 0.0 copy-start.6
  66.0 0.0 copy-start.7
  66.0 0.7 shard_map.188.mine
  66.7 4.0 %collective-permute-start.1 = (f32[512,128]{1,0:T(8,128)S(1)}, f32[512,128]{1,0:T(8,128)S(1)}, u32[]{:S(2)}, u32[]{:S(2)}) collective-permute-start(f32[512,128]{1,0:T(8,128)S(1)} %shard_map.188.mine), channel_id=1, source_target_pairs={{0,1},{1,0},{2,3},{3,2},{4,5},{5,4},{6,7},{7,6},{8,9},{9,8},{10,11... | collective-permute-start | bytes 786440 | tf_op jit(solution)/shard_map/ppermute | solution.py:489
  70.7 1.1 collective-permute-done.1.other
  71.8 0.0 copy-done.2
  71.8 0.0 copy-done.4
  71.8 0.0 copy-done.6
  71.9 0.0 copy-done.7
  71.9 1.5 %shard_map.189 = f32[512,128]{1,0:T(8,128)} custom-call(f32[8,128]{1,0:T(8,128)S(1)} %shard_map.184.info, f32[512,128]{1,0:T(8,128)S(1)} %shard_map.188.mine, f32[512,128]{1,0:T(8,128)S(1)} %collective-permute-done.1.other, bf16[2,512,256]{2,1,0:T(8,128)(2,1)S(1)} %copy-done.2, bf16[2,256,256]{2,1,0:T(8,128)(2,1)S(1)} %copy-done.4, ...), custom_call_target="tpu_custom_call" | custom-call | tf_op jit(solution)/shard_map/pallas_call | solution.py:66
  73.4 9.8 %all-to-all-start.2 = ((f32[256,2,128]{2,1,0:T(2,128)}), f32[256,2,128]{2,1,0:T(2,128)S(1)}, u32[]{:S(2)}, u32[]{:S(2)}) async-start(f32[256,2,128]{2,1,0:T(2,128)} %bitcast.15), calls=%async_computation.2 | async-start | bytes 524288 | tf_op jit(solution)/shard_map/all_to_all | solution.py:452
  83.2 7.6 %collective-permute-start.2 = (f32[56,128]{1,0:T(8,128)S(1)}, f32[56,128]{1,0:T(8,128)S(1)}, u32[]{:S(2)}, u32[]{:S(2)}) collective-permute-start(f32[56,128]{1,0:T(8,128)S(1)} %get-tuple-element.23.mine), channel_id=1, source_target_pairs={{0,480},{32,0},{64,32},{96,64},{128,96},{160,128},{192,160},{224,1... | collective-permute-start | bytes 86024 | tf_op jit(solution)/shard_map/ppermute | solution.py:456
  90.9 1.7 %collective-permute-done.2.parcel.below = f32[56,128]{1,0:T(8,128)S(1)} collective-permute-done((f32[56,128]{1,0:T(8,128)S(1)}, f32[56,128]{1,0:T(8,128)S(1)}, u32[]{:S(2)}, u32[]{:S(2)}) %collective-permute-start.2) | collective-permute-done | bytes 28704 | tf_op jit(solution)/shard_map/ppermute | solution.py:456
  92.6 0.2 shard_map.190.fields
  92.7 2.7 %all-to-all-done.2 = f32[256,2,128]{2,1,0:T(2,128)S(1)} async-done(((f32[256,2,128]{2,1,0:T(2,128)}), f32[256,2,128]{2,1,0:T(2,128)S(1)}, u32[]{:S(2)}, u32[]{:S(2)}) %all-to-all-start.2) | async-done | bytes 262176 | tf_op jit(solution)/shard_map/all_to_all | solution.py:452
  95.4 0.7 shard_map.191
  96.0 0.0 copy-start.13
  96.0 17.9 %all_to_all.22 = f32[544,1,128]{2,1,0:T(1,128)S(1)} all-to-all(f32[544,1,128]{2,1,0:T(1,128)S(1)} %bitcast.39), channel_id=1, replica_groups=mesh['z'=8,'y_hi'=2,'x'=4,'y_lo'=4,'core'=2] {'core','x','y_lo'}, dimensions={0} | all-to-all | bytes 557056 | tf_op jit(solution)/shard_map/all_to_all | solution.py:452
  113.9 0.0 copy-done.13
  113.9 1.0 shard_map.192
  (2 shorter events, 0.0 us)
Async XLA Ops:
  2.1 9.4 %copy-start.15 = (s32[1,256,128]{2,1,0:T(8,128)S(1)}, s32[1,256,128]{2,1,0:T(8,128)}, u32[]{:S(2)}) copy-start(s32[1,256,128]{2,1,0:T(8,128)} %param.17) | copy-start | bytes 393220
  2.1 18.0 %collective-permute-start = (f32[3,8,128]{2,1,0:T(8,128)S(1)}, f32[3,8,128]{2,1,0:T(8,128)S(1)}, u32[]{:S(2)}, u32[]{:S(2)}) collective-permute-start(f32[3,8,128]{2,1,0:T(8,128)S(1)} %select_select_fusion), channel_id=1, source_target_pairs={{0,32},{32,64},{64,96},{96,128},{128,160},{160,192},{192,224},{224... | collective-permute-start | bytes 36872 | tf_op jit(solution)/shard_map/ppermute | solution.py:456
  11.5 1.3 %copy-start = (f32[1,256,128]{2,1,0:T(8,128)S(1)}, f32[1,256,128]{2,1,0:T(8,128)}, u32[]{:S(2)}) copy-start(f32[1,256,128]{2,1,0:T(8,128)} %param.19) | copy-start | bytes 393220
  11.6 0.7 copy-start.14
  20.3 19.0 %copy-start.1 = (bf16[2,224,256]{2,1,0:T(8,128)(2,1)S(1)}, bf16[2,224,256]{2,1,0:T(8,128)(2,1)}, u32[]{:S(2)}) copy-start(bf16[2,224,256]{2,1,0:T(8,128)(2,1)} %constant.60.clone.every) | copy-start | bytes 688132
  20.4 19.0 %copy-start.10 = (bf16[2,128,128]{2,1,0:T(8,128)(2,1)S(1)}, bf16[2,128,128]{2,1,0:T(8,128)(2,1)}, u32[]{:S(2)}) copy-start(bf16[2,128,128]{2,1,0:T(8,128)(2,1)} %constant.63.clone.order) | copy-start | bytes 196612
  20.4 19.0 %copy-start.11 = (f32[32,128]{1,0:T(8,128)S(1)}, f32[32,128]{1,0:T(8,128)}, u32[]{:S(2)}) copy-start(f32[32,128]{1,0:T(8,128)} %constant.62.clone.twist_sin) | copy-start | bytes 49156
  20.4 19.0 %copy-start.12 = (f32[32,128]{1,0:T(8,128)S(1)}, f32[32,128]{1,0:T(8,128)}, u32[]{:S(2)}) copy-start(f32[32,128]{1,0:T(8,128)} %constant.61.clone.twist_cos) | copy-start | bytes 49156
  39.3 26.6 %copy-start.5 = (bf16[2,256,256]{2,1,0:T(8,128)(2,1)S(1)}, bf16[2,256,256]{2,1,0:T(8,128)(2,1)}, u32[]{:S(2)}) copy-start(bf16[2,256,256]{2,1,0:T(8,128)(2,1)} %constant.65.clone.second) | copy-start | bytes 786436
  39.4 26.6 %copy-start.8 = (f32[256,128]{1,0:T(8,128)S(1)}, f32[256,128]{1,0:T(8,128)}, u32[]{:S(2)}) copy-start(f32[256,128]{1,0:T(8,128)} %constant.67.clone.twist_sin) | copy-start | bytes 393220
  39.4 26.6 %copy-start.9 = (f32[256,128]{1,0:T(8,128)S(1)}, f32[256,128]{1,0:T(8,128)}, u32[]{:S(2)}) copy-start(f32[256,128]{1,0:T(8,128)} %constant.66.clone.twist_cos) | copy-start | bytes 393220
  40.7 25.2 %copy-start.3 = (bf16[2,512,256]{2,1,0:T(8,128)(2,1)S(1)}, bf16[2,512,256]{2,1,0:T(8,128)(2,1)}, u32[]{:S(2)}) copy-start(bf16[2,512,256]{2,1,0:T(8,128)(2,1)} %constant.68.clone.first) | copy-start | bytes 1572868
  66.0 5.9 %copy-start.2 = (bf16[2,512,256]{2,1,0:T(8,128)(2,1)S(1)}, bf16[2,512,256]{2,1,0:T(8,128)(2,1)}, u32[]{:S(2)}) copy-start(bf16[2,512,256]{2,1,0:T(8,128)(2,1)} %constant.72.clone.first) | copy-start | bytes 1572868
  66.0 5.9 %copy-start.4 = (bf16[2,256,256]{2,1,0:T(8,128)(2,1)S(1)}, bf16[2,256,256]{2,1,0:T(8,128)(2,1)}, u32[]{:S(2)}) copy-start(bf16[2,256,256]{2,1,0:T(8,128)(2,1)} %constant.69.clone.second) | copy-start | bytes 786436
  66.0 5.9 %copy-start.6 = (f32[256,128]{1,0:T(8,128)S(1)}, f32[256,128]{1,0:T(8,128)}, u32[]{:S(2)}) copy-start(f32[256,128]{1,0:T(8,128)} %constant.71.clone.twist_sin) | copy-start | bytes 393220
  66.0 5.9 %copy-start.7 = (f32[256,128]{1,0:T(8,128)S(1)}, f32[256,128]{1,0:T(8,128)}, u32[]{:S(2)}) copy-start(f32[256,128]{1,0:T(8,128)} %constant.70.clone.twist_cos) | copy-start | bytes 393220
  66.7 5.1 %collective-permute-start.1 = (f32[512,128]{1,0:T(8,128)S(1)}, f32[512,128]{1,0:T(8,128)S(1)}, u32[]{:S(2)}, u32[]{:S(2)}) collective-permute-start(f32[512,128]{1,0:T(8,128)S(1)} %shard_map.188.mine), channel_id=1, source_target_pairs={{0,1},{1,0},{2,3},{3,2},{4,5},{5,4},{6,7},{7,6},{8,9},{9,8},{10,11... | collective-permute-start | bytes 786440 | tf_op jit(solution)/shard_map/ppermute | solution.py:489
  73.4 22.0 %all-to-all-start.2 = ((f32[256,2,128]{2,1,0:T(2,128)}), f32[256,2,128]{2,1,0:T(2,128)S(1)}, u32[]{:S(2)}, u32[]{:S(2)}) async-start(f32[256,2,128]{2,1,0:T(2,128)} %bitcast.15), calls=%async_computation.2 | async-start | bytes 524288 | tf_op jit(solution)/shard_map/all_to_all | solution.py:452
  83.2 9.3 %collective-permute-start.2 = (f32[56,128]{1,0:T(8,128)S(1)}, f32[56,128]{1,0:T(8,128)S(1)}, u32[]{:S(2)}, u32[]{:S(2)}) collective-permute-start(f32[56,128]{1,0:T(8,128)S(1)} %get-tuple-element.23.mine), channel_id=1, source_target_pairs={{0,480},{32,0},{64,32},{96,64},{128,96},{160,128},{192,160},{224,1... | collective-permute-start | bytes 86024 | tf_op jit(solution)/shard_map/ppermute | solution.py:456
  96.0 17.9 %copy-start.13 = (bf16[128,128]{1,0:T(8,128)(2,1)S(1)}, bf16[128,128]{1,0:T(8,128)(2,1)}, u32[]{:S(2)}) copy-start(bf16[128,128]{1,0:T(8,128)(2,1)} %constant.64.clone.columns) | copy-start | bytes 98308

commit v10 on v9

--- a/solution.py
+++ b/solution.py
@@ -323,16 +323,20 @@
     outer = (lane < SHIFT) | (lane >= TILE_COLS - SHIFT)
     parts = []
     for s in range(SLAB):
-        around = roll(packed, -EDGE * s - SHIFT, 1)
-        parts.append(jnp.where(outer, around, data[pl.ds(s, OUTER, stride=BLOCK), :]))
+        parts.append(jnp.where(outer, 0.0, data[pl.ds(s, OUTER, stride=BLOCK), :]))
     rows = jnp.concatenate(parts, axis=1)
     first = slice(128, 128 + 2 * OUTER)
-    spread = dot((every[0, first, :OUTER], every[1, first, :OUTER]), halves(rows))
+    starts = every[0, first, :OUTER], every[1, first, :OUTER]
+    spread = dot(starts, halves(rows))
+    edge = dot(starts, halves(packed))
+    both_outer = jnp.concatenate([outer, outer], axis=0)
     cosine, sine = twist_cos[...], twist_sin[...]
     real, imag = [], []
     for s in range(SLAB):
         part = slice(s * 128, (s + 1) * 128)
-        re, im = spread[:OUTER, part], spread[OUTER:, part]
+        around = jnp.where(both_outer, roll(edge, -EDGE * s - SHIFT, 1), 0.0)
+        whole = spread[:, part] + around
+        re, im = whole[:OUTER], whole[OUTER:]
         real.append(re * cosine + im * sine)
         imag.append(im * cosine - re * sine)
     for g in range(4):

time: 116 us -> 115 us (level)
  no operation moved by 1% of the time
where the time goes in v10:
time: 115 us
  blocking collectives  62.3 us (54%)
  starting transfers between devices  29.5 us (26%)
  waiting for transfers between devices  11.9 us (10%)
  Pallas kernels  7.04 us (6%)
  other arithmetic  2.48 us (2%)
    all_to_all x3, blocking collectives, exchange(): return lax.all_to_all(blocks, axes, split_axis=0, concat_axis=0, tiled=True)  62.3 us
    ppermute x2, starting transfers between devices, shift(): lax.ppermute(block, axes, [(i, (i + step) % count) for i in range(count)])  16 us
    all_to_all x1, starting transfers between devices, exchange(): return lax.all_to_all(blocks, axes, split_axis=0, concat_axis=0, tiled=True)  9.8 us
    ppermute x2, waiting for transfers between devices, shift(): lax.ppermute(block, axes, [(i, (i + step) % count) for i in range(count)])  8.1 us
    pallas_call x9, Pallas kernels, call(): pl.pallas_call(kernel, out_shape=shapes, in_specs=spaces, out_specs=[VMEM...  7.04 us
    ppermute x1, starting transfers between devices, body(): other = lax.ppermute(mine, 'core', [(0, 1), (1, 0)])  3.68 us
    all_to_all x1, waiting for transfers between devices, exchange(): return lax.all_to_all(blocks, axes, split_axis=0, concat_axis=0, tiled=True)  2.65 us
  transfers between devices with their start and end apart: 4, of which 4 were waited for; matrix products, arithmetic and copies ran while one was open for 1% of the time, Pallas kernels for 1%

profile of v10, /device:TPU:1, one launch (start us, length us, event | category | flops | bytes accessed | tf_op | source)
XLA Modules:
  0.0 114.9 jit_solution(7529035154371715165)
XLA Ops:
  0.6 0.7 negate_bitcast_fusion
  1.3 0.7 convert_bitcast_fusion.1
  2.0 0.1 select_select_fusion
  2.1 0.0 copy-start.15
  2.1 8.4 %collective-permute-start = (f32[3,8,128]{2,1,0:T(8,128)S(1)}, f32[3,8,128]{2,1,0:T(8,128)S(1)}, u32[]{:S(2)}, u32[]{:S(2)}) collective-permute-start(f32[3,8,128]{2,1,0:T(8,128)S(1)} %select_select_fusion), channel_id=1, source_target_pairs={{0,32},{32,64},{64,96},{96,128},{128,160},{160,192},{192,224},{224... | collective-permute-start | bytes 36872 | tf_op jit(solution)/shard_map/ppermute | solution.py:460
  10.5 1.0 bitcast_multiply_fusion.phase
  11.5 0.0 copy-done.15
  11.5 0.0 copy-start
  11.6 0.0 copy-start.14
  11.6 0.1 stack.23.place
  11.7 0.6 copy-done.14
  12.3 0.6 shard_map.184.info
  12.8 0.0 copy-done
  12.8 0.8 shard_map.185
  13.7 6.4 %collective-permute-done.above = f32[3,8,128]{2,1,0:T(8,128)S(1)} collective-permute-done((f32[3,8,128]{2,1,0:T(8,128)S(1)}, f32[3,8,128]{2,1,0:T(8,128)S(1)}, u32[]{:S(2)}, u32[]{:S(2)}) %collective-permute-start) | collective-permute-done | bytes 12320 | tf_op jit(solution)/shard_map/ppermute | solution.py:460
  20.1 0.3 shard_map.186
  20.3 0.0 copy-start.1
  20.4 0.0 copy-start.10
  20.4 0.0 copy-start.11
  20.4 0.0 copy-start.12
  20.4 18.9 %all_to_all.20 = f32[160,4,128]{2,1,0:T(4,128)S(1)} all-to-all(f32[160,4,128]{2,1,0:T(4,128)S(1)} %bitcast.42), channel_id=1, replica_groups=mesh['z'=8,'y_hi'=2,'x'=4,'y_lo'=4,'core'=2] {'x','y_lo','core'}, dimensions={0} | all-to-all | bytes 655360 | tf_op jit(solution)/shard_map/all_to_all | solution.py:456
  39.3 0.0 copy-done.1
  39.3 0.0 copy-done.10
  39.3 0.0 copy-done.11
  39.3 0.0 copy-done.12
  39.3 0.0 copy-start.5
  39.4 0.0 copy-start.8
  39.4 0.0 copy-start.9
  39.4 1.3 %shard_map.187 = (f32[512,128]{1,0:T(8,128)S(1)}, f32[56,128]{1,0:T(8,128)S(1)}) custom-call(f32[8,128]{1,0:T(8,128)S(1)} %shard_map.184.info, f32[640,128]{1,0:T(8,128)S(1)} %bitcast.37, f32[256,128]{1,0:T(8,128)S(1)} %convert_bitcast_fusion.porous, f32[256,128]{1,0:T(8,128)S(1)} %bitcast_multiply_fusion.phase, f32[256,128]{1,0:T(8,128)S(1)} %bitcast.35, ...), custom_call_target="tpu_custom_call" | custom-call | tf_op jit(solution)/shard_map/pallas_call | solution.py:66
  40.6 0.0 copy-start.3
  40.6 25.5 %all_to_all.21 = f32[256,2,128]{2,1,0:T(2,128)S(1)} all-to-all(f32[256,2,128]{2,1,0:T(2,128)S(1)} %bitcast.43), channel_id=1, replica_groups=mesh['z'=8,'y_hi'=2,'x'=4,'y_lo'=4,'core'=2] {'y_lo','x','y_hi','z'}, dimensions={0} | all-to-all | bytes 524288 | tf_op jit(solution)/shard_map/all_to_all | solution.py:456
  66.1 0.0 copy-done.5
  66.1 0.0 copy-done.8
  66.1 0.0 copy-done.9
  66.1 0.0 copy-done.3
  66.1 0.0 copy-start.2
  66.1 0.0 copy-start.4
  66.2 0.0 copy-start.6
  66.2 0.0 copy-start.7
  66.2 0.7 shard_map.188.mine
  66.9 3.7 %collective-permute-start.1 = (f32[512,128]{1,0:T(8,128)S(1)}, f32[512,128]{1,0:T(8,128)S(1)}, u32[]{:S(2)}, u32[]{:S(2)}) collective-permute-start(f32[512,128]{1,0:T(8,128)S(1)} %shard_map.188.mine), channel_id=1, source_target_pairs={{0,1},{1,0},{2,3},{3,2},{4,5},{5,4},{6,7},{7,6},{8,9},{9,8},{10,11... | collective-permute-start | bytes 786440 | tf_op jit(solution)/shard_map/ppermute | solution.py:493
  70.6 1.1 collective-permute-done.1.other
  71.7 0.0 copy-done.2
  71.8 0.0 copy-done.4
  71.8 0.0 copy-done.6
  71.8 0.0 copy-done.7
  71.8 1.5 %shard_map.189 = f32[512,128]{1,0:T(8,128)} custom-call(f32[8,128]{1,0:T(8,128)S(1)} %shard_map.184.info, f32[512,128]{1,0:T(8,128)S(1)} %shard_map.188.mine, f32[512,128]{1,0:T(8,128)S(1)} %collective-permute-done.1.other, bf16[2,512,256]{2,1,0:T(8,128)(2,1)S(1)} %copy-done.2, bf16[2,256,256]{2,1,0:T(8,128)(2,1)S(1)} %copy-done.4, ...), custom_call_target="tpu_custom_call" | custom-call | tf_op jit(solution)/shard_map/pallas_call | solution.py:66
  73.3 9.8 %all-to-all-start.2 = ((f32[256,2,128]{2,1,0:T(2,128)}), f32[256,2,128]{2,1,0:T(2,128)S(1)}, u32[]{:S(2)}, u32[]{:S(2)}) async-start(f32[256,2,128]{2,1,0:T(2,128)} %bitcast.15), calls=%async_computation.2 | async-start | bytes 524288 | tf_op jit(solution)/shard_map/all_to_all | solution.py:456
  83.1 7.6 %collective-permute-start.2 = (f32[56,128]{1,0:T(8,128)S(1)}, f32[56,128]{1,0:T(8,128)S(1)}, u32[]{:S(2)}, u32[]{:S(2)}) collective-permute-start(f32[56,128]{1,0:T(8,128)S(1)} %get-tuple-element.23.mine), channel_id=1, source_target_pairs={{0,480},{32,0},{64,32},{96,64},{128,96},{160,128},{192,160},{224,1... | collective-permute-start | bytes 86024 | tf_op jit(solution)/shard_map/ppermute | solution.py:460
  90.7 1.7 %collective-permute-done.2.parcel.below = f32[56,128]{1,0:T(8,128)S(1)} collective-permute-done((f32[56,128]{1,0:T(8,128)S(1)}, f32[56,128]{1,0:T(8,128)S(1)}, u32[]{:S(2)}, u32[]{:S(2)}) %collective-permute-start.2) | collective-permute-done | bytes 28704 | tf_op jit(solution)/shard_map/ppermute | solution.py:460
  92.4 0.2 shard_map.190.fields
  92.6 2.7 %all-to-all-done.2 = f32[256,2,128]{2,1,0:T(2,128)S(1)} async-done(((f32[256,2,128]{2,1,0:T(2,128)}), f32[256,2,128]{2,1,0:T(2,128)S(1)}, u32[]{:S(2)}, u32[]{:S(2)}) %all-to-all-start.2) | async-done | bytes 262176 | tf_op jit(solution)/shard_map/all_to_all | solution.py:456
  95.3 0.6 shard_map.191
  95.9 0.0 copy-start.13
  95.9 17.9 %all_to_all.22 = f32[544,1,128]{2,1,0:T(1,128)S(1)} all-to-all(f32[544,1,128]{2,1,0:T(1,128)S(1)} %bitcast.39), channel_id=1, replica_groups=mesh['z'=8,'y_hi'=2,'x'=4,'y_lo'=4,'core'=2] {'core','x','y_lo'}, dimensions={0} | all-to-all | bytes 557056 | tf_op jit(solution)/shard_map/all_to_all | solution.py:456
  113.8 0.0 copy-done.13
  113.8 1.0 shard_map.192
  (2 shorter events, 0.0 us)
Async XLA Ops:
  2.1 9.4 %copy-start.15 = (s32[1,256,128]{2,1,0:T(8,128)S(1)}, s32[1,256,128]{2,1,0:T(8,128)}, u32[]{:S(2)}) copy-start(s32[1,256,128]{2,1,0:T(8,128)} %param.17) | copy-start | bytes 393220
  2.1 18.0 %collective-permute-start = (f32[3,8,128]{2,1,0:T(8,128)S(1)}, f32[3,8,128]{2,1,0:T(8,128)S(1)}, u32[]{:S(2)}, u32[]{:S(2)}) collective-permute-start(f32[3,8,128]{2,1,0:T(8,128)S(1)} %select_select_fusion), channel_id=1, source_target_pairs={{0,32},{32,64},{64,96},{96,128},{128,160},{160,192},{192,224},{224... | collective-permute-start | bytes 36872 | tf_op jit(solution)/shard_map/ppermute | solution.py:460
  11.5 1.3 %copy-start = (f32[1,256,128]{2,1,0:T(8,128)S(1)}, f32[1,256,128]{2,1,0:T(8,128)}, u32[]{:S(2)}) copy-start(f32[1,256,128]{2,1,0:T(8,128)} %param.19) | copy-start | bytes 393220
  11.6 0.7 copy-start.14
  20.3 19.0 %copy-start.1 = (bf16[2,224,256]{2,1,0:T(8,128)(2,1)S(1)}, bf16[2,224,256]{2,1,0:T(8,128)(2,1)}, u32[]{:S(2)}) copy-start(bf16[2,224,256]{2,1,0:T(8,128)(2,1)} %constant.60.clone.every) | copy-start | bytes 688132
  20.4 19.0 %copy-start.10 = (bf16[2,128,128]{2,1,0:T(8,128)(2,1)S(1)}, bf16[2,128,128]{2,1,0:T(8,128)(2,1)}, u32[]{:S(2)}) copy-start(bf16[2,128,128]{2,1,0:T(8,128)(2,1)} %constant.63.clone.order) | copy-start | bytes 196612
  20.4 19.0 %copy-start.11 = (f32[32,128]{1,0:T(8,128)S(1)}, f32[32,128]{1,0:T(8,128)}, u32[]{:S(2)}) copy-start(f32[32,128]{1,0:T(8,128)} %constant.62.clone.twist_sin) | copy-start | bytes 49156
  20.4 19.0 %copy-start.12 = (f32[32,128]{1,0:T(8,128)S(1)}, f32[32,128]{1,0:T(8,128)}, u32[]{:S(2)}) copy-start(f32[32,128]{1,0:T(8,128)} %constant.61.clone.twist_cos) | copy-start | bytes 49156
  39.3 26.8 %copy-start.5 = (bf16[2,256,256]{2,1,0:T(8,128)(2,1)S(1)}, bf16[2,256,256]{2,1,0:T(8,128)(2,1)}, u32[]{:S(2)}) copy-start(bf16[2,256,256]{2,1,0:T(8,128)(2,1)} %constant.65.clone.second) | copy-start | bytes 786436
  39.4 26.8 %copy-start.8 = (f32[256,128]{1,0:T(8,128)S(1)}, f32[256,128]{1,0:T(8,128)}, u32[]{:S(2)}) copy-start(f32[256,128]{1,0:T(8,128)} %constant.67.clone.twist_sin) | copy-start | bytes 393220
  39.4 26.8 %copy-start.9 = (f32[256,128]{1,0:T(8,128)S(1)}, f32[256,128]{1,0:T(8,128)}, u32[]{:S(2)}) copy-start(f32[256,128]{1,0:T(8,128)} %constant.66.clone.twist_cos) | copy-start | bytes 393220
  40.6 25.5 %copy-start.3 = (bf16[2,512,256]{2,1,0:T(8,128)(2,1)S(1)}, bf16[2,512,256]{2,1,0:T(8,128)(2,1)}, u32[]{:S(2)}) copy-start(bf16[2,512,256]{2,1,0:T(8,128)(2,1)} %constant.68.clone.first) | copy-start | bytes 1572868
  66.1 5.6 %copy-start.2 = (bf16[2,512,256]{2,1,0:T(8,128)(2,1)S(1)}, bf16[2,512,256]{2,1,0:T(8,128)(2,1)}, u32[]{:S(2)}) copy-start(bf16[2,512,256]{2,1,0:T(8,128)(2,1)} %constant.72.clone.first) | copy-start | bytes 1572868
  66.1 5.6 %copy-start.4 = (bf16[2,256,256]{2,1,0:T(8,128)(2,1)S(1)}, bf16[2,256,256]{2,1,0:T(8,128)(2,1)}, u32[]{:S(2)}) copy-start(bf16[2,256,256]{2,1,0:T(8,128)(2,1)} %constant.69.clone.second) | copy-start | bytes 786436
  66.2 5.6 %copy-start.6 = (f32[256,128]{1,0:T(8,128)S(1)}, f32[256,128]{1,0:T(8,128)}, u32[]{:S(2)}) copy-start(f32[256,128]{1,0:T(8,128)} %constant.71.clone.twist_sin) | copy-start | bytes 393220
  66.2 5.6 %copy-start.7 = (f32[256,128]{1,0:T(8,128)S(1)}, f32[256,128]{1,0:T(8,128)}, u32[]{:S(2)}) copy-start(f32[256,128]{1,0:T(8,128)} %constant.70.clone.twist_cos) | copy-start | bytes 393220
  66.9 4.8 %collective-permute-start.1 = (f32[512,128]{1,0:T(8,128)S(1)}, f32[512,128]{1,0:T(8,128)S(1)}, u32[]{:S(2)}, u32[]{:S(2)}) collective-permute-start(f32[512,128]{1,0:T(8,128)S(1)} %shard_map.188.mine), channel_id=1, source_target_pairs={{0,1},{1,0},{2,3},{3,2},{4,5},{5,4},{6,7},{7,6},{8,9},{9,8},{10,11... | collective-permute-start | bytes 786440 | tf_op jit(solution)/shard_map/ppermute | solution.py:493
  73.3 22.0 %all-to-all-start.2 = ((f32[256,2,128]{2,1,0:T(2,128)}), f32[256,2,128]{2,1,0:T(2,128)S(1)}, u32[]{:S(2)}, u32[]{:S(2)}) async-start(f32[256,2,128]{2,1,0:T(2,128)} %bitcast.15), calls=%async_computation.2 | async-start | bytes 524288 | tf_op jit(solution)/shard_map/all_to_all | solution.py:456
  83.1 9.3 %collective-permute-start.2 = (f32[56,128]{1,0:T(8,128)S(1)}, f32[56,128]{1,0:T(8,128)S(1)}, u32[]{:S(2)}, u32[]{:S(2)}) collective-permute-start(f32[56,128]{1,0:T(8,128)S(1)} %get-tuple-element.23.mine), channel_id=1, source_target_pairs={{0,480},{32,0},{64,32},{96,64},{128,96},{160,128},{192,160},{224,1... | collective-permute-start | bytes 86024 | tf_op jit(solution)/shard_map/ppermute | solution.py:460
  95.9 17.9 %copy-start.13 = (bf16[128,128]{1,0:T(8,128)(2,1)S(1)}, bf16[128,128]{1,0:T(8,128)(2,1)}, u32[]{:S(2)}) copy-start(bf16[128,128]{1,0:T(8,128)(2,1)} %constant.64.clone.columns) | copy-start | bytes 98308

commit v11 on v10

--- a/solution.py
+++ b/solution.py
@@ -259,7 +259,7 @@
 
 def tail_kernel(info, porous, phase, heat, fields, parcel, out):
     ends = [
-        jnp.concatenate([field[TILE_ROWS - 2 * EDGE :, :], parcel[f * EDGE : (f + 1) * EDGE, :]])
+        jnp.concatenate([field[TILE_ROWS - 2 * EDGE :, :], roll(parcel[:EDGE, :], -f * SHIFT, 0)])
         for f, field in enumerate((porous, phase, heat))
     ]
     row = lax.broadcasted_iota(jnp.int32, ends[0].shape, 0)
@@ -315,9 +315,10 @@
     info, data, porous, phase, heat, order, every, twist_cos, twist_sin, out, parcel
 ):
     polar, value = edge_polar(info, data)
-    for f, field in enumerate((porous, phase, heat)):
-        parcel[f * EDGE : (f + 1) * EDGE, :] = field[:EDGE, :]
-    parcel[3 * EDGE :, :] = pack(value)
+    row = lax.broadcasted_iota(jnp.int32, (EDGE, TILE_COLS), 0)
+    tops = [roll(field[:EDGE, :], f * SHIFT, 0) for f, field in enumerate((porous, phase, heat))]
+    parcel[:EDGE, :] = jnp.where(row < SHIFT, tops[0], jnp.where(row < 2 * SHIFT, tops[1], tops[2]))
+    parcel[EDGE:, :] = pack(value)
     packed = dot(halves(pack(polar)), (order[0], order[1]))
     lane = lax.broadcasted_iota(jnp.int32, (OUTER, TILE_COLS), 1)
     outer = (lane < SHIFT) | (lane >= TILE_COLS - SHIFT)
@@ -373,7 +374,7 @@
     lane = lax.broadcasted_iota(jnp.int32, (SLAB, TILE_COLS), 1)
     late = (known(info, PLACE) == 0.0) & (lane % SLAB < SHIFT)
     for core in range(2):
-        rows = pl.ds(3 * EDGE + core, SLAB, stride=2)
+        rows = pl.ds(EDGE + core, SLAB, stride=2)
         start = core * SLAB * BACK + SLAB
         out[pl.ds(start, SLAB, stride=BACK), :] = jnp.where(late, below[rows, :], mine[rows, :])
 
@@ -485,7 +486,7 @@
     )
     slab = exchange(polar, GY_AXES, 4).reshape(-1, 128)
     spec, parcel = call(
-        columns_forward_kernel, [(2 * CHIPS, 128), (3 * EDGE + OUTER, 128)],
+        columns_forward_kernel, [(2 * CHIPS, 128), (EDGE + OUTER, 128)],
         info, slab, porous, phase, heat, order, *shared,
     )
     spec = exchange(spec, CHIP_AXES, 2).reshape(-1, 128)

time: 115 us -> 115 us (level)
  no operation moved by 1% of the time
where the time goes in v11:
time: 115 us
  blocking collectives  62 us (54%)
  starting transfers between devices  29.8 us (26%)
  waiting for transfers between devices  11.9 us (10%)
  Pallas kernels  7.05 us (6%)
  other arithmetic  2.48 us (2%)
    all_to_all x3, blocking collectives, exchange(): return lax.all_to_all(blocks, axes, split_axis=0, concat_axis=0, tiled=True)  62 us
    ppermute x2, starting transfers between devices, shift(): lax.ppermute(block, axes, [(i, (i + step) % count) for i in range(count)])  16 us
    all_to_all x1, starting transfers between devices, exchange(): return lax.all_to_all(blocks, axes, split_axis=0, concat_axis=0, tiled=True)  9.82 us
    ppermute x2, waiting for transfers between devices, shift(): lax.ppermute(block, axes, [(i, (i + step) % count) for i in range(count)])  7.81 us
    pallas_call x9, Pallas kernels, call(): pl.pallas_call(kernel, out_shape=shapes, in_specs=spaces, out_specs=[VMEM...  7.05 us
    ppermute x1, starting transfers between devices, body(): other = lax.ppermute(mine, 'core', [(0, 1), (1, 0)])  3.96 us
    all_to_all x1, waiting for transfers between devices, exchange(): return lax.all_to_all(blocks, axes, split_axis=0, concat_axis=0, tiled=True)  2.94 us
  transfers between devices with their start and end apart: 4, of which 4 were waited for; matrix products, arithmetic and copies ran while one was open for 1% of the time, Pallas kernels for 1%

profile of v11, /device:TPU:1, one launch (start us, length us, event | category | flops | bytes accessed | tf_op | source)
XLA Modules:
  0.0 114.9 jit_solution(15552848061518876477)
XLA Ops:
  0.6 0.7 negate_bitcast_fusion
  1.3 0.7 convert_bitcast_fusion.1
  2.0 0.1 select_select_fusion
  2.1 0.0 copy-start.15
  2.1 8.4 %collective-permute-start = (f32[3,8,128]{2,1,0:T(8,128)S(1)}, f32[3,8,128]{2,1,0:T(8,128)S(1)}, u32[]{:S(2)}, u32[]{:S(2)}) collective-permute-start(f32[3,8,128]{2,1,0:T(8,128)S(1)} %select_select_fusion), channel_id=1, source_target_pairs={{0,32},{32,64},{64,96},{96,128},{128,160},{160,192},{192,224},{224... | collective-permute-start | bytes 36872 | tf_op jit(solution)/shard_map/ppermute | solution.py:461
  10.5 1.0 bitcast_multiply_fusion.phase
  11.5 0.0 copy-done.15
  11.5 0.0 copy-start
  11.6 0.0 copy-start.14
  11.6 0.1 stack.23.place
  11.7 0.6 copy-done.14
  12.3 0.6 shard_map.184.info
  12.8 0.0 copy-done
  12.8 0.8 shard_map.185
  13.7 6.4 %collective-permute-done.above = f32[3,8,128]{2,1,0:T(8,128)S(1)} collective-permute-done((f32[3,8,128]{2,1,0:T(8,128)S(1)}, f32[3,8,128]{2,1,0:T(8,128)S(1)}, u32[]{:S(2)}, u32[]{:S(2)}) %collective-permute-start) | collective-permute-done | bytes 12320 | tf_op jit(solution)/shard_map/ppermute | solution.py:461
  20.1 0.3 shard_map.186
  20.3 0.0 copy-start.1
  20.4 0.0 copy-start.10
  20.4 0.0 copy-start.11
  20.4 0.0 copy-start.12
  20.4 18.9 %all_to_all.20 = f32[160,4,128]{2,1,0:T(4,128)S(1)} all-to-all(f32[160,4,128]{2,1,0:T(4,128)S(1)} %bitcast.42), channel_id=1, replica_groups=mesh['z'=8,'y_hi'=2,'x'=4,'y_lo'=4,'core'=2] {'x','y_lo','core'}, dimensions={0} | all-to-all | bytes 655360 | tf_op jit(solution)/shard_map/all_to_all | solution.py:457
  39.3 0.0 copy-done.1
  39.3 0.0 copy-done.10
  39.3 0.0 copy-done.11
  39.3 0.0 copy-done.12
  39.3 0.0 copy-start.5
  39.4 0.0 copy-start.8
  39.4 0.0 copy-start.9
  39.4 1.3 %shard_map.187 = (f32[512,128]{1,0:T(8,128)S(1)}, f32[40,128]{1,0:T(8,128)S(1)}) custom-call(f32[8,128]{1,0:T(8,128)S(1)} %shard_map.184.info, f32[640,128]{1,0:T(8,128)S(1)} %bitcast.37, f32[256,128]{1,0:T(8,128)S(1)} %convert_bitcast_fusion.porous, f32[256,128]{1,0:T(8,128)S(1)} %bitcast_multiply_fusion.phase, f32[256,128]{1,0:T(8,128)S(1)} %bitcast.35, ...), custom_call_target="tpu_custom_call" | custom-call | tf_op jit(solution)/shard_map/pallas_call | solution.py:66
  40.6 0.0 copy-start.3
  40.7 25.2 %all_to_all.21 = f32[256,2,128]{2,1,0:T(2,128)S(1)} all-to-all(f32[256,2,128]{2,1,0:T(2,128)S(1)} %bitcast.43), channel_id=1, replica_groups=mesh['z'=8,'y_hi'=2,'x'=4,'y_lo'=4,'core'=2] {'y_lo','x','y_hi','z'}, dimensions={0} | all-to-all | bytes 524288 | tf_op jit(solution)/shard_map/all_to_all | solution.py:457
  65.8 0.0 copy-done.5
  65.8 0.0 copy-done.8
  65.8 0.0 copy-done.9
  65.8 0.0 copy-done.3
  65.8 0.0 copy-start.2
  65.9 0.0 copy-start.4
  65.9 0.0 copy-start.6
  65.9 0.0 copy-start.7
  65.9 0.7 shard_map.188.mine
  66.6 4.0 %collective-permute-start.1 = (f32[512,128]{1,0:T(8,128)S(1)}, f32[512,128]{1,0:T(8,128)S(1)}, u32[]{:S(2)}, u32[]{:S(2)}) collective-permute-start(f32[512,128]{1,0:T(8,128)S(1)} %shard_map.188.mine), channel_id=1, source_target_pairs={{0,1},{1,0},{2,3},{3,2},{4,5},{5,4},{6,7},{7,6},{8,9},{9,8},{10,11... | collective-permute-start | bytes 786440 | tf_op jit(solution)/shard_map/ppermute | solution.py:494
  70.6 1.1 collective-permute-done.1.other
  71.7 0.0 copy-done.2
  71.7 0.0 copy-done.4
  71.8 0.0 copy-done.6
  71.8 0.0 copy-done.7
  71.8 1.5 %shard_map.189 = f32[512,128]{1,0:T(8,128)} custom-call(f32[8,128]{1,0:T(8,128)S(1)} %shard_map.184.info, f32[512,128]{1,0:T(8,128)S(1)} %shard_map.188.mine, f32[512,128]{1,0:T(8,128)S(1)} %collective-permute-done.1.other, bf16[2,512,256]{2,1,0:T(8,128)(2,1)S(1)} %copy-done.2, bf16[2,256,256]{2,1,0:T(8,128)(2,1)S(1)} %copy-done.4, ...), custom_call_target="tpu_custom_call" | custom-call | tf_op jit(solution)/shard_map/pallas_call | solution.py:66
  73.3 9.8 %all-to-all-start.2 = ((f32[256,2,128]{2,1,0:T(2,128)}), f32[256,2,128]{2,1,0:T(2,128)S(1)}, u32[]{:S(2)}, u32[]{:S(2)}) async-start(f32[256,2,128]{2,1,0:T(2,128)} %bitcast.15), calls=%async_computation.2 | async-start | bytes 524288 | tf_op jit(solution)/shard_map/all_to_all | solution.py:457
  83.1 7.6 %collective-permute-start.2 = (f32[40,128]{1,0:T(8,128)S(1)}, f32[40,128]{1,0:T(8,128)S(1)}, u32[]{:S(2)}, u32[]{:S(2)}) collective-permute-start(f32[40,128]{1,0:T(8,128)S(1)} %get-tuple-element.23.mine), channel_id=1, source_target_pairs={{0,480},{32,0},{64,32},{96,64},{128,96},{160,128},{192,160},{224,1... | collective-permute-start | bytes 61448 | tf_op jit(solution)/shard_map/ppermute | solution.py:461
  90.8 1.4 %collective-permute-done.2.parcel.below = f32[40,128]{1,0:T(8,128)S(1)} collective-permute-done((f32[40,128]{1,0:T(8,128)S(1)}, f32[40,128]{1,0:T(8,128)S(1)}, u32[]{:S(2)}, u32[]{:S(2)}) %collective-permute-start.2) | collective-permute-done | bytes 20512 | tf_op jit(solution)/shard_map/ppermute | solution.py:461
  92.2 0.2 shard_map.190.fields
  92.3 2.9 %all-to-all-done.2 = f32[256,2,128]{2,1,0:T(2,128)S(1)} async-done(((f32[256,2,128]{2,1,0:T(2,128)}), f32[256,2,128]{2,1,0:T(2,128)S(1)}, u32[]{:S(2)}, u32[]{:S(2)}) %all-to-all-start.2) | async-done | bytes 262176 | tf_op jit(solution)/shard_map/all_to_all | solution.py:457
  95.3 0.7 shard_map.191
  95.9 0.0 copy-start.13
  95.9 17.9 %all_to_all.22 = f32[544,1,128]{2,1,0:T(1,128)S(1)} all-to-all(f32[544,1,128]{2,1,0:T(1,128)S(1)} %bitcast.38), channel_id=1, replica_groups=mesh['z'=8,'y_hi'=2,'x'=4,'y_lo'=4,'core'=2] {'core','x','y_lo'}, dimensions={0} | all-to-all | bytes 557056 | tf_op jit(solution)/shard_map/all_to_all | solution.py:457
  113.8 0.0 copy-done.13
  113.8 1.0 shard_map.192
  (2 shorter events, 0.0 us)
Async XLA Ops:
  2.1 9.4 %copy-start.15 = (s32[1,256,128]{2,1,0:T(8,128)S(1)}, s32[1,256,128]{2,1,0:T(8,128)}, u32[]{:S(2)}) copy-start(s32[1,256,128]{2,1,0:T(8,128)} %param.17) | copy-start | bytes 393220
  2.1 18.0 %collective-permute-start = (f32[3,8,128]{2,1,0:T(8,128)S(1)}, f32[3,8,128]{2,1,0:T(8,128)S(1)}, u32[]{:S(2)}, u32[]{:S(2)}) collective-permute-start(f32[3,8,128]{2,1,0:T(8,128)S(1)} %select_select_fusion), channel_id=1, source_target_pairs={{0,32},{32,64},{64,96},{96,128},{128,160},{160,192},{192,224},{224... | collective-permute-start | bytes 36872 | tf_op jit(solution)/shard_map/ppermute | solution.py:461
  11.5 1.3 %copy-start = (f32[1,256,128]{2,1,0:T(8,128)S(1)}, f32[1,256,128]{2,1,0:T(8,128)}, u32[]{:S(2)}) copy-start(f32[1,256,128]{2,1,0:T(8,128)} %param.19) | copy-start | bytes 393220
  11.6 0.7 copy-start.14
  20.3 19.0 %copy-start.1 = (bf16[2,224,256]{2,1,0:T(8,128)(2,1)S(1)}, bf16[2,224,256]{2,1,0:T(8,128)(2,1)}, u32[]{:S(2)}) copy-start(bf16[2,224,256]{2,1,0:T(8,128)(2,1)} %constant.60.clone.every) | copy-start | bytes 688132
  20.4 19.0 %copy-start.10 = (f32[32,128]{1,0:T(8,128)S(1)}, f32[32,128]{1,0:T(8,128)}, u32[]{:S(2)}) copy-start(f32[32,128]{1,0:T(8,128)} %constant.62.clone.twist_sin) | copy-start | bytes 49156
  20.4 19.0 %copy-start.11 = (f32[32,128]{1,0:T(8,128)S(1)}, f32[32,128]{1,0:T(8,128)}, u32[]{:S(2)}) copy-start(f32[32,128]{1,0:T(8,128)} %constant.61.clone.twist_cos) | copy-start | bytes 49156
  20.4 19.0 %copy-start.12 = (bf16[2,128,128]{2,1,0:T(8,128)(2,1)S(1)}, bf16[2,128,128]{2,1,0:T(8,128)(2,1)}, u32[]{:S(2)}) copy-start(bf16[2,128,128]{2,1,0:T(8,128)(2,1)} %constant.63.clone.order) | copy-start | bytes 196612
  39.3 26.5 %copy-start.5 = (bf16[2,256,256]{2,1,0:T(8,128)(2,1)S(1)}, bf16[2,256,256]{2,1,0:T(8,128)(2,1)}, u32[]{:S(2)}) copy-start(bf16[2,256,256]{2,1,0:T(8,128)(2,1)} %constant.65.clone.second) | copy-start | bytes 786436
  39.4 26.5 %copy-start.8 = (f32[256,128]{1,0:T(8,128)S(1)}, f32[256,128]{1,0:T(8,128)}, u32[]{:S(2)}) copy-start(f32[256,128]{1,0:T(8,128)} %constant.67.clone.twist_sin) | copy-start | bytes 393220
  39.4 26.5 %copy-start.9 = (f32[256,128]{1,0:T(8,128)S(1)}, f32[256,128]{1,0:T(8,128)}, u32[]{:S(2)}) copy-start(f32[256,128]{1,0:T(8,128)} %constant.66.clone.twist_cos) | copy-start | bytes 393220
  40.6 25.2 %copy-start.3 = (bf16[2,512,256]{2,1,0:T(8,128)(2,1)S(1)}, bf16[2,512,256]{2,1,0:T(8,128)(2,1)}, u32[]{:S(2)}) copy-start(bf16[2,512,256]{2,1,0:T(8,128)(2,1)} %constant.68.clone.first) | copy-start | bytes 1572868
  65.8 5.9 %copy-start.2 = (bf16[2,512,256]{2,1,0:T(8,128)(2,1)S(1)}, bf16[2,512,256]{2,1,0:T(8,128)(2,1)}, u32[]{:S(2)}) copy-start(bf16[2,512,256]{2,1,0:T(8,128)(2,1)} %constant.72.clone.first) | copy-start | bytes 1572868
  65.9 5.9 %copy-start.4 = (bf16[2,256,256]{2,1,0:T(8,128)(2,1)S(1)}, bf16[2,256,256]{2,1,0:T(8,128)(2,1)}, u32[]{:S(2)}) copy-start(bf16[2,256,256]{2,1,0:T(8,128)(2,1)} %constant.69.clone.second) | copy-start | bytes 786436
  65.9 5.9 %copy-start.6 = (f32[256,128]{1,0:T(8,128)S(1)}, f32[256,128]{1,0:T(8,128)}, u32[]{:S(2)}) copy-start(f32[256,128]{1,0:T(8,128)} %constant.71.clone.twist_sin) | copy-start | bytes 393220
  65.9 5.9 %copy-start.7 = (f32[256,128]{1,0:T(8,128)S(1)}, f32[256,128]{1,0:T(8,128)}, u32[]{:S(2)}) copy-start(f32[256,128]{1,0:T(8,128)} %constant.70.clone.twist_cos) | copy-start | bytes 393220
  66.6 5.1 %collective-permute-start.1 = (f32[512,128]{1,0:T(8,128)S(1)}, f32[512,128]{1,0:T(8,128)S(1)}, u32[]{:S(2)}, u32[]{:S(2)}) collective-permute-start(f32[512,128]{1,0:T(8,128)S(1)} %shard_map.188.mine), channel_id=1, source_target_pairs={{0,1},{1,0},{2,3},{3,2},{4,5},{5,4},{6,7},{7,6},{8,9},{9,8},{10,11... | collective-permute-start | bytes 786440 | tf_op jit(solution)/shard_map/ppermute | solution.py:494
  73.3 22.0 %all-to-all-start.2 = ((f32[256,2,128]{2,1,0:T(2,128)}), f32[256,2,128]{2,1,0:T(2,128)S(1)}, u32[]{:S(2)}, u32[]{:S(2)}) async-start(f32[256,2,128]{2,1,0:T(2,128)} %bitcast.15), calls=%async_computation.2 | async-start | bytes 524288 | tf_op jit(solution)/shard_map/all_to_all | solution.py:457
  83.1 9.1 %collective-permute-start.2 = (f32[40,128]{1,0:T(8,128)S(1)}, f32[40,128]{1,0:T(8,128)S(1)}, u32[]{:S(2)}, u32[]{:S(2)}) collective-permute-start(f32[40,128]{1,0:T(8,128)S(1)} %get-tuple-element.23.mine), channel_id=1, source_target_pairs={{0,480},{32,0},{64,32},{96,64},{128,96},{160,128},{192,160},{224,1... | collective-permute-start | bytes 61448 | tf_op jit(solution)/shard_map/ppermute | solution.py:461
  95.9 17.9 %copy-start.13 = (bf16[128,128]{1,0:T(8,128)(2,1)S(1)}, bf16[128,128]{1,0:T(8,128)(2,1)}, u32[]{:S(2)}) copy-start(bf16[128,128]{1,0:T(8,128)(2,1)} %constant.64.clone.columns) | copy-start | bytes 98308
